TPU v7x, 32 devices: a whole 2x2x4 slice. The times are simulated.
32 devices in a mesh: row: 4 (over z), col: 8 (over y, x, core).
Axes of the slice: x: 2, y: 2, z: 4, core: 2. Of those that a mesh axis runs over, the one named last changes fastest.
Arguments:
- atom_single: bfloat16 [8192, 128], P(('row', 'col')), may hold values from -6 to 6
- atom_token: int32 [8192], P(('row', 'col')), may hold values from 0 to 1023, as said below
- atom_cot: bfloat16 [8192, 128], P(('row', 'col')), may hold values from -6 to 6
- token_cond: bfloat16 [1024, 768], P('row'), may hold values from -6 to 6
- pair: bfloat16 [1024, 1024, 128], P('row', 'col'), may hold values from -12 to 12
- w_pool: bfloat16 [128, 768], replicated, may hold values from -0.5 to 0.5
- w_qkv: bfloat16 [3, 768, 768], P(None, None, 'col'), may hold values from -0.21875 to 0.21875
- w_bias: bfloat16 [128, 16], replicated, may hold values from -0.8 to 0.8
- w_out: bfloat16 [768, 768], P('col'), may hold values from -0.21875 to 0.21875
- w_dec: bfloat16 [768, 128], replicated, may hold values from -0.21875 to 0.21875
Outputs:
- atom_out: bfloat16 [8192, 128], P(('row', 'col'))
- grad_atom: float32 [8192, 128], P(('row', 'col'))
- grad_bias: float32 [128, 16], replicated
Inputs may be any that keep to these rules, and one draw needn't show every extreme that they name: `atom_token`: every token has 1 to 24 atoms and some token exactly 24; the atoms stand in no particular order.
All inputs are finite; a program needn't handle non-finite values.
Results may differ from a plain program's by a relative error of at most 0.014.
The roundings to bfloat16 on the way count: a program that leaves them out, or rounds other values in their place, can miss the bound.
Values may be sent and summed in bfloat16 or wider, within the bound.
A program may use at most 64 MiB of HBM per device.

v0:
```python
import math

import jax
import jax.numpy as jnp
from jax import lax
from jax.sharding import PartitionSpec as P

HD = 48


EPSILON = 1e-05


def layer_norm(single):
    center = single - jnp.mean(single, axis=-1, keepdims=True)
    inverse = lax.rsqrt(jnp.mean(center * center, axis=-1, keepdims=True) + EPSILON)
    return (center * inverse, inverse)


def norm_grad(upstream, normal, inverse):
    return inverse * (
        upstream
        - jnp.mean(upstream, axis=-1, keepdims=True)
        - normal * jnp.mean(upstream * normal, axis=-1, keepdims=True)
    )


def transposed_dot(left, right):
    return lax.dot_general(
        left, right, (((1,), (1,)), ((), ())), preferred_element_type=jnp.float32
    )


def on_device(
    atom_single, atom_token, atom_cot, token_cond, pair, w_pool, w_qkv, w_bias, w_out, w_dec
):
    tok_rows = token_cond.shape[0]
    total_tokens = tok_rows * lax.axis_size("row")
    width = w_out.shape[0]
    local_heads = width // HD
    atom_width = atom_single.shape[1]
    scale = 1.0 / math.sqrt(HD)
    onehot = (atom_token[:, None] == jnp.arange(total_tokens, dtype=jnp.int32)[None, :]).astype(
        jnp.bfloat16
    )
    stacked = jnp.concatenate([atom_single, atom_cot], axis=1)
    partial_sums = lax.dot_general(
        onehot, stacked, (((0,), (0,)), ((), ())), preferred_element_type=jnp.float32
    )
    partial_counts = jnp.sum(onehot.astype(jnp.float32), axis=0)
    share_sums, share_counts = (
        lax.psum_scatter(partial_sums, ("row", "col"), scatter_dimension=0, tiled=True),
        lax.psum_scatter(partial_counts, ("row", "col"), scatter_dimension=0, tiled=True),
    )
    share_rows = jnp.concatenate(
        [share_sums[:, :atom_width] / share_counts[:, None], share_sums[:, atom_width:]], axis=1
    ).astype(jnp.bfloat16)
    row_pooled, row_counts = (
        lax.all_gather(share_rows, "col", axis=0, tiled=True),
        lax.all_gather(share_counts.astype(jnp.bfloat16), "col", axis=0, tiled=True),
    )
    pooled = row_pooled[:, :atom_width]
    cot_pooled = row_pooled[:, atom_width:]
    counts = row_counts.astype(jnp.float32)
    single = token_cond.astype(jnp.float32) + jnp.dot(
        pooled, w_pool, preferred_element_type=jnp.float32
    )
    normal, inverse = layer_norm(single)
    normed = normal.astype(jnp.bfloat16)
    projected = jnp.einsum("td,kdf->ktf", normed, w_qkv, preferred_element_type=jnp.float32).astype(
        jnp.bfloat16
    )
    gathered = lax.all_gather(projected[1:], "row", axis=1, tiled=True)
    queries = projected[0].reshape(tok_rows, local_heads, HD)
    keys_all = gathered[0].reshape(total_tokens, local_heads, HD)
    values_all = gathered[1].reshape(total_tokens, local_heads, HD)
    bias_local = jnp.einsum("ijc,ch->hij", pair, w_bias, preferred_element_type=jnp.float32).astype(
        jnp.bfloat16
    )
    bias_rows = lax.all_to_all(bias_local, "col", split_axis=0, concat_axis=2, tiled=True)
    logits = jnp.einsum(
        "ihd,jhd->hij", queries, keys_all, preferred_element_type=jnp.float32
    ) * scale + bias_rows.astype(jnp.float32)
    shifted = jnp.exp(logits - jnp.max(logits, axis=-1, keepdims=True))
    probs = shifted / jnp.sum(shifted, axis=-1, keepdims=True)
    probs_low = probs.astype(jnp.bfloat16)
    attended = (
        jnp.einsum("hij,jhd->ihd", probs_low, values_all, preferred_element_type=jnp.float32)
        .astype(jnp.bfloat16)
        .reshape(tok_rows, width)
    )
    partial_update = jnp.dot(attended, w_out, preferred_element_type=jnp.float32)
    update = lax.psum(partial_update.astype(jnp.bfloat16), "col").astype(jnp.float32)
    token_out = (single + update).astype(jnp.bfloat16)
    token_back = jnp.dot(token_out, w_dec, preferred_element_type=jnp.float32).astype(jnp.bfloat16)
    all_back = lax.all_gather(token_back, "row", axis=0, tiled=True)
    atom_out = (
        atom_single.astype(jnp.float32)
        + jnp.dot(onehot, all_back, preferred_element_type=jnp.float32)
    ).astype(jnp.bfloat16)
    grad_out = transposed_dot(cot_pooled, w_dec)
    grad_update = grad_out.astype(jnp.bfloat16)
    grad_attended = (
        transposed_dot(grad_update, w_out).astype(jnp.bfloat16).reshape(tok_rows, local_heads, HD)
    )
    grad_probs = jnp.einsum(
        "ihd,jhd->hij", grad_attended, values_all, preferred_element_type=jnp.float32
    )
    delta = jnp.sum(probs * grad_probs, axis=-1, keepdims=True)
    grad_logits = (probs * (grad_probs - delta)).astype(jnp.bfloat16)
    grad_queries = (
        (
            jnp.einsum("hij,jhd->ihd", grad_logits, keys_all, preferred_element_type=jnp.float32)
            * scale
        )
        .astype(jnp.bfloat16)
        .reshape(tok_rows, width)
    )
    key_terms = jnp.stack(
        [
            jnp.einsum("hij,ihd->jhd", grad_logits, queries, preferred_element_type=jnp.float32),
            jnp.einsum(
                "hij,ihd->jhd", probs_low, grad_attended, preferred_element_type=jnp.float32
            ),
        ]
    ).reshape(2, total_tokens, width)
    key_sums = lax.psum_scatter(
        key_terms.astype(jnp.bfloat16), "row", scatter_dimension=1, tiled=True
    ).astype(jnp.float32)
    grad_keys = (key_sums[0] * scale).astype(jnp.bfloat16)
    grad_values = key_sums[1].astype(jnp.bfloat16)
    grad_proj = jnp.stack([grad_queries, grad_keys, grad_values])
    normed_part = jnp.einsum("ktf,kdf->td", grad_proj, w_qkv, preferred_element_type=jnp.float32)
    grad_normed = lax.psum(normed_part.astype(jnp.bfloat16), "col").astype(jnp.float32)
    grad_single = (grad_out + norm_grad(grad_normed, normal, inverse)).astype(jnp.bfloat16)
    token_grad = (transposed_dot(grad_single, w_pool) / counts[:, None]).astype(jnp.bfloat16)
    all_grad = lax.all_gather(token_grad, "row", axis=0, tiled=True)
    grad_atom = atom_cot.astype(jnp.float32) + jnp.dot(
        onehot, all_grad, preferred_element_type=jnp.float32
    )
    bias_back = lax.all_to_all(grad_logits, "col", split_axis=2, concat_axis=0, tiled=True)
    weight_part = jnp.einsum("ijc,hij->ch", pair, bias_back, preferred_element_type=jnp.float32)
    grad_bias = lax.psum(weight_part, ("row", "col"))
    return (atom_out, grad_atom, grad_bias)


def solution(mesh):
    return jax.shard_map(
        on_device,
        mesh=mesh,
        in_specs=(
            P(("row", "col"), None),
            P(("row", "col")),
            P(("row", "col"), None),
            P("row", None),
            P("row", "col", None),
            P(),
            P(None, None, "col"),
            P(),
            P("col", None),
            P(),
        ),
        out_specs=(P(("row", "col"), None), P(("row", "col"), None), P()),
        check_vma=False,
    )
```

profile of v0, /device:TPU:0, one launch (start us, length us, event | category | flops | bytes accessed | tf_op | source)
XLA Modules:
  0.0 309.7 jit_solution(651133389200917041)
XLA Ops:
  7.2 2.5 fusion.6
  9.7 5.7 %convolution_convert_fusion = bf16[16,256,128]{2,0,1:T(8,128)(2,1)S(1)} fusion(bf16[256,128,128]{2,1,0:T(8,128)(2,1)} %param.14, bf16[128,16]{0,1:T(8,128)(2,1)S(1)} %copy-done.18), kind=kOutput, calls=%fused_computation.6 | convolution fusion | flops 134742016 | bytes 9441280 | tf_op jit(solution)/shard_map/ijc,ch->hij/dot_general | solution.py:77
  15.4 1.3 copy.19
  16.7 5.2 %all-to-all-start = ((bf16[16,256,128]{2,1,0:T(8,128)(2,1)}), bf16[16,256,128]{2,1,0:T(8,128)(2,1)S(1)}, u32[]{:S(2)}, u32[]{:S(2)}) async-start(bf16[16,256,128]{2,1,0:T(8,128)(2,1)} %copy.19), calls=%async_computation.1 | async-start | bytes 2097152 | tf_op jit(solution)/shard_map/all_to_all | solution.py:80
  22.1 49.9 %all-reduce.1 = f32[1024]{0:T(1024)S(1)} all-reduce(f32[1024]{0:T(1024)S(1)} %convert_reduce_fusion.1), channel_id=3, replica_groups=mesh['row'=4,'col'=8] {'row','col'}, use_global_device_ids=true, to_apply=%region_2.0.clone | all-reduce | flops 1024 | bytes 8192
  72.1 1.0 copy-done.4
  73.1 1.8 copy.24
  74.9 1.5 reshape.51
  76.4 71.8 %reduce-scatter.3.cloned.1.call-done = f32[32,256]{1,0:T(8,128)} async-done(((f32[1024,256]{1,0:T(8,128)}), f32[32,256]{1,0:T(8,128)}) %reduce-scatter.3.cloned.1.call-update) | async-done | bytes 32784 | tf_op jit(solution)/shard_map/reduce_scatter | solution.py:52
  148.3 0.7 slice.66
  149.0 0.8 fusion.39
  149.8 7.8 %all_gather.15 = bf16[256,256]{1,0:T(8,128)(2,1)S(1)} all-gather(bf16[32,256]{1,0:T(8,128)(2,1)S(1)} %pad_maximum_fusion.1), channel_id=1, replica_groups=mesh['row'=4,'col'=8] {'col'}, dimensions={0}, use_global_device_ids=true | all-gather | bytes 147456 | tf_op jit(solution)/shard_map/all_gather | solution.py:59
  157.6 1.3 fusion.45
  159.1 0.4 fusion.18
  159.6 15.2 %all_gather.16 = bf16[2,1024,96]{1,2,0:T(8,128)(2,1)S(1)} all-gather(bf16[2,256,96]{1,2,0:T(8,128)(2,1)S(1)} %slice.49), channel_id=1, replica_groups=mesh['row'=4,'col'=8] {'row'}, dimensions={1}, use_global_device_ids=true | all-gather | bytes 491520 | tf_op jit(solution)/shard_map/all_gather | solution.py:73
  174.8 0.7 fusion.44
  175.6 0.5 multiply_add_fusion
  176.1 1.7 fusion.46
  178.0 0.9 copy-done.5
  178.9 0.9 convolution_convert_fusion.6
  179.8 2.6 convolution_convert_fusion.2
  182.4 2.4 multiply_reduce_fusion
  184.8 0.4 multiply_convert_fusion
  185.2 0.4 copy-done.11
  185.6 0.3 convolution_convert_fusion.3
  185.9 0.8 pad_maximum_fusion
  186.7 0.6 dynamic-slice
  188.2 12.1 %all-reduce = bf16[256]{0:T(256)(128)(2,1)S(1)} all-reduce(bf16[256]{0:T(256)(128)(2,1)S(1)} %dynamic-update-slice), channel_id=1, replica_groups=mesh['row'=4,'col'=8] {'col'}, use_global_device_ids=true, to_apply=%add | all-reduce | flops 256 | bytes 1024
  200.3 2.1 copy.21
  202.4 3.6 %all-to-all-start.1 = ((bf16[2,256,1024]{1,0,2:T(2,128)(2,1)}), bf16[2,256,1024]{1,0,2:T(2,128)(2,1)S(1)}, u32[]{:S(2)}, u32[]{:S(2)}) async-start(bf16[2,256,1024]{1,0,2:T(2,128)(2,1)} %copy.21), calls=%async_computation.3 | async-start | bytes 2097152 | tf_op jit(solution)/shard_map/all_to_all | solution.py:141
  206.2 4.1 %convolution_convert_fusion.5 = bf16[2,48,256]{2,1,0:T(8,128)(2,1)} fusion(bf16[1024,2,48]{0,2,1:T(8,128)(2,1)} %bitcast.84, f32[2,256]{1,0:T(2,128)S(1)} %get-tuple-element.13, f32[2,256,1024]{2,1,0:T(8,128)} %copy-done.1), kind=kOutput, calls=%fused_computation.24 | convolution fusion | flops 51930624 | bytes 2344960 | tf_op jit(solution)/shard_map/hij,jhd->ihd/dot_general | solution.py:88
  210.3 2.0 convolution_convert_fusion.1
  212.3 1.1 fusion.4
  213.3 0.8 slice.55
  214.2 0.8 multiply_convert_fusion.1
  215.0 1.9 fusion.1
  216.9 4.4 %all-to-all-done.1 = bf16[2,256,1024]{1,0,2:T(2,128)(2,1)S(1)} async-done(((bf16[2,256,1024]{1,0,2:T(2,128)(2,1)}), bf16[2,256,1024]{1,0,2:T(2,128)(2,1)S(1)}, u32[]{:S(2)}, u32[]{:S(2)}) %all-to-all-start.1) | async-done | bytes 1048608 | tf_op jit(solution)/shard_map/all_to_all | solution.py:141
  221.3 2.5 copy.22
  223.8 4.7 %convolution_bitcast_fusion.1 = f32[128,16]{0,1:T(8,128)S(1)} fusion(bf16[16,256,128]{2,0,1:T(8,128)(2,1)S(1)} %bitcast.73, bf16[256,128,128]{2,1,0:T(8,128)(2,1)} %param.14), kind=kOutput, calls=%fused_computation.26 | convolution fusion | flops 134217728 | bytes 9445376 | tf_op jit(solution)/shard_map/ijc,hij->ch/dot_general | solution.py:142
  228.6 37.3 %psum.23 = f32[128,16]{0,1:T(8,128)} all-reduce(f32[128,16]{0,1:T(8,128)S(1)} %convolution_bitcast_fusion.1), channel_id=1, replica_groups=mesh['row'=4,'col'=8] {'row','col'}, use_global_device_ids=true, to_apply=%region_13.0 | all-reduce | flops 2048 | bytes 16384 | tf_op jit(solution)/shard_map/psum | solution.py:143
  265.9 5.4 %all-reduce.5.cloned.1.call-done = (bf16[256,768]{1,0:T(8,128)(2,1)}, bf16[256,768]{1,0:T(8,128)(2,1)}) async-done(((bf16[256,768]{1,0:T(8,128)(2,1)}, bf16[256,768]{1,0:T(8,128)(2,1)}), (bf16[256,768]{1,0:T(8,128)(2,1)}, bf16[256,768]{1,0:T(8,128)(2,1)})) %all-reduce.5.cloned.1.call-update) | async-done | bytes 786448 | tf_op jit(solution)/shard_map/psum | solution.py:93
  271.2 1.3 convolution_convert_fusion.4
  272.5 14.0 %all_gather.17 = bf16[1024,128]{1,0:T(8,128)(2,1)S(1)} all-gather(bf16[256,128]{1,0:T(8,128)(2,1)S(1)} %convolution_convert_fusion.4), channel_id=1, replica_groups=mesh['row'=4,'col'=8] {'row'}, dimensions={0}, use_global_device_ids=true | all-gather | bytes 327680 | tf_op jit(solution)/shard_map/all_gather | solution.py:96
  286.5 1.0 fusion.2
  287.5 0.3 convert_reduce_fusion
  287.9 0.4 fusion.3
  288.3 13.9 %all_gather.19 = bf16[1024,128]{1,0:T(8,128)(2,1)S(1)} all-gather(bf16[256,128]{1,0:T(8,128)(2,1)S(1)} %fusion.3), channel_id=1, replica_groups=mesh['row'=4,'col'=8] {'row'}, dimensions={0}, use_global_device_ids=true | all-gather | bytes 327680 | tf_op jit(solution)/shard_map/all_gather | solution.py:137
  302.2 1.0 convolution_add_fusion.1
  (61 shorter events, 1.5 us)
Async XLA Ops:
  7.2 152.0 %copy-start = (bf16[3,768,96]{1,2,0:T(8,128)(2,1)S(1)}, bf16[3,768,96]{1,2,0:T(8,128)(2,1)}, u32[]{:S(2)}) copy-start(bf16[3,768,96]{1,2,0:T(8,128)(2,1)} %param.16) | copy-start | bytes 1327108
  7.2 2.6 copy-start.18
  7.2 141.1 %reduce-scatter.3.cloned.1.call-start = ((), (), s32[]{:S(2)}) async-start(), calls=%async_computation.4 | async-start | bytes 1081344 | tf_op jit(solution)/shard_map/reduce_scatter | solution.py:52
  15.4 6.5 %copy-start.19 = (s32[256]{0:T(256)S(1)}, s32[256]{0:T(256)}, u32[]{:S(2)}) copy-start(s32[256]{0:T(256)} %param.11) | copy-start | bytes 3076
  16.7 55.4 %all-to-all-start = ((bf16[16,256,128]{2,1,0:T(8,128)(2,1)}), bf16[16,256,128]{2,1,0:T(8,128)(2,1)S(1)}, u32[]{:S(2)}, u32[]{:S(2)}) async-start(bf16[16,256,128]{2,1,0:T(8,128)(2,1)} %copy.19), calls=%async_computation.1 | async-start | bytes 2097152 | tf_op jit(solution)/shard_map/all_to_all | solution.py:80
  21.9 191.5 %reduce-scatter.5.cloned.1.call-start = ((), (), s32[]{:S(2)}) async-start(), calls=%async_computation.5 | async-start | bytes 491520 | tf_op jit(solution)/shard_map/reduce_scatter | solution.py:127
  72.1 1.0 copy-start.4
  74.9 82.7 %copy-start.13 = (bf16[128,768]{1,0:T(8,128)(2,1)S(1)}, bf16[128,768]{1,0:T(8,128)(2,1)}, u32[]{:S(2)}) copy-start(bf16[128,768]{1,0:T(8,128)(2,1)} %param.15) | copy-start | bytes 589828
  158.9 16.7 %copy-start.2 = (f32[2,256,1024]{2,1,0:T(8,128)S(1)}, f32[2,256,1024]{2,1,0:T(8,128)}, u32[]{:S(2)}) copy-start(f32[2,256,1024]{2,1,0:T(8,128)} %reshape.51) | copy-start | bytes 6291460
  159.6 16.0 %copy-start.10 = (bf16[1,256,96]{1,2,0:T(8,128)(2,1)}, bf16[1,256,96]{1,2,0:T(8,128)(2,1)S(1)}, u32[]{:S(2)}) copy-start(bf16[1,256,96]{1,2,0:T(8,128)(2,1)S(1)} %slice.51) | copy-start | bytes 147460
  176.0 3.8 %copy-start.1 = (f32[2,256,1024]{2,1,0:T(8,128)}, f32[2,256,1024]{2,1,0:T(8,128)S(1)}, u32[]{:S(2)}) copy-start(f32[2,256,1024]{2,1,0:T(8,128)S(1)} %multiply_add_fusion) | copy-start | bytes 6291460
  176.0 1.7 copy-start.7
  176.1 2.8 copy-start.9
  178.0 0.9 copy-start.5
  182.4 2.4 copy-start.3
  184.8 0.8 copy-start.11
  184.8 1.1 copy-start.15
  185.6 1.1 copy-start.20
  202.4 18.9 %all-to-all-start.1 = ((bf16[2,256,1024]{1,0,2:T(2,128)(2,1)}), bf16[2,256,1024]{1,0,2:T(2,128)(2,1)S(1)}, u32[]{:S(2)}, u32[]{:S(2)}) async-start(bf16[2,256,1024]{1,0,2:T(2,128)(2,1)} %copy.21), calls=%async_computation.3 | async-start | bytes 2097152 | tf_op jit(solution)/shard_map/all_to_all | solution.py:141
  206.0 65.3 %all-reduce.5.cloned.1.call-start = ((), (), s32[]{:S(2)}) async-start(), calls=%async_computation.6 | async-start | bytes 1572864 | tf_op jit(solution)/shard_map/psum | solution.py:93
  223.8 47.4 %copy-start.8 = (bf16[768,128]{1,0:T(8,128)(2,1)S(1)}, bf16[768,128]{1,0:T(8,128)(2,1)}, u32[]{:S(2)}) copy-start(bf16[768,128]{1,0:T(8,128)(2,1)} %param.19) | copy-start | bytes 589828
  223.8 62.7 %copy-start.16 = (bf16[256,128]{1,0:T(8,128)(2,1)S(1)}, bf16[256,128]{1,0:T(8,128)(2,1)}, u32[]{:S(2)}) copy-start(bf16[256,128]{1,0:T(8,128)(2,1)} %param.10) | copy-start | bytes 196612
  228.5 59.3 %copy-start.6 = (f32[256,768]{1,0:T(8,128)S(1)}, f32[256,768]{1,0:T(8,128)}, u32[]{:S(2)}) copy-start(f32[256,768]{1,0:T(8,128)} %copy-done.5) | copy-start | bytes 2359300
  228.6 59.3 %copy-start.14 = (bf16[128,768]{1,0:T(8,128)(2,1)S(1)}, bf16[128,768]{1,0:T(8,128)(2,1)}, u32[]{:S(2)}) copy-start(bf16[128,768]{1,0:T(8,128)(2,1)} %param.15) | copy-start | bytes 589828
  271.2 16.3 %copy-start.12 = (bf16[256,768]{1,0:T(8,128)(2,1)S(1)}, bf16[256,768]{1,0:T(8,128)(2,1)}, u32[]{:S(2)}) copy-start(bf16[256,768]{1,0:T(8,128)(2,1)} %get-tuple-element.6) | copy-start | bytes 1179652
  287.5 14.7 %copy-start.17 = (bf16[256,128]{1,0:T(8,128)(2,1)S(1)}, bf16[256,128]{1,0:T(8,128)(2,1)}, u32[]{:S(2)}) copy-start(bf16[256,128]{1,0:T(8,128)(2,1)} %param.12) | copy-start | bytes 196612
Sparse Core Ops, SparseCore 0:
  10.3 137.9 reduce-scatter.2
  186.8 18.5 reduce-scatter.4
  217.1 54.1 all-reduce.4
where the time goes:
time: 311 us; the launch traced here: 310 us
  blocking collectives  150 us (48%)
  waiting for transfers between devices  81.6 us (26%)
  matrix products  34.3 us (11%)
  local copies, waits for them, and re-layouts  14.7 us (5%)
  between operations  14.7 us (5%)
  starting transfers between devices  9.03 us (3%)
  other arithmetic  5.24 us (2%)
    reduce_scatter x1, waiting for transfers between devices, on_device(): lax.psum_scatter(partial_sums, ('row', 'col'), scatter_dimension=0, tiled...  71.8 us
    unnamed x2, blocking collectives  62 us
    psum x1, blocking collectives, on_device(): grad_bias = lax.psum(weight_part, ('row', 'col'))  37.3 us
    all_gather x1, blocking collectives, on_device(): gathered = lax.all_gather(projected[1:], 'row', axis=1, tiled=True)  15.2 us
    all_gather x1, blocking collectives, on_device(): all_back = lax.all_gather(token_back, 'row', axis=0, tiled=True)  14 us
    all_gather x1, blocking collectives, on_device(): all_grad = lax.all_gather(token_grad, 'row', axis=0, tiled=True)  13.9 us
    all_gather x1, blocking collectives, on_device(): lax.all_gather(share_rows, 'col', axis=0, tiled=True)  7.77 us
  transfers between devices with their start and end apart: 5, of which 3 were waited for; matrix products, arithmetic and copies ran while one was open for 10% of the time, Pallas kernels for 0%

commit v1 on v0

--- a/solution.py
+++ b/solution.py
@@ -29,6 +29,35 @@
     return lax.dot_general(
         left, right, (((1,), (1,)), ((), ())), preferred_element_type=jnp.float32
     )
+
+
+def exchange_blocks(blocks, axis):
+    return lax.all_to_all(blocks, axis, split_axis=0, concat_axis=0, tiled=True)
+
+
+def exchange(rows, axis):
+    return exchange_blocks(rows.reshape(lax.axis_size(axis), -1, rows.shape[-1]), axis)
+
+
+def gather(block, axis):
+    return exchange_blocks(
+        jnp.broadcast_to(block[None], (lax.axis_size(axis),) + block.shape), axis
+    )
+
+
+def share_order(token, tok_rows, share):
+    row, inside = token // tok_rows, token % tok_rows
+    return (inside // share * lax.axis_size("row") + row) * share + inside % share
+
+
+def split_two(values):
+    high = lax.reduce_precision(values, exponent_bits=8, mantissa_bits=7)
+    return jnp.concatenate([high, values - high], axis=-1).astype(jnp.bfloat16)
+
+
+def join_two(terms):
+    high, low = jnp.split(terms.astype(jnp.float32), 2, axis=-1)
+    return high + low
 
 
 def on_device(
@@ -40,28 +69,28 @@
     local_heads = width // HD
     atom_width = atom_single.shape[1]
     scale = 1.0 / math.sqrt(HD)
-    onehot = (atom_token[:, None] == jnp.arange(total_tokens, dtype=jnp.int32)[None, :]).astype(
-        jnp.bfloat16
-    )
-    stacked = jnp.concatenate([atom_single, atom_cot], axis=1)
+    share = tok_rows // lax.axis_size("col")
+    onehot = (
+        share_order(atom_token, tok_rows, share)[:, None]
+        == jnp.arange(total_tokens, dtype=jnp.int32)[None, :]
+    ).astype(jnp.bfloat16)
+    stacked = jnp.concatenate([atom_single, atom_cot, jnp.ones_like(atom_cot)], axis=1)
     partial_sums = lax.dot_general(
         onehot, stacked, (((0,), (0,)), ((), ())), preferred_element_type=jnp.float32
-    )
-    partial_counts = jnp.sum(onehot.astype(jnp.float32), axis=0)
-    share_sums, share_counts = (
-        lax.psum_scatter(partial_sums, ("row", "col"), scatter_dimension=0, tiled=True),
-        lax.psum_scatter(partial_counts, ("row", "col"), scatter_dimension=0, tiled=True),
-    )
+    ).astype(jnp.bfloat16)
+    col_sums = jnp.sum(exchange(partial_sums, "col").astype(jnp.float32), axis=0)
+    share_sums = jnp.sum(exchange(col_sums, "row"), axis=0)
+    share_counts = share_sums[:, 2 * atom_width :]
     share_rows = jnp.concatenate(
-        [share_sums[:, :atom_width] / share_counts[:, None], share_sums[:, atom_width:]], axis=1
+        [
+            share_sums[:, :atom_width] / share_counts,
+            share_sums[:, atom_width:],
+        ],
+        axis=1,
     ).astype(jnp.bfloat16)
-    row_pooled, row_counts = (
-        lax.all_gather(share_rows, "col", axis=0, tiled=True),
-        lax.all_gather(share_counts.astype(jnp.bfloat16), "col", axis=0, tiled=True),
-    )
+    row_pooled = gather(share_rows, "col").reshape(tok_rows, 3 * atom_width)
     pooled = row_pooled[:, :atom_width]
-    cot_pooled = row_pooled[:, atom_width:]
-    counts = row_counts.astype(jnp.float32)
+    cot_pooled = row_pooled[:, atom_width : 2 * atom_width]
     single = token_cond.astype(jnp.float32) + jnp.dot(
         pooled, w_pool, preferred_element_type=jnp.float32
     )
@@ -70,7 +99,7 @@
     projected = jnp.einsum("td,kdf->ktf", normed, w_qkv, preferred_element_type=jnp.float32).astype(
         jnp.bfloat16
     )
-    gathered = lax.all_gather(projected[1:], "row", axis=1, tiled=True)
+    gathered = jnp.swapaxes(gather(projected[1:], "row"), 0, 1)
     queries = projected[0].reshape(tok_rows, local_heads, HD)
     keys_all = gathered[0].reshape(total_tokens, local_heads, HD)
     values_all = gathered[1].reshape(total_tokens, local_heads, HD)
@@ -90,14 +119,6 @@
         .reshape(tok_rows, width)
     )
     partial_update = jnp.dot(attended, w_out, preferred_element_type=jnp.float32)
-    update = lax.psum(partial_update.astype(jnp.bfloat16), "col").astype(jnp.float32)
-    token_out = (single + update).astype(jnp.bfloat16)
-    token_back = jnp.dot(token_out, w_dec, preferred_element_type=jnp.float32).astype(jnp.bfloat16)
-    all_back = lax.all_gather(token_back, "row", axis=0, tiled=True)
-    atom_out = (
-        atom_single.astype(jnp.float32)
-        + jnp.dot(onehot, all_back, preferred_element_type=jnp.float32)
-    ).astype(jnp.bfloat16)
     grad_out = transposed_dot(cot_pooled, w_dec)
     grad_update = grad_out.astype(jnp.bfloat16)
     grad_attended = (
@@ -124,23 +145,46 @@
             ),
         ]
     ).reshape(2, total_tokens, width)
-    key_sums = lax.psum_scatter(
-        key_terms.astype(jnp.bfloat16), "row", scatter_dimension=1, tiled=True
-    ).astype(jnp.float32)
+    key_blocks = jnp.swapaxes(
+        key_terms.astype(jnp.bfloat16).reshape(2, -1, tok_rows, width), 0, 1
+    )
+    key_sums = jnp.sum(exchange_blocks(key_blocks, "row").astype(jnp.float32), axis=0)
     grad_keys = (key_sums[0] * scale).astype(jnp.bfloat16)
     grad_values = key_sums[1].astype(jnp.bfloat16)
     grad_proj = jnp.stack([grad_queries, grad_keys, grad_values])
     normed_part = jnp.einsum("ktf,kdf->td", grad_proj, w_qkv, preferred_element_type=jnp.float32)
-    grad_normed = lax.psum(normed_part.astype(jnp.bfloat16), "col").astype(jnp.float32)
-    grad_single = (grad_out + norm_grad(grad_normed, normal, inverse)).astype(jnp.bfloat16)
-    token_grad = (transposed_dot(grad_single, w_pool) / counts[:, None]).astype(jnp.bfloat16)
-    all_grad = lax.all_gather(token_grad, "row", axis=0, tiled=True)
-    grad_atom = atom_cot.astype(jnp.float32) + jnp.dot(
-        onehot, all_grad, preferred_element_type=jnp.float32
-    )
+    width_all = partial_update.shape[1]
+    both = jnp.concatenate([partial_update, normed_part], axis=1).astype(jnp.bfloat16)
     bias_back = lax.all_to_all(grad_logits, "col", split_axis=2, concat_axis=0, tiled=True)
-    weight_part = jnp.einsum("ijc,hij->ch", pair, bias_back, preferred_element_type=jnp.float32)
-    grad_bias = lax.psum(weight_part, ("row", "col"))
+    both_sums = jnp.sum(exchange(both, "col").astype(jnp.float32), axis=0)
+    weight_part = jnp.einsum("ijc,hij->hc", pair, bias_back, preferred_element_type=jnp.float32)
+
+    def mine(rows):
+        return lax.dynamic_slice_in_dim(rows, lax.axis_index("col") * share, share, axis=0)
+
+    token_out = (mine(single) + both_sums[:, :width_all]).astype(jnp.bfloat16)
+    token_back = jnp.dot(token_out, w_dec, preferred_element_type=jnp.float32).astype(jnp.bfloat16)
+    grad_normed = both_sums[:, width_all:]
+    grad_single = (mine(grad_out) + norm_grad(grad_normed, mine(normal), mine(inverse))).astype(
+        jnp.bfloat16
+    )
+    token_grad = (transposed_dot(grad_single, w_pool) / share_counts[:, :atom_width]).astype(
+        jnp.bfloat16
+    )
+    share_back = jnp.concatenate([token_back, token_grad], axis=1)
+    first = gather(jnp.concatenate([share_back, split_two(weight_part)], axis=0), "row")
+    row_weight = jnp.sum(join_two(first[:, share:]), axis=0)
+    second = gather(
+        jnp.concatenate(
+            [first[:, :share].reshape(-1, 2 * atom_width), split_two(row_weight)], axis=0
+        ),
+        "col",
+    )
+    grad_bias = jnp.sum(join_two(second[:, -weight_part.shape[0] :]), axis=0).T
+    all_back = second[:, : -weight_part.shape[0]].reshape(total_tokens, 2 * atom_width)
+    picked = jnp.dot(onehot, all_back, preferred_element_type=jnp.float32)
+    atom_out = (atom_single.astype(jnp.float32) + picked[:, :atom_width]).astype(jnp.bfloat16)
+    grad_atom = atom_cot.astype(jnp.float32) + picked[:, atom_width:]
     return (atom_out, grad_atom, grad_bias)
 
 

time: 311 us -> 172 us (0.55)
  blocking collectives: 150 us -> 50.2 us
  waiting for transfers between devices: 81.6 us -> 33.2 us
  starting transfers between devices: 9.03 us -> 26.7 us
  between operations: 14.7 us -> 1.23 us
  other arithmetic: 5.24 us -> 10 us
  local copies, waits for them, and re-layouts: 14.7 us -> 18.9 us
  matrix products: 34.3 us -> 30.4 us
    reduce_scatter x2 -> x0, waiting for transfers between devices: 71.8 us -> none  [the longest x1 71.8 us: on_device(): lax.psum_scatter(partial_sums, ('row', 'col'), scatter_dimension=0, tiled...]
    unnamed x2 -> x0, blocking collectives: 62 us -> none
    all_gather x4 -> x0, blocking collectives: 50.9 us -> none  [the longest x1 15.2 us: on_device(): gathered = lax.all_gather(projected[1:], 'row', axis=1, tiled=True)]
    all_to_all x0 -> x4, blocking collectives: none -> 50.2 us  [exchange_blocks(): return lax.all_to_all(blocks, axis, split_axis=0, concat_axis=0, tiled=True)]
    psum x1 -> x0, blocking collectives: 37.3 us -> none  [on_device(): grad_bias = lax.psum(weight_part, ('row', 'col'))]
    all_to_all x0 -> x4, starting transfers between devices: none -> 16.3 us  [exchange_blocks(): return lax.all_to_all(blocks, axis, split_axis=0, concat_axis=0, tiled=True)]
    all_to_all x1, waiting for transfers between devices: 0.01 us -> 14.3 us  [on_device(): lax.all_to_all(bias_local, 'col', split_axis=0, concat_axis=2, tiled=True)]
    all_to_all x1, waiting for transfers between devices: 4.37 us -> 11.8 us  [on_device(): lax.all_to_all(grad_logits, 'col', split_axis=2, concat_axis=0, tiled=True)]
  transfers between devices with their start and end apart: 5 -> 6, of which waited for: 3 -> 5; matrix products, arithmetic and copies ran while one was open for 10% -> 20% of each run, Pallas kernels for 0% -> 0%
where the time goes in v1:
time: 172 us; the launch traced here: 171 us
  blocking collectives  50.2 us (29%)
  waiting for transfers between devices  33.2 us (19%)
  matrix products  30.4 us (18%)
  starting transfers between devices  26.7 us (16%)
  local copies, waits for them, and re-layouts  18.9 us (11%)
  other arithmetic  10 us (6%)
    all_to_all x4, blocking collectives, exchange_blocks(): return lax.all_to_all(blocks, axis, split_axis=0, concat_axis=0, tiled=True)  50.2 us
    all_to_all x4, starting transfers between devices, exchange_blocks(): return lax.all_to_all(blocks, axis, split_axis=0, concat_axis=0, tiled=True)  16.3 us
    all_to_all x1, waiting for transfers between devices, on_device(): lax.all_to_all(bias_local, 'col', split_axis=0, concat_axis=2, tiled=True)  14.3 us
    all_to_all x1, waiting for transfers between devices, on_device(): lax.all_to_all(grad_logits, 'col', split_axis=2, concat_axis=0, tiled=True)  11.8 us
    all_to_all x4, waiting for transfers between devices, exchange_blocks(): return lax.all_to_all(blocks, axis, split_axis=0, concat_axis=0, tiled=True)  7.14 us
    all_to_all x1, starting transfers between devices, on_device(): lax.all_to_all(grad_logits, 'col', split_axis=2, concat_axis=0, tiled=True)  6.26 us
    dot_general x1, matrix products, on_device(): jnp.einsum('ijc,ch->hij', pair, w_bias, preferred_element_type=jnp.float32)  5.66 us
    dot_general x1, matrix products, on_device(): jnp.einsum('ijc,hij->hc', pair, bias_back, preferred_element_type=jnp.flo...  4.69 us
  transfers between devices with their start and end apart: 6, of which 5 were waited for; matrix products, arithmetic and copies ran while one was open for 20% of the time, Pallas kernels for 0%

profile of v1, /device:TPU:0, one launch (start us, length us, event | category | flops | bytes accessed | tf_op | source)
XLA Modules:
  0.0 170.6 jit_solution(13293646140144373709)
XLA Ops:
  0.6 0.8 fusion.43
  1.4 1.4 convolution_convert_fusion.1
  2.9 17.5 %all_to_all.67 = bf16[8,128,384]{2,1,0:T(8,128)(2,1)S(1)} all-to-all(bf16[8,128,384]{2,1,0:T(8,128)(2,1)S(1)} %bitcast.89), channel_id=1, replica_groups=mesh['row'=4,'col'=8] {'col'}, dimensions={0} | all-to-all | bytes 1572864 | tf_op jit(solution)/shard_map/all_to_all | solution.py:35
  20.5 11.5 %all_to_all.68 = f32[4,32,384]{2,1,0:T(8,128)S(1)} all-to-all(f32[4,32,384]{2,1,0:T(8,128)S(1)} %bitcast.90), channel_id=1, replica_groups=mesh['row'=4,'col'=8] {'row'}, dimensions={0} | all-to-all | bytes 393216 | tf_op jit(solution)/shard_map/all_to_all | solution.py:35
  32.1 0.7 broadcast_in_dim.11
  32.8 3.4 %all-to-all-start.2 = ((bf16[8,32,384]{2,1,0:T(8,128)(2,1)}), bf16[8,32,384]{2,1,0:T(8,128)(2,1)S(1)}, u32[]{:S(2)}, u32[]{:S(2)}) async-start(bf16[8,32,384]{2,1,0:T(8,128)(2,1)} %broadcast_in_dim.11), calls=%async_computation.2 | async-start | bytes 393216 | tf_op jit(solution)/shard_map/all_to_all | solution.py:35
  36.2 5.7 %convolution_convert_fusion = bf16[16,256,128]{2,0,1:T(8,128)(2,1)S(1)} fusion(bf16[256,128,128]{2,1,0:T(8,128)(2,1)} %param.14, bf16[128,16]{0,1:T(8,128)(2,1)S(1)} %copy-done.21), kind=kOutput, calls=%fused_computation.8 | convolution fusion | flops 134742016 | bytes 9441280 | tf_op jit(solution)/shard_map/ijc,ch->hij/dot_general | solution.py:106
  41.9 1.3 copy.30
  43.2 4.1 %all-to-all-start.4 = ((bf16[16,256,128]{2,1,0:T(8,128)(2,1)}), bf16[16,256,128]{2,1,0:T(8,128)(2,1)S(1)}, u32[]{:S(2)}, u32[]{:S(2)}) async-start(bf16[16,256,128]{2,1,0:T(8,128)(2,1)} %copy.30), calls=%async_computation.4 | async-start | bytes 2097152 | tf_op jit(solution)/shard_map/all_to_all | solution.py:109
  48.4 14.3 %all-to-all-done.4 = bf16[16,256,128]{2,1,0:T(8,128)(2,1)S(1)} async-done(((bf16[16,256,128]{2,1,0:T(8,128)(2,1)}), bf16[16,256,128]{2,1,0:T(8,128)(2,1)S(1)}, u32[]{:S(2)}, u32[]{:S(2)}) %all-to-all-start.4) | async-done | bytes 1048608 | tf_op jit(solution)/shard_map/all_to_all | solution.py:109
  62.7 0.8 broadcast_in_dim.12
  63.5 4.1 %all-to-all-start.3 = ((bf16[4,2,256,96]{2,3,1,0:T(8,128)(2,1)}), bf16[4,2,256,96]{2,3,1,0:T(8,128)(2,1)}, u32[]{:S(2)}, u32[]{:S(2)}) async-start(bf16[4,2,256,96]{2,3,1,0:T(8,128)(2,1)} %broadcast_in_dim.12), calls=%async_computation.3 | async-start | bytes 786432 | tf_op jit(solution)/shard_map/all_to_all | solution.py:35
  67.6 1.8 %copy.38 = f32[8,2,256,128]{3,0,2,1:T(8,128)S(1)} copy(bf16[8,2,256,128]{3,2,1,0:T(8,128)(2,1)} %bitcast.86) | data formatting | bytes 3145728 | tf_op jit(solution)/shard_map/convert_element_type | solution.py:112
  69.5 1.5 reshape.110
  71.0 1.4 slice.84
  72.4 1.1 fusion.30
  73.6 0.9 copy-done.5
  74.5 1.8 %convolution_convert_fusion.6 = bf16[256,96]{0,1:T(8,128)(2,1)} fusion(bf16[96,768]{1,0:T(8,128)(2,1)} %param.18, f32[256,768]{1,0:T(8,128)S(1)} %fusion.30), kind=kOutput, calls=%fused_computation.21 | convolution fusion | flops 37969920 | bytes 983040 | tf_op jit(solution)/shard_map/dot_general | solution.py:29
  76.9 1.0 fusion.48
  78.4 0.8 reshape_squeeze.9
  79.2 2.1 %multiply_add_fusion = f32[2,256,1024]{2,1,0:T(8,128)S(1)} fusion(f32[2,256,1024]{2,1,0:T(8,128)} %reshape.110, bf16[256,2,48]{0,2,1:T(8,128)(2,1)} %bitcast.94, bf16[1024,2,48]{0,2,1:T(8,128)(2,1)S(1)} %reshape_squeeze.11), kind=kOutput, calls=%fused_computation.5 | convolution fusion | flops 51380224 | bytes 4440064 | tf_op jit(solution)/shard_map/ihd,jhd->hij/dot_general | solution.py:110
  81.3 1.9 %fusion.50 = (f32[2,256]{1,0:T(2,128)S(1)}, f32[2,256,1024]{2,1,0:T(8,128)}) fusion(f32[2,256,1024]{2,1,0:T(8,128)S(1)} %multiply_add_fusion), kind=kOutput, calls=%fused_computation.112 | output fusion | flops 1049599 | bytes 4196352 | tf_op jit(solution)/shard_map/sub | solution.py:113
  83.2 2.6 %fusion.3 = bf16[1024,2,48]{0,2,1:T(8,128)(2,1)} fusion(bf16[256,2,48]{0,2,1:T(8,128)(2,1)} %bitcast.99, f32[2,256]{1,0:T(2,128)S(1)} %get-tuple-element.15, f32[2,256,1024]{2,1,0:T(8,128)S(1)} %multiply_add_fusion), kind=kOutput, calls=%fused_computation.17 | convolution fusion | flops 52004352 | bytes 2344960 | tf_op jit(solution)/shard_map/hij,ihd->jhd/dot_general | solution.py:143
  85.7 1.1 stack.15
  86.8 2.4 %multiply_reduce_fusion = (f32[2,256]{1,0:T(2,128)S(1)}, f32[2,256,1024]{2,1,0:T(8,128)S(1)}) fusion(f32[2,256,1024]{2,1,0:T(8,128)} %get-tuple-element.16, f32[2,256]{1,0:T(2,128)S(1)} %get-tuple-element.15, bf16[256,2,48]{0,2,1:T(8,128)(2,1)} %bitcast.100, bf16[1024,2,48]{0,2,1:T(8,128)(2,1)} %reshape_squeeze.9), kind=kOutput, calls=%fused_computation.3 | convolution fusion | flops 51904000 | bytes 4444160 | tf_op jit(solution)/shard_map/ihd,jhd->hij/dot_general | solution.py:127
  90.6 0.8 maximum_bitcast_fusion
  91.3 4.4 %all-to-all-start.5 = ((bf16[4,2,256,96]{2,3,1,0:T(8,128)(2,1)}), bf16[4,2,256,96]{2,3,1,0:T(8,128)(2,1)S(1)}, u32[]{:S(2)}, u32[]{:S(2)}) async-start(bf16[4,2,256,96]{2,3,1,0:T(8,128)(2,1)} %maximum_bitcast_fusion), calls=%async_computation.5 | async-start | bytes 786432 | tf_op jit(solution)/shard_map/all_to_all | solution.py:35
  95.8 2.1 %copy.35 = bf16[2,256,1024]{1,0,2:T(2,128)(2,1)} copy(bf16[2,256,1024]{2,1,0:T(8,128)(2,1)S(1)} %multiply_convert_fusion) | data formatting | bytes 2097152 | tf_op jit(solution)/shard_map/convert_element_type | solution.py:131
  97.8 3.4 %fusion.5 = bf16[256,2,48]{0,2,1:T(8,128)(2,1)S(1)} fusion(bf16[1024,2,48]{0,2,1:T(8,128)(2,1)S(1)} %copy-done.17, f32[2,256]{1,0:T(2,128)S(1)} %get-tuple-element.15, f32[2,256,1024]{2,1,0:T(8,128)} %copy-done.1), kind=kOutput, calls=%fused_computation.22 | convolution fusion | flops 51930624 | bytes 2344960 | tf_op jit(solution)/shard_map/hij,jhd->ihd/dot_general | solution.py:117
  101.4 0.7 dot_general.62
  102.2 1.1 fusion.4
  103.2 1.4 all-to-all-done.5
  104.7 0.7 copy-done.6
  105.4 6.3 %all-to-all-start.7 = ((bf16[2,256,1024]{1,0,2:T(2,128)(2,1)}), bf16[2,256,1024]{1,0,2:T(2,128)(2,1)S(1)}, u32[]{:S(2)}, u32[]{:S(2)}) async-start(bf16[2,256,1024]{1,0,2:T(2,128)(2,1)} %copy.35), calls=%async_computation.7 | async-start | bytes 2097152 | tf_op jit(solution)/shard_map/all_to_all | solution.py:158
  111.7 1.1 convolution_convert_fusion.2
  112.8 1.1 convert_reduce_fusion.2
  114.3 0.9 pad_maximum_fusion
  115.3 11.8 %all-to-all-done.7 = bf16[2,256,1024]{1,0,2:T(2,128)(2,1)S(1)} async-done(((bf16[2,256,1024]{1,0,2:T(2,128)(2,1)}), bf16[2,256,1024]{1,0,2:T(2,128)(2,1)S(1)}, u32[]{:S(2)}, u32[]{:S(2)}) %all-to-all-start.7) | async-done | bytes 1048608 | tf_op jit(solution)/shard_map/all_to_all | solution.py:158
  127.1 4.4 %all-to-all-start.6 = ((bf16[8,32,1536]{2,1,0:T(8,128)(2,1)}), bf16[8,32,1536]{2,1,0:T(8,128)(2,1)}, u32[]{:S(2)}, u32[]{:S(2)}) async-start(bf16[8,32,1536]{2,1,0:T(8,128)(2,1)} %pad_maximum_fusion), calls=%async_computation.6 | async-start | bytes 1572864 | tf_op jit(solution)/shard_map/all_to_all | solution.py:35
  131.5 2.5 %copy.36 = bf16[2,256,8,128]{3,0,2,1:T(2,128)(2,1)S(1)} copy(bf16[2,256,8,128]{1,0,3,2:T(2,128)(2,1)S(1)} %bitcast.87) | data formatting | bytes 2097152 | tf_op jit(solution)/shard_map/all_to_all | solution.py:158
  134.1 4.7 %reduce-precision_convert_fusion.1 = (bf16[16,128]{1,0:T(8,128)(2,1)S(1)}, bf16[16,128]{1,0:T(8,128)(2,1)S(1)}) fusion(bf16[16,256,128]{2,0,1:T(8,128)(2,1)S(1)} %bitcast.84, bf16[256,128,128]{2,1,0:T(8,128)(2,1)} %param.14), kind=kOutput, calls=%fused_computation.86 | convolution fusion | flops 134225920 | bytes 9445376 | tf_op jit(solution)/shard_map/ijc,hij->hc/dot_general | solution.py:160
  138.8 5.1 %all-to-all-done.6 = bf16[8,32,1536]{2,1,0:T(8,128)(2,1)} async-done(((bf16[8,32,1536]{2,1,0:T(8,128)(2,1)}), bf16[8,32,1536]{2,1,0:T(8,128)(2,1)}, u32[]{:S(2)}, u32[]{:S(2)}) %all-to-all-start.6) | async-done | bytes 786464 | tf_op jit(solution)/shard_map/all_to_all | solution.py:35
  143.9 1.3 convert_reduce_fusion
  145.3 1.0 slice_reduce_fusion
  146.4 1.2 fusion.6
  147.6 8.4 %all_to_all.69 = bf16[4,48,256]{2,1,0:T(8,128)(2,1)S(1)} all-to-all(bf16[4,48,256]{2,1,0:T(8,128)(2,1)S(1)} %broadcast_in_dim.13), channel_id=1, replica_groups=mesh['row'=4,'col'=8] {'row'}, dimensions={0} | all-to-all | bytes 196608 | tf_op jit(solution)/shard_map/all_to_all | solution.py:35
  156.1 12.8 %all_to_all.70 = bf16[8,144,256]{2,1,0:T(8,128)(2,1)S(1)} all-to-all(bf16[8,144,256]{2,1,0:T(8,128)(2,1)S(1)} %broadcast_in_dim.14), channel_id=1, replica_groups=mesh['row'=4,'col'=8] {'col'}, dimensions={0} | all-to-all | bytes 1179648 | tf_op jit(solution)/shard_map/all_to_all | solution.py:35
  169.9 0.7 slice_add_fusion
  (86 shorter events, 5.5 us)
Async XLA Ops:
  0.6 47.4 %copy-start = (bf16[3,768,96]{1,2,0:T(8,128)(2,1)S(1)}, bf16[3,768,96]{1,2,0:T(8,128)(2,1)}, u32[]{:S(2)}) copy-start(bf16[3,768,96]{1,2,0:T(8,128)(2,1)} %param.16) | copy-start | bytes 1327108
  2.9 33.3 %copy-start.21 = (bf16[128,16]{0,1:T(8,128)(2,1)S(1)}, bf16[128,16]{0,1:T(8,128)(2,1)}, u32[]{:S(2)}) copy-start(bf16[128,16]{0,1:T(8,128)(2,1)} %param.17) | copy-start | bytes 12292
  32.0 9.8 %copy-start.15 = (f32[32,384]{1,0:T(8,128)}, f32[32,384]{1,0:T(8,128)S(1)}, u32[]{:S(2)}) copy-start(f32[32,384]{1,0:T(8,128)S(1)} %reduce_sum.109) | copy-start | bytes 147460
  32.8 10.4 %all-to-all-start.2 = ((bf16[8,32,384]{2,1,0:T(8,128)(2,1)}), bf16[8,32,384]{2,1,0:T(8,128)(2,1)S(1)}, u32[]{:S(2)}, u32[]{:S(2)}) async-start(bf16[8,32,384]{2,1,0:T(8,128)(2,1)} %broadcast_in_dim.11), calls=%async_computation.2 | async-start | bytes 393216 | tf_op jit(solution)/shard_map/all_to_all | solution.py:35
  41.9 5.4 %copy-start.9 = (bf16[128,768]{1,0:T(8,128)(2,1)S(1)}, bf16[128,768]{1,0:T(8,128)(2,1)}, u32[]{:S(2)}) copy-start(bf16[128,768]{1,0:T(8,128)(2,1)} %param.15) | copy-start | bytes 589828
  41.9 5.4 %copy-start.14 = (bf16[256,768]{1,0:T(8,128)(2,1)S(1)}, bf16[256,768]{1,0:T(8,128)(2,1)}, u32[]{:S(2)}) copy-start(bf16[256,768]{1,0:T(8,128)(2,1)} %param.13) | copy-start | bytes 1179652
  43.1 4.7 %copy-start.12 = (bf16[8,32,384]{2,1,0:T(8,128)(2,1)}, bf16[8,32,384]{2,1,0:T(8,128)(2,1)S(1)}, u32[]{:S(2)}) copy-start(bf16[8,32,384]{2,1,0:T(8,128)(2,1)S(1)} %all-to-all-done.2) | copy-start | bytes 589828
  43.2 19.5 %all-to-all-start.4 = ((bf16[16,256,128]{2,1,0:T(8,128)(2,1)}), bf16[16,256,128]{2,1,0:T(8,128)(2,1)S(1)}, u32[]{:S(2)}, u32[]{:S(2)}) async-start(bf16[16,256,128]{2,1,0:T(8,128)(2,1)} %copy.30), calls=%async_computation.4 | async-start | bytes 2097152 | tf_op jit(solution)/shard_map/all_to_all | solution.py:109
  48.0 19.6 %copy-start.4 = (f32[256,768]{1,0:T(8,128)}, f32[256,768]{1,0:T(8,128)S(1)}, u32[]{:S(2)}) copy-start(f32[256,768]{1,0:T(8,128)S(1)} %subtract_multiply_fusion) | copy-start | bytes 2359300
  48.4 19.2 %copy-start.11 = (bf16[3,256,96]{1,2,0:T(8,128)(2,1)}, bf16[3,256,96]{1,2,0:T(8,128)(2,1)S(1)}, u32[]{:S(2)}) copy-start(bf16[3,256,96]{1,2,0:T(8,128)(2,1)S(1)} %convert_bitcast_fusion) | copy-start | bytes 442372
  62.7 5.0 %copy-start.3 = (bf16[16,256,128]{2,1,0:T(8,128)(2,1)}, bf16[16,256,128]{2,1,0:T(8,128)(2,1)S(1)}, u32[]{:S(2)}) copy-start(bf16[16,256,128]{2,1,0:T(8,128)(2,1)S(1)} %all-to-all-done.4) | copy-start | bytes 3145732
  63.5 13.4 %all-to-all-start.3 = ((bf16[4,2,256,96]{2,3,1,0:T(8,128)(2,1)}), bf16[4,2,256,96]{2,3,1,0:T(8,128)(2,1)}, u32[]{:S(2)}, u32[]{:S(2)}) async-start(bf16[4,2,256,96]{2,3,1,0:T(8,128)(2,1)} %broadcast_in_dim.12), calls=%async_computation.3 | async-start | bytes 786432 | tf_op jit(solution)/shard_map/all_to_all | solution.py:35
  69.5 3.0 %copy-start.7 = (bf16[768,128]{1,0:T(8,128)(2,1)S(1)}, bf16[768,128]{1,0:T(8,128)(2,1)}, u32[]{:S(2)}) copy-start(bf16[768,128]{1,0:T(8,128)(2,1)} %param.19) | copy-start | bytes 589828
  73.5 0.9 copy-start.5
  81.3 1.9 %copy-start.1 = (f32[2,256,1024]{2,1,0:T(8,128)}, f32[2,256,1024]{2,1,0:T(8,128)S(1)}, u32[]{:S(2)}) copy-start(f32[2,256,1024]{2,1,0:T(8,128)S(1)} %multiply_add_fusion) | copy-start | bytes 6291460
  86.8 2.4 %copy-start.2 = (f32[2,256,1024]{2,1,0:T(8,128)S(1)}, f32[2,256,1024]{2,1,0:T(8,128)}, u32[]{:S(2)}) copy-start(f32[2,256,1024]{2,1,0:T(8,128)} %get-tuple-element.16) | copy-start | bytes 6291460
  89.3 0.8 copy-start.13
  90.5 7.3 %copy-start.17 = (bf16[1024,2,48]{0,2,1:T(8,128)(2,1)S(1)}, bf16[1024,2,48]{0,2,1:T(8,128)(2,1)}, u32[]{:S(2)}) copy-start(bf16[1024,2,48]{0,2,1:T(8,128)(2,1)} %reshape_squeeze.9) | copy-start | bytes 589828
  91.3 13.3 %all-to-all-start.5 = ((bf16[4,2,256,96]{2,3,1,0:T(8,128)(2,1)}), bf16[4,2,256,96]{2,3,1,0:T(8,128)(2,1)S(1)}, u32[]{:S(2)}, u32[]{:S(2)}) async-start(bf16[4,2,256,96]{2,3,1,0:T(8,128)(2,1)} %maximum_bitcast_fusion), calls=%async_computation.5 | async-start | bytes 786432 | tf_op jit(solution)/shard_map/all_to_all | solution.py:35
  103.2 8.4 %copy-start.16 = (bf16[8,32,96]{2,1,0:T(8,128)(2,1)S(1)}, bf16[8,32,96]{2,1,0:T(8,128)(2,1)}, u32[]{:S(2)}) copy-start(bf16[8,32,96]{2,1,0:T(8,128)(2,1)} %dot_general.62) | copy-start | bytes 147460
  103.2 10.7 %copy-start.20 = (bf16[2,48,256]{2,1,0:T(8,128)(2,1)S(1)}, bf16[2,48,256]{2,1,0:T(8,128)(2,1)}, u32[]{:S(2)}) copy-start(bf16[2,48,256]{2,1,0:T(8,128)(2,1)} %fusion.4) | copy-start | bytes 147460
  104.7 0.7 copy-start.6
  105.4 21.7 %all-to-all-start.7 = ((bf16[2,256,1024]{1,0,2:T(2,128)(2,1)}), bf16[2,256,1024]{1,0,2:T(2,128)(2,1)S(1)}, u32[]{:S(2)}, u32[]{:S(2)}) async-start(bf16[2,256,1024]{1,0,2:T(2,128)(2,1)} %copy.35), calls=%async_computation.7 | async-start | bytes 2097152 | tf_op jit(solution)/shard_map/all_to_all | solution.py:158
  127.1 16.8 %all-to-all-start.6 = ((bf16[8,32,1536]{2,1,0:T(8,128)(2,1)}), bf16[8,32,1536]{2,1,0:T(8,128)(2,1)}, u32[]{:S(2)}, u32[]{:S(2)}) async-start(bf16[8,32,1536]{2,1,0:T(8,128)(2,1)} %pad_maximum_fusion), calls=%async_computation.6 | async-start | bytes 1572864 | tf_op jit(solution)/shard_map/all_to_all | solution.py:35
  134.1 11.1 %copy-start.8 = (bf16[768,128]{1,0:T(8,128)(2,1)S(1)}, bf16[768,128]{1,0:T(8,128)(2,1)}, u32[]{:S(2)}) copy-start(bf16[768,128]{1,0:T(8,128)(2,1)} %param.19) | copy-start | bytes 589828
  134.1 12.3 %copy-start.10 = (bf16[128,768]{1,0:T(8,128)(2,1)S(1)}, bf16[128,768]{1,0:T(8,128)(2,1)}, u32[]{:S(2)}) copy-start(bf16[128,768]{1,0:T(8,128)(2,1)} %param.15) | copy-start | bytes 589828
  156.0 13.9 %copy-start.18 = (bf16[256,128]{1,0:T(8,128)(2,1)S(1)}, bf16[256,128]{1,0:T(8,128)(2,1)}, u32[]{:S(2)}) copy-start(bf16[256,128]{1,0:T(8,128)(2,1)} %param.12) | copy-start | bytes 196612
  156.0 13.9 %copy-start.19 = (bf16[256,128]{1,0:T(8,128)(2,1)S(1)}, bf16[256,128]{1,0:T(8,128)(2,1)}, u32[]{:S(2)}) copy-start(bf16[256,128]{1,0:T(8,128)(2,1)} %param.10) | copy-start | bytes 196612

commit v2 on v1

--- a/solution.py
+++ b/solution.py
@@ -1,8 +1,11 @@
+import functools
 import math
 
 import jax
 import jax.numpy as jnp
 from jax import lax
+from jax.experimental import pallas as pl
+from jax.experimental.pallas import tpu as pltpu
 from jax.sharding import PartitionSpec as P
 
 HD = 48
@@ -35,10 +38,6 @@
     return lax.all_to_all(blocks, axis, split_axis=0, concat_axis=0, tiled=True)
 
 
-def exchange(rows, axis):
-    return exchange_blocks(rows.reshape(lax.axis_size(axis), -1, rows.shape[-1]), axis)
-
-
 def gather(block, axis):
     return exchange_blocks(
         jnp.broadcast_to(block[None], (lax.axis_size(axis),) + block.shape), axis
@@ -50,14 +49,232 @@
     return (inside // share * lax.axis_size("row") + row) * share + inside % share
 
 
-def split_two(values):
-    high = lax.reduce_precision(values, exponent_bits=8, mantissa_bits=7)
-    return jnp.concatenate([high, values - high], axis=-1).astype(jnp.bfloat16)
-
-
-def join_two(terms):
-    high, low = jnp.split(terms.astype(jnp.float32), 2, axis=-1)
-    return high + low
+def push(source, target, send_sems, recv_sems, at, axis, peer):
+    copy = pltpu.make_async_remote_copy(
+        src_ref=source,
+        dst_ref=target,
+        send_sem=send_sems.at[at],
+        recv_sem=recv_sems.at[at],
+        device_id={axis: peer},
+        device_id_type=pl.DeviceIdType.MESH,
+    )
+    copy.start()
+    return copy
+
+
+def peers_of(axis, size):
+    me = lax.axis_index(axis)
+    return [(step, lax.rem(me + step, size)) for step in range(1, size)]
+
+
+def greet(sizes):
+    barrier = pltpu.get_barrier_semaphore()
+    for axis, size in sizes:
+        for _, peer in peers_of(axis, size):
+            pl.semaphore_signal(
+                barrier, inc=1, device_id={axis: peer}, device_id_type=pl.DeviceIdType.MESH
+            )
+    pl.semaphore_wait(barrier, sum(size - 1 for _, size in sizes))
+
+
+def pool_kernel(
+    rows, cols, sums_ref, out_ref, counts_ref, got_col, col_sum, got_row, send_sems, recv_sems
+):
+    row, col = lax.axis_index("row"), lax.axis_index("col")
+    greet((("row", rows), ("col", cols)))
+    width = out_ref.shape[-1] // 3
+    copies = [
+        push(sums_ref.at[peer], got_col.at[step - 1], send_sems, recv_sems, step - 1, "col", peer)
+        for step, peer in peers_of("col", cols)
+    ]
+    total = sums_ref[col].astype(jnp.float32)
+    for at, copy in enumerate(copies):
+        copy.wait()
+        total = total + got_col[at].astype(jnp.float32)
+    col_sum[...] = total.reshape(col_sum.shape)
+    base = cols - 1
+    copies = [
+        push(
+            col_sum.at[peer],
+            got_row.at[step - 1],
+            send_sems,
+            recv_sems,
+            base + step - 1,
+            "row",
+            peer,
+        )
+        for step, peer in peers_of("row", rows)
+    ]
+    total = col_sum[row]
+    for at, copy in enumerate(copies):
+        copy.wait()
+        total = total + got_row[at]
+    counts = total[:, 2 * width :]
+    counts_ref[...] = counts
+    out_ref[col] = jnp.concatenate(
+        [total[:, :width] / counts, total[:, width:]], axis=1
+    ).astype(out_ref.dtype)
+    base += rows - 1
+    copies = [
+        push(
+            out_ref.at[col], out_ref.at[col], send_sems, recv_sems, base + step - 1, "col", peer
+        )
+        for step, peer in peers_of("col", cols)
+    ]
+    for copy in copies:
+        copy.wait()
+
+
+def pool_call(partial_sums, share):
+    rows, cols = lax.axis_size("row"), lax.axis_size("col")
+    width = partial_sums.shape[-1]
+    copies = 2 * (cols - 1) + rows - 1
+    return pl.pallas_call(
+        functools.partial(pool_kernel, rows, cols),
+        out_shape=(
+            jax.ShapeDtypeStruct((cols, share, width), jnp.bfloat16),
+            jax.ShapeDtypeStruct((share, width // 3), jnp.float32),
+        ),
+        in_specs=[pl.BlockSpec(memory_space=pltpu.VMEM)],
+        out_specs=(pl.BlockSpec(memory_space=pltpu.VMEM),) * 2,
+        scratch_shapes=[
+            pltpu.VMEM((cols - 1, rows * share, width), jnp.bfloat16),
+            pltpu.VMEM((rows, share, width), jnp.float32),
+            pltpu.VMEM((rows - 1, share, width), jnp.float32),
+            pltpu.SemaphoreType.DMA((copies,)),
+            pltpu.SemaphoreType.DMA((copies,)),
+        ],
+        compiler_params=pltpu.CompilerParams(collective_id=0, has_side_effects=True),
+    )(partial_sums.reshape(cols, rows * share, width))
+
+
+def tail_kernel(
+    rows,
+    cols,
+    both_ref,
+    single_ref,
+    grad_out_ref,
+    normal_ref,
+    inverse_ref,
+    counts_ref,
+    dec_ref,
+    pool_ref,
+    weight_ref,
+    out_ref,
+    weight_out_ref,
+    got_both,
+    held,
+    row_weights,
+    col_weights,
+    send_sems,
+    recv_sems,
+):
+    row, col = lax.axis_index("row"), lax.axis_index("col")
+    greet((("row", rows), ("col", cols)))
+    width = single_ref.shape[-1]
+    copies = [
+        push(both_ref.at[peer], got_both.at[step - 1], send_sems, recv_sems, step - 1, "col", peer)
+        for step, peer in peers_of("col", cols)
+    ]
+    base = cols - 1
+    row_weights[row] = weight_ref[...]
+    weight_copies = [
+        push(
+            row_weights.at[row],
+            row_weights.at[row],
+            send_sems,
+            recv_sems,
+            base + step - 1,
+            "row",
+            peer,
+        )
+        for step, peer in peers_of("row", rows)
+    ]
+    base += rows - 1
+    total = both_ref[col].astype(jnp.float32)
+    for at, copy in enumerate(copies):
+        copy.wait()
+        total = total + got_both[at].astype(jnp.float32)
+    token_out = (single_ref[...] + total[:, :width]).astype(jnp.bfloat16)
+    token_back = jnp.dot(token_out, dec_ref[...], preferred_element_type=jnp.float32)
+    grad_single = (
+        grad_out_ref[...] + norm_grad(total[:, width:], normal_ref[...], inverse_ref[...])
+    ).astype(jnp.bfloat16)
+    token_grad = transposed_dot(grad_single, pool_ref[...]) / counts_ref[...]
+    held[row] = jnp.concatenate([token_back, token_grad], axis=1).astype(jnp.bfloat16)
+    copies = [
+        push(held.at[row], held.at[row], send_sems, recv_sems, base + step - 1, "row", peer)
+        for step, peer in peers_of("row", rows)
+    ]
+    base += rows - 1
+    for copy in weight_copies:
+        copy.wait()
+    weight = row_weights[0]
+    for at in range(1, rows):
+        weight = weight + row_weights[at]
+    col_weights[col] = weight
+    weight_copies = [
+        push(
+            col_weights.at[col],
+            col_weights.at[col],
+            send_sems,
+            recv_sems,
+            base + step - 1,
+            "col",
+            peer,
+        )
+        for step, peer in peers_of("col", cols)
+    ]
+    base += cols - 1
+    for copy in copies:
+        copy.wait()
+    copies = [
+        push(held, out_ref.at[col], send_sems, recv_sems, base + step - 1, "col", peer)
+        for step, peer in peers_of("col", cols)
+    ]
+    out_ref[col] = held[...]
+    for copy in weight_copies:
+        copy.wait()
+    weight = col_weights[0]
+    for at in range(1, cols):
+        weight = weight + col_weights[at]
+    weight_out_ref[...] = weight
+    for copy in copies:
+        copy.wait()
+
+
+def tail_call(both, single, grad_out, normal, inverse, counts, w_dec, w_pool, weight):
+    rows, cols = lax.axis_size("row"), lax.axis_size("col")
+    share, atom_width = counts.shape
+    copies = 3 * (cols - 1) + 2 * (rows - 1)
+    return pl.pallas_call(
+        functools.partial(tail_kernel, rows, cols),
+        out_shape=(
+            jax.ShapeDtypeStruct((cols, rows, share, 2 * atom_width), jnp.bfloat16),
+            jax.ShapeDtypeStruct(weight.shape, jnp.float32),
+        ),
+        in_specs=[pl.BlockSpec(memory_space=pltpu.VMEM)] * 9,
+        out_specs=(pl.BlockSpec(memory_space=pltpu.VMEM),) * 2,
+        scratch_shapes=[
+            pltpu.VMEM((cols - 1, share, both.shape[-1]), jnp.bfloat16),
+            pltpu.VMEM((rows, share, 2 * atom_width), jnp.bfloat16),
+            pltpu.VMEM((rows,) + weight.shape, jnp.float32),
+            pltpu.VMEM((cols,) + weight.shape, jnp.float32),
+            pltpu.SemaphoreType.DMA((copies,)),
+            pltpu.SemaphoreType.DMA((copies,)),
+        ],
+        compiler_params=pltpu.CompilerParams(collective_id=1, has_side_effects=True),
+    )(
+        both.reshape(cols, share, -1),
+        single,
+        grad_out,
+        normal,
+        inverse,
+        counts,
+        w_dec,
+        w_pool,
+        weight,
+    )
 
 
 def on_device(
@@ -78,17 +295,8 @@
     partial_sums = lax.dot_general(
         onehot, stacked, (((0,), (0,)), ((), ())), preferred_element_type=jnp.float32
     ).astype(jnp.bfloat16)
-    col_sums = jnp.sum(exchange(partial_sums, "col").astype(jnp.float32), axis=0)
-    share_sums = jnp.sum(exchange(col_sums, "row"), axis=0)
-    share_counts = share_sums[:, 2 * atom_width :]
-    share_rows = jnp.concatenate(
-        [
-            share_sums[:, :atom_width] / share_counts,
-            share_sums[:, atom_width:],
-        ],
-        axis=1,
-    ).astype(jnp.bfloat16)
-    row_pooled = gather(share_rows, "col").reshape(tok_rows, 3 * atom_width)
+    row_pooled, share_counts = pool_call(partial_sums, share)
+    row_pooled = row_pooled.reshape(tok_rows, 3 * atom_width)
     pooled = row_pooled[:, :atom_width]
     cot_pooled = row_pooled[:, atom_width : 2 * atom_width]
     single = token_cond.astype(jnp.float32) + jnp.dot(
@@ -153,35 +361,26 @@
     grad_values = key_sums[1].astype(jnp.bfloat16)
     grad_proj = jnp.stack([grad_queries, grad_keys, grad_values])
     normed_part = jnp.einsum("ktf,kdf->td", grad_proj, w_qkv, preferred_element_type=jnp.float32)
-    width_all = partial_update.shape[1]
     both = jnp.concatenate([partial_update, normed_part], axis=1).astype(jnp.bfloat16)
     bias_back = lax.all_to_all(grad_logits, "col", split_axis=2, concat_axis=0, tiled=True)
-    both_sums = jnp.sum(exchange(both, "col").astype(jnp.float32), axis=0)
     weight_part = jnp.einsum("ijc,hij->hc", pair, bias_back, preferred_element_type=jnp.float32)
 
     def mine(rows):
         return lax.dynamic_slice_in_dim(rows, lax.axis_index("col") * share, share, axis=0)
 
-    token_out = (mine(single) + both_sums[:, :width_all]).astype(jnp.bfloat16)
-    token_back = jnp.dot(token_out, w_dec, preferred_element_type=jnp.float32).astype(jnp.bfloat16)
-    grad_normed = both_sums[:, width_all:]
-    grad_single = (mine(grad_out) + norm_grad(grad_normed, mine(normal), mine(inverse))).astype(
-        jnp.bfloat16
-    )
-    token_grad = (transposed_dot(grad_single, w_pool) / share_counts[:, :atom_width]).astype(
-        jnp.bfloat16
-    )
-    share_back = jnp.concatenate([token_back, token_grad], axis=1)
-    first = gather(jnp.concatenate([share_back, split_two(weight_part)], axis=0), "row")
-    row_weight = jnp.sum(join_two(first[:, share:]), axis=0)
-    second = gather(
-        jnp.concatenate(
-            [first[:, :share].reshape(-1, 2 * atom_width), split_two(row_weight)], axis=0
-        ),
-        "col",
-    )
-    grad_bias = jnp.sum(join_two(second[:, -weight_part.shape[0] :]), axis=0).T
-    all_back = second[:, : -weight_part.shape[0]].reshape(total_tokens, 2 * atom_width)
+    all_back, grad_bias = tail_call(
+        both,
+        mine(single),
+        mine(grad_out),
+        mine(normal),
+        mine(inverse),
+        share_counts,
+        w_dec,
+        w_pool,
+        weight_part,
+    )
+    all_back = all_back.reshape(total_tokens, 2 * atom_width)
+    grad_bias = grad_bias.T
     picked = jnp.dot(onehot, all_back, preferred_element_type=jnp.float32)
     atom_out = (atom_single.astype(jnp.float32) + picked[:, :atom_width]).astype(jnp.bfloat16)
     grad_atom = atom_cot.astype(jnp.float32) + picked[:, atom_width:]

time: 172 us -> 155 us (0.901)
  blocking collectives: 50.2 us -> 0 us
  Pallas kernels: 0 us -> 50 us
  starting transfers between devices: 26.7 us -> 16.2 us
  waiting for transfers between devices: 33.2 us -> 29.9 us
  other arithmetic: 10 us -> 7 us
    all_to_all x4 -> x0, blocking collectives: 50.2 us -> none  [exchange_blocks(): return lax.all_to_all(blocks, axis, split_axis=0, concat_axis=0, tiled=True)]
    pallas_call x0 -> x2, Pallas kernels: none -> 50 us  [the longest x1 26.2 us: pool_call(): pl.pallas_call(functools.partial(pool_kernel, rows, cols), out_shape=(jax...]
    all_to_all x4 -> x2, starting transfers between devices: 16.3 us -> 7.78 us  [exchange_blocks(): return lax.all_to_all(blocks, axis, split_axis=0, concat_axis=0, tiled=True)]
    all_to_all x1, waiting for transfers between devices: 14.3 us -> 10.5 us  [on_device(): lax.all_to_all(bias_local, 'col', split_axis=0, concat_axis=2, tiled=True)]
    reduce_sum x6 -> x0, other arithmetic: 3.02 us -> none  [the longest x1 1.25 us: on_device(): both_sums = jnp.sum(exchange(both, 'col').astype(jnp.float32), axis=0)]
    dynamic_slice x0 -> x4, local copies, waits for them, and re-layouts: none -> 2.12 us  [mine(): lax.dynamic_slice_in_dim(rows, lax.axis_index('col') * share, share, axis=0)]
    unnamed x44 -> x35, local copies, waits for them, and re-layouts: 2.17 us -> 4.25 us
    dot_general x3 -> x2, matrix products: 4.05 us -> 2.05 us  [transposed_dot(): lax.dot_general(left, right, (((1,), (1,)), ((), ())), preferred_element_...]
  transfers between devices with their start and end apart: 6 -> 4, of which waited for: 5 -> 4; matrix products, arithmetic and copies ran while one was open for 20% -> 14% of each run, Pallas kernels for 0% -> 0%
where the time goes in v2:
time: 155 us; the launch traced here: 154 us
  Pallas kernels  50 us (32%)
  matrix products  30 us (19%)
  waiting for transfers between devices  29.9 us (19%)
  local copies, waits for them, and re-layouts  19.7 us (13%)
  starting transfers between devices  16.2 us (10%)
  other arithmetic  7 us (5%)
    pallas_call x1, Pallas kernels, pool_call(): pl.pallas_call(functools.partial(pool_kernel, rows, cols), out_shape=(jax...  26.2 us
    pallas_call x1, Pallas kernels, tail_call(): pl.pallas_call(functools.partial(tail_kernel, rows, cols), out_shape=(jax...  23.8 us
    all_to_all x1, waiting for transfers between devices, on_device(): lax.all_to_all(grad_logits, 'col', split_axis=2, concat_axis=0, tiled=True)  12.7 us
    all_to_all x1, waiting for transfers between devices, on_device(): lax.all_to_all(bias_local, 'col', split_axis=0, concat_axis=2, tiled=True)  10.5 us
    all_to_all x2, starting transfers between devices, exchange_blocks(): return lax.all_to_all(blocks, axis, split_axis=0, concat_axis=0, tiled=True)  7.78 us
    all_to_all x2, waiting for transfers between devices, exchange_blocks(): return lax.all_to_all(blocks, axis, split_axis=0, concat_axis=0, tiled=True)  6.64 us
    dot_general x1, matrix products, on_device(): jnp.einsum('ijc,ch->hij', pair, w_bias, preferred_element_type=jnp.float32)  5.66 us
    dot_general x1, matrix products, on_device(): jnp.einsum('ijc,hij->hc', pair, bias_back, preferred_element_type=jnp.flo...  5.2 us
  transfers between devices with their start and end apart: 4, of which 4 were waited for; matrix products, arithmetic and copies ran while one was open for 14% of the time, Pallas kernels for 0%

profile of v2, /device:TPU:0, one launch (start us, length us, event | category | flops | bytes accessed | tf_op | source)
XLA Modules:
  0.0 153.7 jit_solution(6955711858802705519)
XLA Ops:
  0.7 0.8 fusion.32
  1.5 2.3 %convolution_convert_fusion.1 = bf16[1024,384]{1,0:T(8,128)(2,1)} fusion(s32[256]{0:T(256)S(1)} %fusion.32, bf16[256,128]{1,0:T(8,128)(2,1)} %param.12, bf16[256,128]{1,0:T(8,128)(2,1)} %param.10, bf16[384]{0:T(512)(128)(2,1)S(1)} %pad.9.clone), kind=kOutput, calls=%fused_computation.7 | convolution fusion | flops 202571776 | bytes 919296 | tf_op jit(solution)/shard_map/dot_general | solution.py:295
  3.8 26.2 %shard_map.121 = (bf16[8,32,384]{2,1,0:T(8,128)(2,1)}, f32[32,128]{1,0:T(8,128)}) custom-call(bf16[8,128,384]{2,1,0:T(8,128)(2,1)} %bitcast.88), custom_call_target="tpu_custom_call" | custom-call | tf_op jit(solution)/shard_map/pallas_call | solution.py:132
  30.0 1.2 fusion.36
  31.6 0.3 fusion.12
  32.0 0.8 broadcast_in_dim.5
  32.7 4.3 %all-to-all-start = ((bf16[4,2,256,96]{2,3,1,0:T(8,128)(2,1)}), bf16[4,2,256,96]{2,3,1,0:T(8,128)(2,1)S(1)}, u32[]{:S(2)}, u32[]{:S(2)}) async-start(bf16[4,2,256,96]{2,3,1,0:T(8,128)(2,1)} %broadcast_in_dim.5), calls=%async_computation | async-start | bytes 786432 | tf_op jit(solution)/shard_map/all_to_all | solution.py:38
  37.1 0.6 slice.44
  37.7 5.7 %convolution_convert_fusion = bf16[16,256,128]{2,0,1:T(8,128)(2,1)S(1)} fusion(bf16[256,128,128]{2,1,0:T(8,128)(2,1)} %param.14, bf16[128,16]{0,1:T(8,128)(2,1)S(1)} %copy-done.16), kind=kOutput, calls=%fused_computation.6 | convolution fusion | flops 134742016 | bytes 9441280 | tf_op jit(solution)/shard_map/ijc,ch->hij/dot_general | solution.py:314
  43.4 1.3 copy.23
  44.6 4.4 %all-to-all-done = bf16[4,2,256,96]{2,3,1,0:T(8,128)(2,1)S(1)} async-done(((bf16[4,2,256,96]{2,3,1,0:T(8,128)(2,1)}), bf16[4,2,256,96]{2,3,1,0:T(8,128)(2,1)S(1)}, u32[]{:S(2)}, u32[]{:S(2)}) %all-to-all-start) | async-done | bytes 393248 | tf_op jit(solution)/shard_map/all_to_all | solution.py:38
  49.0 0.8 copy-done.4
  49.8 3.6 %all-to-all-start.1 = ((bf16[16,256,128]{2,1,0:T(8,128)(2,1)}), bf16[16,256,128]{2,1,0:T(8,128)(2,1)S(1)}, u32[]{:S(2)}, u32[]{:S(2)}) async-start(bf16[16,256,128]{2,1,0:T(8,128)(2,1)} %copy.23), calls=%async_computation.1 | async-start | bytes 2097152 | tf_op jit(solution)/shard_map/all_to_all | solution.py:317
  53.4 0.7 copy.30.inverse_ref
  54.1 1.2 fusion.27
  55.3 0.7 constant_dynamic-slice_fusion
  56.0 0.9 convolution_convert_fusion.6
  57.1 0.8 reshape_squeeze.9
  58.2 10.5 %all-to-all-done.1 = bf16[16,256,128]{2,1,0:T(8,128)(2,1)S(1)} async-done(((bf16[16,256,128]{2,1,0:T(8,128)(2,1)}), bf16[16,256,128]{2,1,0:T(8,128)(2,1)S(1)}, u32[]{:S(2)}, u32[]{:S(2)}) %all-to-all-start.1) | async-done | bytes 1048608 | tf_op jit(solution)/shard_map/all_to_all | solution.py:317
  68.7 1.0 copy-done.3
  69.7 1.8 %copy.32 = f32[8,2,256,128]{3,0,2,1:T(8,128)S(1)} copy(bf16[8,2,256,128]{3,2,1,0:T(8,128)(2,1)} %bitcast.84) | data formatting | bytes 3145728 | tf_op jit(solution)/shard_map/convert_element_type | solution.py:320
  71.5 1.5 reshape.76
  73.0 2.1 %multiply_add_fusion = f32[2,256,1024]{2,1,0:T(8,128)S(1)} fusion(f32[2,256,1024]{2,1,0:T(8,128)} %reshape.76, bf16[256,2,48]{0,2,1:T(8,128)(2,1)} %bitcast.89, bf16[1024,2,48]{0,2,1:T(8,128)(2,1)S(1)} %reshape_squeeze.11), kind=kOutput, calls=%fused_computation.5 | convolution fusion | flops 51380224 | bytes 4440064 | tf_op jit(solution)/shard_map/ihd,jhd->hij/dot_general | solution.py:318
  75.1 1.9 %fusion.37 = (f32[2,256]{1,0:T(2,128)S(1)}, f32[2,256,1024]{2,1,0:T(8,128)}) fusion(f32[2,256,1024]{2,1,0:T(8,128)S(1)} %multiply_add_fusion), kind=kOutput, calls=%fused_computation.81 | output fusion | flops 1049599 | bytes 4196352 | tf_op jit(solution)/shard_map/sub | solution.py:321
  77.1 2.6 %fusion.3 = bf16[1024,2,48]{0,2,1:T(8,128)(2,1)} fusion(bf16[256,2,48]{0,2,1:T(8,128)(2,1)} %bitcast.95, f32[2,256]{1,0:T(2,128)S(1)} %get-tuple-element.17, f32[2,256,1024]{2,1,0:T(8,128)S(1)} %multiply_add_fusion), kind=kOutput, calls=%fused_computation.15 | convolution fusion | flops 52004352 | bytes 2344960 | tf_op jit(solution)/shard_map/hij,ihd->jhd/dot_general | solution.py:351
  79.6 1.1 stack.15
  80.7 2.4 %multiply_reduce_fusion = (f32[2,256]{1,0:T(2,128)S(1)}, f32[2,256,1024]{2,1,0:T(8,128)S(1)}) fusion(f32[2,256,1024]{2,1,0:T(8,128)} %get-tuple-element.18, f32[2,256]{1,0:T(2,128)S(1)} %get-tuple-element.17, bf16[256,2,48]{0,2,1:T(8,128)(2,1)} %bitcast.96, bf16[1024,2,48]{0,2,1:T(8,128)(2,1)} %reshape_squeeze.9), kind=kOutput, calls=%fused_computation.3 | convolution fusion | flops 51904000 | bytes 4444160 | tf_op jit(solution)/shard_map/ihd,jhd->hij/dot_general | solution.py:335
  83.2 0.4 multiply_convert_fusion
  83.5 0.4 copy-done.11
  84.5 0.8 maximum_bitcast_fusion
  85.2 3.5 %all-to-all-start.2 = ((bf16[4,2,256,96]{2,3,1,0:T(8,128)(2,1)}), bf16[4,2,256,96]{2,3,1,0:T(8,128)(2,1)S(1)}, u32[]{:S(2)}, u32[]{:S(2)}) async-start(bf16[4,2,256,96]{2,3,1,0:T(8,128)(2,1)} %maximum_bitcast_fusion), calls=%async_computation.2 | async-start | bytes 786432 | tf_op jit(solution)/shard_map/all_to_all | solution.py:38
  88.7 0.7 constant_dynamic-slice_fusion.2.single_ref
  89.4 2.0 %copy.28 = bf16[2,256,1024]{1,0,2:T(2,128)(2,1)} copy(bf16[2,256,1024]{2,1,0:T(8,128)(2,1)S(1)} %multiply_convert_fusion) | data formatting | bytes 2097152 | tf_op jit(solution)/shard_map/convert_element_type | solution.py:339
  91.4 3.4 %fusion.5 = bf16[256,2,48]{0,2,1:T(8,128)(2,1)S(1)} fusion(bf16[1024,2,48]{0,2,1:T(8,128)(2,1)S(1)} %copy-done.13, f32[2,256]{1,0:T(2,128)S(1)} %get-tuple-element.17, f32[2,256,1024]{2,1,0:T(8,128)} %copy-done.1), kind=kOutput, calls=%fused_computation.20 | convolution fusion | flops 51930624 | bytes 2344960 | tf_op jit(solution)/shard_map/hij,jhd->ihd/dot_general | solution.py:325
  95.1 0.4 fusion.4
  95.5 2.2 %all-to-all-done.2 = bf16[4,2,256,96]{2,3,1,0:T(8,128)(2,1)S(1)} async-done(((bf16[4,2,256,96]{2,3,1,0:T(8,128)(2,1)}), bf16[4,2,256,96]{2,3,1,0:T(8,128)(2,1)S(1)}, u32[]{:S(2)}, u32[]{:S(2)}) %all-to-all-start.2) | async-done | bytes 393248 | tf_op jit(solution)/shard_map/all_to_all | solution.py:38
  97.8 0.7 copy-done.6
  98.5 4.9 %all-to-all-start.3 = ((bf16[2,256,1024]{1,0,2:T(2,128)(2,1)}), bf16[2,256,1024]{1,0,2:T(2,128)(2,1)S(1)}, u32[]{:S(2)}, u32[]{:S(2)}) async-start(bf16[2,256,1024]{1,0,2:T(2,128)(2,1)} %copy.28), calls=%async_computation.3 | async-start | bytes 2097152 | tf_op jit(solution)/shard_map/all_to_all | solution.py:365
  103.6 1.1 convert_reduce_fusion
  104.7 0.4 fusion.1
  105.1 0.9 pad_maximum_fusion.both_ref
  106.1 12.7 %all-to-all-done.3 = bf16[2,256,1024]{1,0,2:T(2,128)(2,1)S(1)} async-done(((bf16[2,256,1024]{1,0,2:T(2,128)(2,1)}), bf16[2,256,1024]{1,0,2:T(2,128)(2,1)S(1)}, u32[]{:S(2)}, u32[]{:S(2)}) %all-to-all-start.3) | async-done | bytes 1048608 | tf_op jit(solution)/shard_map/all_to_all | solution.py:365
  118.8 2.5 %copy.29 = bf16[2,256,8,128]{3,0,2,1:T(2,128)(2,1)S(1)} copy(bf16[2,256,8,128]{1,0,3,2:T(2,128)(2,1)S(1)} %bitcast.85) | data formatting | bytes 2097152 | tf_op jit(solution)/shard_map/all_to_all | solution.py:365
  121.3 5.2 %convolution_bitcast_fusion.1.weight_ref = f32[16,128]{1,0:T(8,128)} fusion(bf16[16,256,128]{2,0,1:T(8,128)(2,1)S(1)} %bitcast.82, bf16[256,128,128]{2,1,0:T(8,128)(2,1)} %param.14), kind=kOutput, calls=%fused_computation.21 | convolution fusion | flops 134217728 | bytes 9445376 | tf_op jit(solution)/shard_map/ijc,hij->hc/dot_general | solution.py:366
  126.5 23.8 %shard_map.122 = (bf16[8,4,32,256]{3,2,1,0:T(8,128)(2,1)}, f32[16,128]{1,0:T(8,128)}) custom-call(bf16[8,32,1536]{2,1,0:T(8,128)(2,1)} %pad_maximum_fusion.both_ref, f32[32,768]{1,0:T(8,128)} %constant_dynamic-slice_fusion.2.single_ref, f32[32,768]{1,0:T(8,128)} %get-tuple-element.22.grad_out_ref, f32[32,768]{1,0:T(8,128)} %get-tuple-element.21.normal_ref, ...), custom_call_target="tpu_custom_call" | custom-call | tf_op jit(solution)/shard_map/pallas_call | solution.py:250
  150.3 1.4 fusion.6
  151.7 0.7 slice_add_fusion
  152.4 1.3 copy.34
  (52 shorter events, 2.0 us)
Async XLA Ops:
  0.6 30.9 %copy-start = (bf16[3,768,96]{1,2,0:T(8,128)(2,1)S(1)}, bf16[3,768,96]{1,2,0:T(8,128)(2,1)}, u32[]{:S(2)}) copy-start(bf16[3,768,96]{1,2,0:T(8,128)(2,1)} %param.16) | copy-start | bytes 1327108
  0.6 29.3 %copy-start.8 = (bf16[128,768]{1,0:T(8,128)(2,1)S(1)}, bf16[128,768]{1,0:T(8,128)(2,1)}, u32[]{:S(2)}) copy-start(bf16[128,768]{1,0:T(8,128)(2,1)} %pool_ref.1) | copy-start | bytes 589828
  0.7 29.3 %copy-start.12 = (bf16[256,768]{1,0:T(8,128)(2,1)S(1)}, bf16[256,768]{1,0:T(8,128)(2,1)}, u32[]{:S(2)}) copy-start(bf16[256,768]{1,0:T(8,128)(2,1)} %param.13) | copy-start | bytes 1179652
  31.6 6.1 %copy-start.16 = (bf16[128,16]{0,1:T(8,128)(2,1)S(1)}, bf16[128,16]{0,1:T(8,128)(2,1)}, u32[]{:S(2)}) copy-start(bf16[128,16]{0,1:T(8,128)(2,1)} %param.17) | copy-start | bytes 12292
  32.7 16.3 %all-to-all-start = ((bf16[4,2,256,96]{2,3,1,0:T(8,128)(2,1)}), bf16[4,2,256,96]{2,3,1,0:T(8,128)(2,1)S(1)}, u32[]{:S(2)}, u32[]{:S(2)}) async-start(bf16[4,2,256,96]{2,3,1,0:T(8,128)(2,1)} %broadcast_in_dim.5), calls=%async_computation | async-start | bytes 786432 | tf_op jit(solution)/shard_map/all_to_all | solution.py:38
  43.4 10.8 %copy-start.7 = (bf16[768,128]{1,0:T(8,128)(2,1)S(1)}, bf16[768,128]{1,0:T(8,128)(2,1)}, u32[]{:S(2)}) copy-start(bf16[768,128]{1,0:T(8,128)(2,1)} %dec_ref.1) | copy-start | bytes 589828
  44.6 11.4 %copy-start.9 = (bf16[96,768]{1,0:T(8,128)(2,1)S(1)}, bf16[96,768]{1,0:T(8,128)(2,1)}, u32[]{:S(2)}) copy-start(bf16[96,768]{1,0:T(8,128)(2,1)} %param.18) | copy-start | bytes 442372
  49.0 0.8 copy-start.4
  49.8 18.9 %all-to-all-start.1 = ((bf16[16,256,128]{2,1,0:T(8,128)(2,1)}), bf16[16,256,128]{2,1,0:T(8,128)(2,1)S(1)}, u32[]{:S(2)}, u32[]{:S(2)}) async-start(bf16[16,256,128]{2,1,0:T(8,128)(2,1)} %copy.23), calls=%async_computation.1 | async-start | bytes 2097152 | tf_op jit(solution)/shard_map/all_to_all | solution.py:317
  54.1 2.8 %copy-start.5 = (bf16[4,2,256,96]{2,3,1,0:T(8,128)(2,1)S(1)}, bf16[4,2,256,96]{2,3,1,0:T(8,128)(2,1)}, u32[]{:S(2)}) copy-start(bf16[4,2,256,96]{2,3,1,0:T(8,128)(2,1)} %copy-done.4) | copy-start | bytes 1179652
  68.7 1.0 copy-start.3
  75.1 2.0 %copy-start.1 = (f32[2,256,1024]{2,1,0:T(8,128)}, f32[2,256,1024]{2,1,0:T(8,128)S(1)}, u32[]{:S(2)}) copy-start(f32[2,256,1024]{2,1,0:T(8,128)S(1)} %multiply_add_fusion) | copy-start | bytes 6291460
  80.7 2.4 %copy-start.2 = (f32[2,256,1024]{2,1,0:T(8,128)S(1)}, f32[2,256,1024]{2,1,0:T(8,128)}, u32[]{:S(2)}) copy-start(f32[2,256,1024]{2,1,0:T(8,128)} %get-tuple-element.18) | copy-start | bytes 6291460
  83.2 0.8 copy-start.11
  84.4 7.0 %copy-start.13 = (bf16[1024,2,48]{0,2,1:T(8,128)(2,1)S(1)}, bf16[1024,2,48]{0,2,1:T(8,128)(2,1)}, u32[]{:S(2)}) copy-start(bf16[1024,2,48]{0,2,1:T(8,128)(2,1)} %reshape_squeeze.9) | copy-start | bytes 589828
  85.2 12.5 %all-to-all-start.2 = ((bf16[4,2,256,96]{2,3,1,0:T(8,128)(2,1)}), bf16[4,2,256,96]{2,3,1,0:T(8,128)(2,1)S(1)}, u32[]{:S(2)}, u32[]{:S(2)}) async-start(bf16[4,2,256,96]{2,3,1,0:T(8,128)(2,1)} %maximum_bitcast_fusion), calls=%async_computation.2 | async-start | bytes 786432 | tf_op jit(solution)/shard_map/all_to_all | solution.py:38
  94.9 8.5 %copy-start.10 = (bf16[96,768]{1,0:T(8,128)(2,1)S(1)}, bf16[96,768]{1,0:T(8,128)(2,1)}, u32[]{:S(2)}) copy-start(bf16[96,768]{1,0:T(8,128)(2,1)} %param.18) | copy-start | bytes 442372
  97.8 0.7 copy-start.6
  98.5 20.3 %all-to-all-start.3 = ((bf16[2,256,1024]{1,0,2:T(2,128)(2,1)}), bf16[2,256,1024]{1,0,2:T(2,128)(2,1)S(1)}, u32[]{:S(2)}, u32[]{:S(2)}) async-start(bf16[2,256,1024]{1,0,2:T(2,128)(2,1)} %copy.28), calls=%async_computation.3 | async-start | bytes 2097152 | tf_op jit(solution)/shard_map/all_to_all | solution.py:365
  126.5 25.2 %copy-start.14 = (bf16[256,128]{1,0:T(8,128)(2,1)S(1)}, bf16[256,128]{1,0:T(8,128)(2,1)}, u32[]{:S(2)}) copy-start(bf16[256,128]{1,0:T(8,128)(2,1)} %param.12) | copy-start | bytes 196612
  126.5 25.2 %copy-start.15 = (bf16[256,128]{1,0:T(8,128)(2,1)S(1)}, bf16[256,128]{1,0:T(8,128)(2,1)}, u32[]{:S(2)}) copy-start(bf16[256,128]{1,0:T(8,128)(2,1)} %param.10) | copy-start | bytes 196612

commit v3 on v2

--- a/solution.py
+++ b/solution.py
@@ -78,7 +78,18 @@
 
 
 def pool_kernel(
-    rows, cols, sums_ref, out_ref, counts_ref, got_col, col_sum, got_row, send_sems, recv_sems
+    rows,
+    cols,
+    sums_ref,
+    bias_ref,
+    out_ref,
+    counts_ref,
+    bias_out_ref,
+    got_col,
+    col_sum,
+    got_row,
+    send_sems,
+    recv_sems,
 ):
     row, col = lax.axis_index("row"), lax.axis_index("col")
     greet((("row", rows), ("col", cols)))
@@ -87,6 +98,20 @@
         push(sums_ref.at[peer], got_col.at[step - 1], send_sems, recv_sems, step - 1, "col", peer)
         for step, peer in peers_of("col", cols)
     ]
+    base = 2 * (cols - 1) + rows - 1
+    bias_copies = [
+        push(
+            bias_ref.at[peer],
+            bias_out_ref.at[col],
+            send_sems,
+            recv_sems,
+            base + step - 1,
+            "col",
+            peer,
+        )
+        for step, peer in peers_of("col", cols)
+    ]
+    bias_out_ref[col] = bias_ref[col]
     total = sums_ref[col].astype(jnp.float32)
     for at, copy in enumerate(copies):
         copy.wait()
@@ -121,22 +146,24 @@
         )
         for step, peer in peers_of("col", cols)
     ]
-    for copy in copies:
-        copy.wait()
-
-
-def pool_call(partial_sums, share):
+    for copy in copies + bias_copies:
+        copy.wait()
+
+
+def pool_call(partial_sums, bias, share):
     rows, cols = lax.axis_size("row"), lax.axis_size("col")
     width = partial_sums.shape[-1]
-    copies = 2 * (cols - 1) + rows - 1
+    copies = 3 * (cols - 1) + rows - 1
+    bias = bias.reshape((cols, -1) + bias.shape[1:])
     return pl.pallas_call(
         functools.partial(pool_kernel, rows, cols),
         out_shape=(
             jax.ShapeDtypeStruct((cols, share, width), jnp.bfloat16),
             jax.ShapeDtypeStruct((share, width // 3), jnp.float32),
+            jax.ShapeDtypeStruct(bias.shape, bias.dtype),
         ),
-        in_specs=[pl.BlockSpec(memory_space=pltpu.VMEM)],
-        out_specs=(pl.BlockSpec(memory_space=pltpu.VMEM),) * 2,
+        in_specs=[pl.BlockSpec(memory_space=pltpu.VMEM)] * 2,
+        out_specs=(pl.BlockSpec(memory_space=pltpu.VMEM),) * 3,
         scratch_shapes=[
             pltpu.VMEM((cols - 1, rows * share, width), jnp.bfloat16),
             pltpu.VMEM((rows, share, width), jnp.float32),
@@ -145,7 +172,7 @@
             pltpu.SemaphoreType.DMA((copies,)),
         ],
         compiler_params=pltpu.CompilerParams(collective_id=0, has_side_effects=True),
-    )(partial_sums.reshape(cols, rows * share, width))
+    )(partial_sums.reshape(cols, rows * share, width), bias)
 
 
 def tail_kernel(
@@ -295,7 +322,10 @@
     partial_sums = lax.dot_general(
         onehot, stacked, (((0,), (0,)), ((), ())), preferred_element_type=jnp.float32
     ).astype(jnp.bfloat16)
-    row_pooled, share_counts = pool_call(partial_sums, share)
+    bias_local = jnp.einsum("ijc,ch->hij", pair, w_bias, preferred_element_type=jnp.float32).astype(
+        jnp.bfloat16
+    )
+    row_pooled, share_counts, bias_blocks = pool_call(partial_sums, bias_local, share)
     row_pooled = row_pooled.reshape(tok_rows, 3 * atom_width)
     pooled = row_pooled[:, :atom_width]
     cot_pooled = row_pooled[:, atom_width : 2 * atom_width]
@@ -311,10 +341,9 @@
     queries = projected[0].reshape(tok_rows, local_heads, HD)
     keys_all = gathered[0].reshape(total_tokens, local_heads, HD)
     values_all = gathered[1].reshape(total_tokens, local_heads, HD)
-    bias_local = jnp.einsum("ijc,ch->hij", pair, w_bias, preferred_element_type=jnp.float32).astype(
-        jnp.bfloat16
-    )
-    bias_rows = lax.all_to_all(bias_local, "col", split_axis=0, concat_axis=2, tiled=True)
+    bias_rows = jnp.transpose(bias_blocks, (1, 2, 0, 3)).reshape(
+        local_heads, tok_rows, total_tokens
+    )
     logits = jnp.einsum(
         "ihd,jhd->hij", queries, keys_all, preferred_element_type=jnp.float32
     ) * scale + bias_rows.astype(jnp.float32)

time: 155 us -> 148 us (0.955)
  waiting for transfers between devices: 29.9 us -> 18.3 us
  Pallas kernels: 50 us -> 55.7 us
  starting transfers between devices: 16.2 us -> 11.9 us
  local copies, waits for them, and re-layouts: 19.7 us -> 22.3 us
    all_to_all x1 -> x0, waiting for transfers between devices: 10.5 us -> none  [on_device(): lax.all_to_all(bias_local, 'col', split_axis=0, concat_axis=2, tiled=True)]
    pallas_call x1, Pallas kernels: 26.2 us -> 32 us  [pool_call(): pl.pallas_call(functools.partial(pool_kernel, rows, cols), out_shape=(jax...]
    all_to_all x1 -> x0, starting transfers between devices: 3.56 us -> none  [on_device(): lax.all_to_all(bias_local, 'col', split_axis=0, concat_axis=2, tiled=True)]
    unnamed x35 -> x33, local copies, waits for them, and re-layouts: 4.25 us -> 3.43 us
  transfers between devices with their start and end apart: 4 -> 3, of which waited for: 4 -> 3; matrix products, arithmetic and copies ran while one was open for 14% -> 14% of each run, Pallas kernels for 0% -> 0%
where the time goes in v3:
time: 148 us; the launch traced here: 147 us
  Pallas kernels  55.7 us (38%)
  matrix products  29.1 us (20%)
  local copies, waits for them, and re-layouts  22.3 us (15%)
  waiting for transfers between devices  18.3 us (12%)
  starting transfers between devices  11.9 us (8%)
  other arithmetic  8.4 us (6%)
    pallas_call x1, Pallas kernels, pool_call(): pl.pallas_call(functools.partial(pool_kernel, rows, cols), out_shape=(jax...  32 us
    pallas_call x1, Pallas kernels, tail_call(): pl.pallas_call(functools.partial(tail_kernel, rows, cols), out_shape=(jax...  23.8 us
    all_to_all x1, waiting for transfers between devices, on_device(): lax.all_to_all(grad_logits, 'col', split_axis=2, concat_axis=0, tiled=True)  12.4 us
    all_to_all x2, starting transfers between devices, exchange_blocks(): return lax.all_to_all(blocks, axis, split_axis=0, concat_axis=0, tiled=True)  8.13 us
    all_to_all x2, waiting for transfers between devices, exchange_blocks(): return lax.all_to_all(blocks, axis, split_axis=0, concat_axis=0, tiled=True)  5.88 us
    dot_general x1, matrix products, on_device(): jnp.einsum('ijc,ch->hij', pair, w_bias, preferred_element_type=jnp.float32)  5.68 us
    dot_general x1, matrix products, on_device(): jnp.einsum('ijc,hij->hc', pair, bias_back, preferred_element_type=jnp.flo...  5.2 us
    convert_element_type x2, local copies, waits for them, and re-layouts, on_device(): bias_rows.astype(jnp.float32)  4.83 us
  transfers between devices with their start and end apart: 3, of which 3 were waited for; matrix products, arithmetic and copies ran while one was open for 14% of the time, Pallas kernels for 0%

profile of v3, /device:TPU:0, one launch (start us, length us, event | category | flops | bytes accessed | tf_op | source)
XLA Modules:
  0.0 146.7 jit_solution(888792576112389026)
XLA Ops:
  0.6 0.8 fusion.32
  1.4 5.7 %convolution_convert_fusion = bf16[16,256,128]{2,0,1:T(8,128)(2,1)S(1)} fusion(bf16[256,128,128]{2,1,0:T(8,128)(2,1)} %param.14, bf16[128,16]{0,1:T(8,128)(2,1)} %param.17), kind=kOutput, calls=%fused_computation.6 | convolution fusion | flops 134742016 | bytes 9441280 | tf_op jit(solution)/shard_map/ijc,ch->hij/dot_general | solution.py:325
  7.1 1.3 copy.23
  8.5 1.4 convolution_convert_fusion.1
  9.9 32.0 %shard_map.121 = (bf16[8,32,384]{2,1,0:T(8,128)(2,1)}, f32[32,128]{1,0:T(8,128)}, bf16[8,2,256,128]{3,2,1,0:T(8,128)(2,1)}) custom-call(bf16[8,128,384]{2,1,0:T(8,128)(2,1)} %bitcast.84, bf16[8,2,256,128]{3,2,1,0:T(8,128)(2,1)} %bitcast.81), custom_call_target="tpu_custom_call" | custom-call | tf_op jit(solution)/shard_map/pallas_call | solution.py:158
  41.9 1.2 fusion.36
  43.5 0.9 copy-done.3
  44.4 0.3 fusion.12
  44.7 0.8 broadcast_in_dim.5
  45.5 4.1 %all-to-all-start = ((bf16[4,2,256,96]{2,3,1,0:T(8,128)(2,1)}), bf16[4,2,256,96]{2,3,1,0:T(8,128)(2,1)}, u32[]{:S(2)}, u32[]{:S(2)}) async-start(bf16[4,2,256,96]{2,3,1,0:T(8,128)(2,1)} %broadcast_in_dim.5), calls=%async_computation | async-start | bytes 786432 | tf_op jit(solution)/shard_map/all_to_all | solution.py:38
  49.6 0.6 slice.44
  50.3 0.7 copy.33.inverse_ref
  51.0 1.4 convert_bitcast_fusion
  52.5 1.8 %copy.26 = f32[2,256,8,128]{1,3,2,0:T(8,128)} copy(f32[2,256,8,128]{3,1,0,2:T(8,128)S(1)} %convert_bitcast_fusion) | data formatting | bytes 4194304 | tf_op jit(solution)/shard_map/convert_element_type | solution.py:349
  54.3 3.0 %copy.27 = f32[2,256,1024]{2,1,0:T(8,128)} copy(f32[2,256,1024]{1,2,0:T(8,128)} %bitcast.80) | data formatting | bytes 4194304 | tf_op jit(solution)/shard_map/convert_element_type | solution.py:349
  57.3 1.1 fusion.27
  58.4 1.6 %constant_dynamic-slice_fusion = (f32[32,768]{1,0:T(8,128)}, f32[32,768]{1,0:T(8,128)}) fusion(f32[256,768]{1,0:T(8,128)} %copy-done.3, s32[]{:T(128)S(6)} %select_n.29, f32[256,768]{1,0:T(8,128)S(1)} %fusion.27), kind=kLoop, calls=%fused_computation.72 | loop fusion | bytes 393220 | tf_op jit(solution)/shard_map/dynamic_slice | solution.py:398
  60.0 0.9 convolution_convert_fusion.6
  60.9 1.0 all-to-all-done
  61.9 1.0 fusion.35
  63.2 0.8 reshape_squeeze.9
  64.2 2.1 %multiply_add_fusion = f32[2,256,1024]{2,1,0:T(8,128)S(1)} fusion(f32[2,256,1024]{2,1,0:T(8,128)} %copy.27, bf16[256,2,48]{0,2,1:T(8,128)(2,1)} %bitcast.85, bf16[1024,2,48]{0,2,1:T(8,128)(2,1)S(1)} %reshape_squeeze.11), kind=kOutput, calls=%fused_computation.5 | convolution fusion | flops 51380224 | bytes 4440064 | tf_op jit(solution)/shard_map/ihd,jhd->hij/dot_general | solution.py:347
  66.3 1.9 %fusion.37 = (f32[2,256]{1,0:T(2,128)S(1)}, f32[2,256,1024]{2,1,0:T(8,128)}) fusion(f32[2,256,1024]{2,1,0:T(8,128)S(1)} %multiply_add_fusion), kind=kOutput, calls=%fused_computation.81 | output fusion | flops 1049599 | bytes 4196352 | tf_op jit(solution)/shard_map/sub | solution.py:350
  68.3 2.6 %fusion.3 = bf16[1024,2,48]{0,2,1:T(8,128)(2,1)} fusion(bf16[256,2,48]{0,2,1:T(8,128)(2,1)} %bitcast.91, f32[2,256]{1,0:T(2,128)S(1)} %get-tuple-element.19, f32[2,256,1024]{2,1,0:T(8,128)S(1)} %multiply_add_fusion), kind=kOutput, calls=%fused_computation.15 | convolution fusion | flops 52004352 | bytes 2344960 | tf_op jit(solution)/shard_map/hij,ihd->jhd/dot_general | solution.py:380
  70.8 1.1 stack.15
  71.9 2.4 %multiply_reduce_fusion = (f32[2,256]{1,0:T(2,128)S(1)}, f32[2,256,1024]{2,1,0:T(8,128)S(1)}) fusion(f32[2,256,1024]{2,1,0:T(8,128)} %get-tuple-element.20, f32[2,256]{1,0:T(2,128)S(1)} %get-tuple-element.19, bf16[256,2,48]{0,2,1:T(8,128)(2,1)} %bitcast.92, bf16[1024,2,48]{0,2,1:T(8,128)(2,1)} %reshape_squeeze.9), kind=kOutput, calls=%fused_computation.3 | convolution fusion | flops 51904000 | bytes 4444160 | tf_op jit(solution)/shard_map/ihd,jhd->hij/dot_general | solution.py:364
  74.4 0.4 multiply_convert_fusion
  74.7 0.4 copy-done.9
  75.2 0.3 fusion.2
  75.7 0.8 maximum_bitcast_fusion
  76.4 4.0 %all-to-all-start.1 = ((bf16[4,2,256,96]{2,3,1,0:T(8,128)(2,1)}), bf16[4,2,256,96]{2,3,1,0:T(8,128)(2,1)S(1)}, u32[]{:S(2)}, u32[]{:S(2)}) async-start(bf16[4,2,256,96]{2,3,1,0:T(8,128)(2,1)} %maximum_bitcast_fusion), calls=%async_computation.1 | async-start | bytes 786432 | tf_op jit(solution)/shard_map/all_to_all | solution.py:38
  80.4 0.6 constant_dynamic-slice_fusion.2.single_ref
  81.1 2.1 %copy.31 = bf16[2,256,1024]{1,0,2:T(2,128)(2,1)} copy(bf16[2,256,1024]{2,1,0:T(8,128)(2,1)S(1)} %multiply_convert_fusion) | data formatting | bytes 2097152 | tf_op jit(solution)/shard_map/convert_element_type | solution.py:368
  83.1 3.4 %fusion.5 = bf16[256,2,48]{0,2,1:T(8,128)(2,1)S(1)} fusion(bf16[1024,2,48]{0,2,1:T(8,128)(2,1)S(1)} %copy-done.11, f32[2,256]{1,0:T(2,128)S(1)} %get-tuple-element.19, f32[2,256,1024]{2,1,0:T(8,128)} %copy-done.1), kind=kOutput, calls=%fused_computation.20 | convolution fusion | flops 51930624 | bytes 2344960 | tf_op jit(solution)/shard_map/hij,jhd->ihd/dot_general | solution.py:354
  86.9 0.4 fusion.4
  87.3 4.8 %all-to-all-done.1 = bf16[4,2,256,96]{2,3,1,0:T(8,128)(2,1)S(1)} async-done(((bf16[4,2,256,96]{2,3,1,0:T(8,128)(2,1)}), bf16[4,2,256,96]{2,3,1,0:T(8,128)(2,1)S(1)}, u32[]{:S(2)}, u32[]{:S(2)}) %all-to-all-start.1) | async-done | bytes 393248 | tf_op jit(solution)/shard_map/all_to_all | solution.py:38
  92.1 0.8 copy-done.4
  92.9 3.7 %all-to-all-start.2 = ((bf16[2,256,1024]{1,0,2:T(2,128)(2,1)}), bf16[2,256,1024]{1,0,2:T(2,128)(2,1)S(1)}, u32[]{:S(2)}, u32[]{:S(2)}) async-start(bf16[2,256,1024]{1,0,2:T(2,128)(2,1)} %copy.31), calls=%async_computation.2 | async-start | bytes 2097152 | tf_op jit(solution)/shard_map/all_to_all | solution.py:394
  96.9 1.1 convert_reduce_fusion
  98.0 0.4 fusion.1
  98.4 1.0 pad_maximum_fusion.both_ref
  99.4 12.4 %all-to-all-done.2 = bf16[2,256,1024]{1,0,2:T(2,128)(2,1)S(1)} async-done(((bf16[2,256,1024]{1,0,2:T(2,128)(2,1)}), bf16[2,256,1024]{1,0,2:T(2,128)(2,1)S(1)}, u32[]{:S(2)}, u32[]{:S(2)}) %all-to-all-start.2) | async-done | bytes 1048608 | tf_op jit(solution)/shard_map/all_to_all | solution.py:394
  111.8 2.5 %copy.32 = bf16[2,256,8,128]{3,0,2,1:T(2,128)(2,1)S(1)} copy(bf16[2,256,8,128]{1,0,3,2:T(2,128)(2,1)S(1)} %bitcast.82) | data formatting | bytes 2097152 | tf_op jit(solution)/shard_map/all_to_all | solution.py:394
  114.3 5.2 %convolution_bitcast_fusion.1.weight_ref = f32[16,128]{1,0:T(8,128)} fusion(bf16[16,256,128]{2,0,1:T(8,128)(2,1)S(1)} %bitcast.79, bf16[256,128,128]{2,1,0:T(8,128)(2,1)} %param.14), kind=kOutput, calls=%fused_computation.21 | convolution fusion | flops 134217728 | bytes 9445376 | tf_op jit(solution)/shard_map/ijc,hij->hc/dot_general | solution.py:395
  119.5 23.8 %shard_map.122 = (bf16[8,4,32,256]{3,2,1,0:T(8,128)(2,1)}, f32[16,128]{1,0:T(8,128)}) custom-call(bf16[8,32,1536]{2,1,0:T(8,128)(2,1)} %pad_maximum_fusion.both_ref, f32[32,768]{1,0:T(8,128)} %constant_dynamic-slice_fusion.2.single_ref, f32[32,768]{1,0:T(8,128)} %get-tuple-element.24.grad_out_ref, f32[32,768]{1,0:T(8,128)} %get-tuple-element.23.normal_ref, ...), custom_call_target="tpu_custom_call" | custom-call | tf_op jit(solution)/shard_map/pallas_call | solution.py:277
  143.3 1.4 fusion.6
  144.7 0.7 slice_add_fusion
  145.4 1.3 copy.35
  (49 shorter events, 1.7 us)
Async XLA Ops:
  0.6 42.8 %copy-start = (bf16[3,768,96]{1,2,0:T(8,128)(2,1)S(1)}, bf16[3,768,96]{1,2,0:T(8,128)(2,1)}, u32[]{:S(2)}) copy-start(bf16[3,768,96]{1,2,0:T(8,128)(2,1)} %param.16) | copy-start | bytes 1327108
  7.1 1.4 copy-start.12
  7.1 1.4 copy-start.14
  7.1 34.8 %copy-start.6 = (bf16[128,768]{1,0:T(8,128)(2,1)S(1)}, bf16[128,768]{1,0:T(8,128)(2,1)}, u32[]{:S(2)}) copy-start(bf16[128,768]{1,0:T(8,128)(2,1)} %pool_ref.1) | copy-start | bytes 589828
  7.1 34.8 %copy-start.10 = (bf16[256,768]{1,0:T(8,128)(2,1)S(1)}, bf16[256,768]{1,0:T(8,128)(2,1)}, u32[]{:S(2)}) copy-start(bf16[256,768]{1,0:T(8,128)(2,1)} %param.13) | copy-start | bytes 1179652
  43.5 0.9 copy-start.3
  45.5 16.4 %all-to-all-start = ((bf16[4,2,256,96]{2,3,1,0:T(8,128)(2,1)}), bf16[4,2,256,96]{2,3,1,0:T(8,128)(2,1)}, u32[]{:S(2)}, u32[]{:S(2)}) async-start(bf16[4,2,256,96]{2,3,1,0:T(8,128)(2,1)} %broadcast_in_dim.5), calls=%async_computation | async-start | bytes 786432 | tf_op jit(solution)/shard_map/all_to_all | solution.py:38
  54.3 3.0 %copy-start.5 = (bf16[768,128]{1,0:T(8,128)(2,1)S(1)}, bf16[768,128]{1,0:T(8,128)(2,1)}, u32[]{:S(2)}) copy-start(bf16[768,128]{1,0:T(8,128)(2,1)} %dec_ref.1) | copy-start | bytes 589828
  54.3 5.7 %copy-start.7 = (bf16[96,768]{1,0:T(8,128)(2,1)S(1)}, bf16[96,768]{1,0:T(8,128)(2,1)}, u32[]{:S(2)}) copy-start(bf16[96,768]{1,0:T(8,128)(2,1)} %param.18) | copy-start | bytes 442372
  66.3 1.9 %copy-start.1 = (f32[2,256,1024]{2,1,0:T(8,128)}, f32[2,256,1024]{2,1,0:T(8,128)S(1)}, u32[]{:S(2)}) copy-start(f32[2,256,1024]{2,1,0:T(8,128)S(1)} %multiply_add_fusion) | copy-start | bytes 6291460
  71.9 2.4 %copy-start.2 = (f32[2,256,1024]{2,1,0:T(8,128)S(1)}, f32[2,256,1024]{2,1,0:T(8,128)}, u32[]{:S(2)}) copy-start(f32[2,256,1024]{2,1,0:T(8,128)} %get-tuple-element.20) | copy-start | bytes 6291460
  74.4 0.8 copy-start.9
  75.6 7.5 %copy-start.11 = (bf16[1024,2,48]{0,2,1:T(8,128)(2,1)S(1)}, bf16[1024,2,48]{0,2,1:T(8,128)(2,1)}, u32[]{:S(2)}) copy-start(bf16[1024,2,48]{0,2,1:T(8,128)(2,1)} %reshape_squeeze.9) | copy-start | bytes 589828
  76.4 15.7 %all-to-all-start.1 = ((bf16[4,2,256,96]{2,3,1,0:T(8,128)(2,1)}), bf16[4,2,256,96]{2,3,1,0:T(8,128)(2,1)S(1)}, u32[]{:S(2)}, u32[]{:S(2)}) async-start(bf16[4,2,256,96]{2,3,1,0:T(8,128)(2,1)} %maximum_bitcast_fusion), calls=%async_computation.1 | async-start | bytes 786432 | tf_op jit(solution)/shard_map/all_to_all | solution.py:38
  86.6 10.0 %copy-start.8 = (bf16[96,768]{1,0:T(8,128)(2,1)S(1)}, bf16[96,768]{1,0:T(8,128)(2,1)}, u32[]{:S(2)}) copy-start(bf16[96,768]{1,0:T(8,128)(2,1)} %param.18) | copy-start | bytes 442372
  92.1 0.8 copy-start.4
  92.9 18.9 %all-to-all-start.2 = ((bf16[2,256,1024]{1,0,2:T(2,128)(2,1)}), bf16[2,256,1024]{1,0,2:T(2,128)(2,1)S(1)}, u32[]{:S(2)}, u32[]{:S(2)}) async-start(bf16[2,256,1024]{1,0,2:T(2,128)(2,1)} %copy.31), calls=%async_computation.2 | async-start | bytes 2097152 | tf_op jit(solution)/shard_map/all_to_all | solution.py:394
  119.5 25.2 %copy-start.13 = (bf16[256,128]{1,0:T(8,128)(2,1)S(1)}, bf16[256,128]{1,0:T(8,128)(2,1)}, u32[]{:S(2)}) copy-start(bf16[256,128]{1,0:T(8,128)(2,1)} %param.12) | copy-start | bytes 196612
  119.5 25.2 %copy-start.15 = (bf16[256,128]{1,0:T(8,128)(2,1)S(1)}, bf16[256,128]{1,0:T(8,128)(2,1)}, u32[]{:S(2)}) copy-start(bf16[256,128]{1,0:T(8,128)(2,1)} %param.10) | copy-start | bytes 196612

commit v4 on v3

--- a/solution.py
+++ b/solution.py
@@ -385,13 +385,14 @@
     key_blocks = jnp.swapaxes(
         key_terms.astype(jnp.bfloat16).reshape(2, -1, tok_rows, width), 0, 1
     )
+    bias_back = lax.all_to_all(grad_logits, "col", split_axis=2, concat_axis=0, tiled=True)
+    key_blocks, bias_back = lax.optimization_barrier((key_blocks, bias_back))
     key_sums = jnp.sum(exchange_blocks(key_blocks, "row").astype(jnp.float32), axis=0)
     grad_keys = (key_sums[0] * scale).astype(jnp.bfloat16)
     grad_values = key_sums[1].astype(jnp.bfloat16)
     grad_proj = jnp.stack([grad_queries, grad_keys, grad_values])
     normed_part = jnp.einsum("ktf,kdf->td", grad_proj, w_qkv, preferred_element_type=jnp.float32)
     both = jnp.concatenate([partial_update, normed_part], axis=1).astype(jnp.bfloat16)
-    bias_back = lax.all_to_all(grad_logits, "col", split_axis=2, concat_axis=0, tiled=True)
     weight_part = jnp.einsum("ijc,hij->hc", pair, bias_back, preferred_element_type=jnp.float32)
 
     def mine(rows):

time: 148 us -> 134 us (0.905)
  waiting for transfers between devices: 18.3 us -> 11.8 us
  local copies, waits for them, and re-layouts: 22.3 us -> 17.4 us
  Pallas kernels: 55.7 us -> 58.2 us
  matrix products: 29.1 us -> 26.7 us
  other arithmetic: 8.4 us -> 6.13 us
    all_to_all x1, waiting for transfers between devices: 12.4 us -> 6.4 us  [on_device(): lax.all_to_all(grad_logits, 'col', split_axis=2, concat_axis=0, tiled=True)]
    pallas_call x1, Pallas kernels: 23.8 us -> 26.3 us  [tail_call(): pl.pallas_call(functools.partial(tail_kernel, rows, cols), out_shape=(jax...]
    dot_general x1, matrix products: 2.42 us -> 0.59 us  [on_device(): jnp.einsum('ihd,jhd->hij', grad_attended, values_all, preferred_element_t...]
    dot_general x1, matrix products: 2.09 us -> 0.47 us  [on_device(): jnp.einsum('ihd,jhd->hij', queries, keys_all, preferred_element_type=jnp....]
    unnamed x33 -> x27, local copies, waits for them, and re-layouts: 3.43 us -> 2 us
  transfers between devices with their start and end apart: 3 -> 3, of which waited for: 3 -> 3; matrix products, arithmetic and copies ran while one was open for 14% -> 19% of each run, Pallas kernels for 0% -> 0%
where the time goes in v4:
time: 134 us; the launch traced here: 133 us
  Pallas kernels  58.2 us (43%)
  matrix products  26.7 us (20%)
  local copies, waits for them, and re-layouts  17.4 us (13%)
  waiting for transfers between devices  11.8 us (9%)
  starting transfers between devices  11.3 us (8%)
  other arithmetic  6.13 us (5%)
    pallas_call x1, Pallas kernels, pool_call(): pl.pallas_call(functools.partial(pool_kernel, rows, cols), out_shape=(jax...  31.9 us
    pallas_call x1, Pallas kernels, tail_call(): pl.pallas_call(functools.partial(tail_kernel, rows, cols), out_shape=(jax...  26.3 us
    all_to_all x2, starting transfers between devices, exchange_blocks(): return lax.all_to_all(blocks, axis, split_axis=0, concat_axis=0, tiled=True)  7.76 us
    all_to_all x1, waiting for transfers between devices, on_device(): lax.all_to_all(grad_logits, 'col', split_axis=2, concat_axis=0, tiled=True)  6.4 us
    dot_general x1, matrix products, on_device(): jnp.einsum('ijc,ch->hij', pair, w_bias, preferred_element_type=jnp.float32)  5.68 us
    all_to_all x2, waiting for transfers between devices, exchange_blocks(): return lax.all_to_all(blocks, axis, split_axis=0, concat_axis=0, tiled=True)  5.41 us
    dot_general x1, matrix products, on_device(): jnp.einsum('ijc,hij->hc', pair, bias_back, preferred_element_type=jnp.flo...  5.2 us
    convert_element_type x2, local copies, waits for them, and re-layouts, on_device(): bias_rows.astype(jnp.float32)  3.82 us
  transfers between devices with their start and end apart: 3, of which 3 were waited for; matrix products, arithmetic and copies ran while one was open for 19% of the time, Pallas kernels for 0%

profile of v4, /device:TPU:0, one launch (start us, length us, event | category | flops | bytes accessed | tf_op | source)
XLA Modules:
  0.0 132.6 jit_solution(7491423406020605119)
XLA Ops:
  0.6 0.8 fusion.32
  1.4 5.7 %convolution_convert_fusion = bf16[16,256,128]{2,0,1:T(8,128)(2,1)S(1)} fusion(bf16[256,128,128]{2,1,0:T(8,128)(2,1)} %param.14, bf16[128,16]{0,1:T(8,128)(2,1)} %param.17), kind=kOutput, calls=%fused_computation.6 | convolution fusion | flops 134742016 | bytes 9441280 | tf_op jit(solution)/shard_map/ijc,ch->hij/dot_general | solution.py:325
  7.1 1.3 copy.23
  8.4 1.5 %convolution_convert_fusion.1 = bf16[1024,384]{1,0:T(8,128)(2,1)} fusion(s32[256]{0:T(256)S(1)} %fusion.32, bf16[256,128]{1,0:T(8,128)(2,1)S(1)} %copy-done.9, bf16[256,128]{1,0:T(8,128)(2,1)S(1)} %copy-done.11, bf16[384]{0:T(512)(128)(2,1)S(1)} %pad.9.clone), kind=kOutput, calls=%fused_computation.7 | convolution fusion | flops 202571776 | bytes 919296 | tf_op jit(solution)/shard_map/dot_general | solution.py:322
  9.9 31.9 %shard_map.121 = (bf16[8,32,384]{2,1,0:T(8,128)(2,1)}, f32[32,128]{1,0:T(8,128)}, bf16[8,2,256,128]{3,2,1,0:T(8,128)(2,1)}) custom-call(bf16[8,128,384]{2,1,0:T(8,128)(2,1)} %bitcast.84, bf16[8,2,256,128]{3,2,1,0:T(8,128)(2,1)} %bitcast.81), custom_call_target="tpu_custom_call" | custom-call | tf_op jit(solution)/shard_map/pallas_call | solution.py:158
  41.9 1.2 fusion.36
  43.0 0.2 multiply_reduce_fusion.1
  43.3 0.2 subtract_multiply_fusion
  43.5 0.3 fusion.12
  43.8 0.8 broadcast_in_dim.5
  44.6 4.1 %all-to-all-start = ((bf16[4,2,256,96]{2,3,1,0:T(8,128)(2,1)}), bf16[4,2,256,96]{2,3,1,0:T(8,128)(2,1)}, u32[]{:S(2)}, u32[]{:S(2)}) async-start(bf16[4,2,256,96]{2,3,1,0:T(8,128)(2,1)} %broadcast_in_dim.5), calls=%async_computation | async-start | bytes 786432 | tf_op jit(solution)/shard_map/all_to_all | solution.py:38
  48.8 0.6 constant_dynamic-slice_fusion.2.single_ref
  49.4 0.6 slice.44
  50.0 0.7 copy.33.inverse_ref
  50.7 1.4 %convert_bitcast_fusion = f32[2,256,8,128]{3,1,0,2:T(8,128)S(1)} fusion(bf16[8,2,256,128]{3,2,1,0:T(8,128)(2,1)} %get-tuple-element.11), kind=kLoop, calls=%fused_computation.1 | loop fusion | flops 524288 | bytes 3145728 | tf_op jit(solution)/shard_map/convert_element_type | solution.py:349
  52.2 1.9 %copy.26 = f32[2,256,8,128]{1,3,2,0:T(8,128)} copy(f32[2,256,8,128]{3,1,0,2:T(8,128)S(1)} %convert_bitcast_fusion) | data formatting | bytes 4194304 | tf_op jit(solution)/shard_map/convert_element_type | solution.py:349
  54.0 2.0 %copy.27 = f32[2,256,1024]{2,1,0:T(8,128)S(1)} copy(f32[2,256,1024]{1,2,0:T(8,128)} %bitcast.80) | data formatting | bytes 4194304 | tf_op jit(solution)/shard_map/convert_element_type | solution.py:349
  56.0 1.1 fusion.27
  57.1 0.7 constant_dynamic-slice_fusion
  57.8 1.2 convolution_convert_fusion.6
  59.0 2.0 %all-to-all-done = bf16[4,2,256,96]{2,3,1,0:T(8,128)(2,1)} async-done(((bf16[4,2,256,96]{2,3,1,0:T(8,128)(2,1)}), bf16[4,2,256,96]{2,3,1,0:T(8,128)(2,1)}, u32[]{:S(2)}, u32[]{:S(2)}) %all-to-all-start) | async-done | bytes 393248 | tf_op jit(solution)/shard_map/all_to_all | solution.py:38
  61.0 1.0 fusion.35
  62.0 0.2 copy.24
  62.3 0.2 copy.25
  62.6 0.5 multiply_add_fusion
  63.1 0.7 fusion.37
  63.8 0.6 copy-done.1
  64.5 0.6 multiply_reduce_fusion
  65.0 0.4 multiply_convert_fusion
  65.4 2.1 %copy.31 = bf16[2,256,1024]{1,0,2:T(2,128)(2,1)} copy(bf16[2,256,1024]{2,1,0:T(8,128)(2,1)S(1)} %multiply_convert_fusion) | data formatting | bytes 2097152 | tf_op jit(solution)/shard_map/convert_element_type | solution.py:368
  67.5 3.6 %all-to-all-start.1 = ((bf16[2,256,1024]{1,0,2:T(2,128)(2,1)}), bf16[2,256,1024]{1,0,2:T(2,128)(2,1)S(1)}, u32[]{:S(2)}, u32[]{:S(2)}) async-start(bf16[2,256,1024]{1,0,2:T(2,128)(2,1)} %copy.31), calls=%async_computation.1 | async-start | bytes 2097152 | tf_op jit(solution)/shard_map/all_to_all | solution.py:388
  71.1 3.3 %fusion.3 = bf16[1024,2,48]{0,2,1:T(8,128)(2,1)S(1)} fusion(bf16[256,2,48]{0,2,1:T(8,128)(2,1)S(1)} %bitcast.92, f32[2,256]{1,0:T(2,128)S(1)} %get-tuple-element.23, f32[2,256,1024]{2,1,0:T(8,128)} %copy-done.1), kind=kOutput, calls=%fused_computation.15 | convolution fusion | flops 52004352 | bytes 2344960 | tf_op jit(solution)/shard_map/hij,ihd->jhd/dot_general | solution.py:380
  74.6 3.5 %fusion.5 = bf16[256,2,48]{0,2,1:T(8,128)(2,1)S(1)} fusion(bf16[1024,2,48]{0,2,1:T(8,128)(2,1)S(1)} %copy-done.8, f32[2,256]{1,0:T(2,128)S(1)} %get-tuple-element.23, f32[2,256,1024]{2,1,0:T(8,128)} %copy-done.1), kind=kOutput, calls=%fused_computation.20 | convolution fusion | flops 51930624 | bytes 2344960 | tf_op jit(solution)/shard_map/hij,jhd->ihd/dot_general | solution.py:354
  78.3 0.3 fusion.2
  78.8 0.8 maximum_bitcast_fusion
  79.6 0.4 fusion.4
  80.0 6.4 %all-to-all-done.1 = bf16[2,256,1024]{1,0,2:T(2,128)(2,1)S(1)} async-done(((bf16[2,256,1024]{1,0,2:T(2,128)(2,1)}), bf16[2,256,1024]{1,0,2:T(2,128)(2,1)S(1)}, u32[]{:S(2)}, u32[]{:S(2)}) %all-to-all-start.1) | async-done | bytes 1048608 | tf_op jit(solution)/shard_map/all_to_all | solution.py:388
  86.4 2.5 %copy.32 = bf16[8,2,256,128]{3,1,0,2:T(2,128)(2,1)S(1)} copy(bf16[8,2,256,128]{2,1,3,0:T(2,128)(2,1)S(1)} %bitcast.82) | data formatting | bytes 2097152 | tf_op jit(solution)/shard_map/all_to_all | solution.py:388
  88.9 3.7 %all-to-all-start.2 = ((bf16[4,2,256,96]{2,3,1,0:T(8,128)(2,1)}), bf16[4,2,256,96]{2,3,1,0:T(8,128)(2,1)S(1)}, u32[]{:S(2)}, u32[]{:S(2)}) async-start(bf16[4,2,256,96]{2,3,1,0:T(8,128)(2,1)} %maximum_bitcast_fusion), calls=%async_computation.2 | async-start | bytes 786432 | tf_op jit(solution)/shard_map/all_to_all | solution.py:38
  92.6 0.2 convolution_convert_fusion.2
  92.8 5.2 %convolution_bitcast_fusion.1.weight_ref = f32[16,128]{1,0:T(8,128)} fusion(bf16[16,256,128]{2,0,1:T(8,128)(2,1)S(1)} %bitcast.79, bf16[256,128,128]{2,1,0:T(8,128)(2,1)} %param.14), kind=kOutput, calls=%fused_computation.21 | convolution fusion | flops 134217728 | bytes 9445376 | tf_op jit(solution)/shard_map/ijc,hij->hc/dot_general | solution.py:396
  98.0 3.4 %all-to-all-done.2 = bf16[4,2,256,96]{2,3,1,0:T(8,128)(2,1)S(1)} async-done(((bf16[4,2,256,96]{2,3,1,0:T(8,128)(2,1)}), bf16[4,2,256,96]{2,3,1,0:T(8,128)(2,1)S(1)}, u32[]{:S(2)}, u32[]{:S(2)}) %all-to-all-start.2) | async-done | bytes 393248 | tf_op jit(solution)/shard_map/all_to_all | solution.py:38
  101.5 0.4 fusion.1
  102.0 1.0 pad_maximum_fusion.both_ref
  102.9 26.3 %shard_map.122 = (bf16[8,4,32,256]{3,2,1,0:T(8,128)(2,1)}, f32[16,128]{1,0:T(8,128)}) custom-call(bf16[8,32,1536]{2,1,0:T(8,128)(2,1)} %pad_maximum_fusion.both_ref, f32[32,768]{1,0:T(8,128)} %constant_dynamic-slice_fusion.2.single_ref, f32[32,768]{1,0:T(8,128)} %get-tuple-element.28.grad_out_ref, f32[32,768]{1,0:T(8,128)} %get-tuple-element.27.normal_ref, ...), custom_call_target="tpu_custom_call" | custom-call | tf_op jit(solution)/shard_map/pallas_call | solution.py:277
  129.2 1.4 %fusion.6 = f32[256,256]{1,0:T(8,128)S(1)} fusion(bf16[1024,256]{1,0:T(8,128)(2,1)} %bitcast.94, s32[256]{0:T(256)S(1)} %fusion.32), kind=kOutput, calls=%fused_computation.24 | convolution fusion | flops 134479872 | bytes 787456 | tf_op jit(solution)/shard_map/dot_general | solution.py:414
  130.6 0.7 slice_add_fusion
  131.3 1.3 copy.35
  (43 shorter events, 1.0 us)
Async XLA Ops:
  0.6 42.8 %copy-start = (bf16[3,768,96]{1,2,0:T(8,128)(2,1)S(1)}, bf16[3,768,96]{1,2,0:T(8,128)(2,1)}, u32[]{:S(2)}) copy-start(bf16[3,768,96]{1,2,0:T(8,128)(2,1)} %param.16) | copy-start | bytes 1327108
  7.1 1.3 %copy-start.9 = (bf16[256,128]{1,0:T(8,128)(2,1)S(1)}, bf16[256,128]{1,0:T(8,128)(2,1)}, u32[]{:S(2)}) copy-start(bf16[256,128]{1,0:T(8,128)(2,1)} %param.12) | copy-start | bytes 196612
  7.1 1.4 %copy-start.11 = (bf16[256,128]{1,0:T(8,128)(2,1)S(1)}, bf16[256,128]{1,0:T(8,128)(2,1)}, u32[]{:S(2)}) copy-start(bf16[256,128]{1,0:T(8,128)(2,1)} %param.10) | copy-start | bytes 196612
  7.1 34.8 %copy-start.3 = (bf16[128,768]{1,0:T(8,128)(2,1)S(1)}, bf16[128,768]{1,0:T(8,128)(2,1)}, u32[]{:S(2)}) copy-start(bf16[128,768]{1,0:T(8,128)(2,1)} %pool_ref.1) | copy-start | bytes 589828
  7.1 34.8 %copy-start.6 = (bf16[256,768]{1,0:T(8,128)(2,1)S(1)}, bf16[256,768]{1,0:T(8,128)(2,1)}, u32[]{:S(2)}) copy-start(bf16[256,768]{1,0:T(8,128)(2,1)} %param.13) | copy-start | bytes 1179652
  44.6 16.4 %all-to-all-start = ((bf16[4,2,256,96]{2,3,1,0:T(8,128)(2,1)}), bf16[4,2,256,96]{2,3,1,0:T(8,128)(2,1)}, u32[]{:S(2)}, u32[]{:S(2)}) async-start(bf16[4,2,256,96]{2,3,1,0:T(8,128)(2,1)} %broadcast_in_dim.5), calls=%async_computation | async-start | bytes 786432 | tf_op jit(solution)/shard_map/all_to_all | solution.py:38
  54.0 2.0 %copy-start.2 = (bf16[768,128]{1,0:T(8,128)(2,1)S(1)}, bf16[768,128]{1,0:T(8,128)(2,1)}, u32[]{:S(2)}) copy-start(bf16[768,128]{1,0:T(8,128)(2,1)} %dec_ref.1) | copy-start | bytes 589828
  57.1 5.5 %copy-start.5 = (bf16[1,256,96]{1,2,0:T(8,128)(2,1)S(1)}, bf16[1,256,96]{1,2,0:T(8,128)(2,1)}, u32[]{:S(2)}) copy-start(bf16[1,256,96]{1,2,0:T(8,128)(2,1)} %slice.44) | copy-start | bytes 147460
  62.3 2.1 %copy-start.7 = (bf16[1024,2,48]{0,2,1:T(8,128)(2,1)}, bf16[1024,2,48]{0,2,1:T(8,128)(2,1)S(1)}, u32[]{:S(2)}) copy-start(bf16[1024,2,48]{0,2,1:T(8,128)(2,1)S(1)} %reshape_squeeze.9) | copy-start | bytes 589828
  63.1 1.3 %copy-start.1 = (f32[2,256,1024]{2,1,0:T(8,128)}, f32[2,256,1024]{2,1,0:T(8,128)S(1)}, u32[]{:S(2)}) copy-start(f32[2,256,1024]{2,1,0:T(8,128)S(1)} %multiply_add_fusion) | copy-start | bytes 6291460
  67.5 18.9 %all-to-all-start.1 = ((bf16[2,256,1024]{1,0,2:T(2,128)(2,1)}), bf16[2,256,1024]{1,0,2:T(2,128)(2,1)S(1)}, u32[]{:S(2)}, u32[]{:S(2)}) async-start(bf16[2,256,1024]{1,0,2:T(2,128)(2,1)} %copy.31), calls=%async_computation.1 | async-start | bytes 2097152 | tf_op jit(solution)/shard_map/all_to_all | solution.py:388
  71.1 3.5 %copy-start.8 = (bf16[1024,2,48]{0,2,1:T(8,128)(2,1)S(1)}, bf16[1024,2,48]{0,2,1:T(8,128)(2,1)}, u32[]{:S(2)}) copy-start(bf16[1024,2,48]{0,2,1:T(8,128)(2,1)} %copy-done.7) | copy-start | bytes 589828
  79.5 13.0 %copy-start.4 = (bf16[96,768]{1,0:T(8,128)(2,1)S(1)}, bf16[96,768]{1,0:T(8,128)(2,1)}, u32[]{:S(2)}) copy-start(bf16[96,768]{1,0:T(8,128)(2,1)} %param.18) | copy-start | bytes 442372
  88.9 12.5 %all-to-all-start.2 = ((bf16[4,2,256,96]{2,3,1,0:T(8,128)(2,1)}), bf16[4,2,256,96]{2,3,1,0:T(8,128)(2,1)S(1)}, u32[]{:S(2)}, u32[]{:S(2)}) async-start(bf16[4,2,256,96]{2,3,1,0:T(8,128)(2,1)} %maximum_bitcast_fusion), calls=%async_computation.2 | async-start | bytes 786432 | tf_op jit(solution)/shard_map/all_to_all | solution.py:38
  101.9 28.7 %copy-start.10 = (bf16[256,128]{1,0:T(8,128)(2,1)S(1)}, bf16[256,128]{1,0:T(8,128)(2,1)}, u32[]{:S(2)}) copy-start(bf16[256,128]{1,0:T(8,128)(2,1)} %param.12) | copy-start | bytes 196612
  101.9 28.7 %copy-start.12 = (bf16[256,128]{1,0:T(8,128)(2,1)S(1)}, bf16[256,128]{1,0:T(8,128)(2,1)}, u32[]{:S(2)}) copy-start(bf16[256,128]{1,0:T(8,128)(2,1)} %param.10) | copy-start | bytes 196612

commit v5 on v4

--- a/solution.py
+++ b/solution.py
@@ -81,98 +81,108 @@
     rows,
     cols,
     sums_ref,
+    tally_ref,
     bias_ref,
     out_ref,
     counts_ref,
     bias_out_ref,
+    got_row,
+    row_sum,
     got_col,
-    col_sum,
-    got_row,
+    row_tally,
+    sum_tally,
+    col_tally,
+    all_tally,
     send_sems,
     recv_sems,
 ):
     row, col = lax.axis_index("row"), lax.axis_index("col")
     greet((("row", rows), ("col", cols)))
-    width = out_ref.shape[-1] // 3
-    copies = [
-        push(sums_ref.at[peer], got_col.at[step - 1], send_sems, recv_sems, step - 1, "col", peer)
-        for step, peer in peers_of("col", cols)
-    ]
-    base = 2 * (cols - 1) + rows - 1
-    bias_copies = [
-        push(
-            bias_ref.at[peer],
-            bias_out_ref.at[col],
-            send_sems,
-            recv_sems,
-            base + step - 1,
-            "col",
-            peer,
-        )
-        for step, peer in peers_of("col", cols)
-    ]
+    share, width = out_ref.shape[1:]
+    base = 0
+
+    def send_all(axis, size, source, target):
+        nonlocal base
+        copies = [
+            push(
+                source(peer), target(step - 1), send_sems, recv_sems, base + step - 1, axis, peer
+            )
+            for step, peer in peers_of(axis, size)
+        ]
+        base += size - 1
+        return copies
+
+    sums = send_all("row", rows, lambda peer: sums_ref.at[:, peer], lambda at: got_row.at[at])
+    tallies = send_all("row", rows, lambda peer: tally_ref.at[peer], lambda at: row_tally.at[at])
+    bias_copies = send_all(
+        "col", cols, lambda peer: bias_ref.at[peer], lambda at: bias_out_ref.at[col]
+    )
     bias_out_ref[col] = bias_ref[col]
-    total = sums_ref[col].astype(jnp.float32)
-    for at, copy in enumerate(copies):
-        copy.wait()
-        total = total + got_col[at].astype(jnp.float32)
-    col_sum[...] = total.reshape(col_sum.shape)
-    base = cols - 1
-    copies = [
-        push(
-            col_sum.at[peer],
-            got_row.at[step - 1],
-            send_sems,
-            recv_sems,
-            base + step - 1,
-            "row",
-            peer,
-        )
-        for step, peer in peers_of("row", rows)
-    ]
-    total = col_sum[row]
-    for at, copy in enumerate(copies):
-        copy.wait()
-        total = total + got_row[at]
-    counts = total[:, 2 * width :]
-    counts_ref[...] = counts
-    out_ref[col] = jnp.concatenate(
-        [total[:, :width] / counts, total[:, width:]], axis=1
-    ).astype(out_ref.dtype)
-    base += rows - 1
-    copies = [
-        push(
-            out_ref.at[col], out_ref.at[col], send_sems, recv_sems, base + step - 1, "col", peer
-        )
-        for step, peer in peers_of("col", cols)
-    ]
+    tally = tally_ref[row]
+    for at, copy in enumerate(tallies):
+        copy.wait()
+        tally = tally + row_tally[at]
+    sum_tally[...] = tally
+    tallies = send_all("col", cols, lambda peer: sum_tally, lambda at: col_tally.at[at])
+    total = sums_ref[:, row].astype(jnp.float32)
+    for at, copy in enumerate(sums):
+        copy.wait()
+        total = total + got_row[at].astype(jnp.float32)
+    row_sum[...] = total
+    sums = send_all("col", cols, lambda peer: row_sum.at[peer], lambda at: got_col.at[at])
+    for at, copy in enumerate(tallies):
+        copy.wait()
+        tally = tally + col_tally[at]
+    all_tally[...] = tally
+    mine = jnp.broadcast_to(all_tally[pl.ds(col, 1), :], (share, tally.shape[1]))
+    diagonal = lax.broadcasted_iota(jnp.int32, mine.shape, 0) == lax.broadcasted_iota(
+        jnp.int32, mine.shape, 1
+    )
+    counts = jnp.sum(jnp.where(diagonal, mine, 0.0), axis=1, keepdims=True)
+    counts_ref[...] = jnp.broadcast_to(counts, counts_ref.shape)
+    total = row_sum[col]
+    for at, copy in enumerate(sums):
+        copy.wait()
+        total = total + got_col[at]
+    half = width // 2
+    out_ref[col] = jnp.concatenate([total[:, :half] / counts, total[:, half:]], axis=1).astype(
+        out_ref.dtype
+    )
+    copies = send_all("col", cols, lambda peer: out_ref.at[col], lambda at: out_ref.at[col])
     for copy in copies + bias_copies:
         copy.wait()
 
 
-def pool_call(partial_sums, bias, share):
+def pool_call(partial_sums, partial_counts, bias, share):
     rows, cols = lax.axis_size("row"), lax.axis_size("col")
     width = partial_sums.shape[-1]
-    copies = 3 * (cols - 1) + rows - 1
+    copies = 4 * (cols - 1) + 2 * (rows - 1)
     bias = bias.reshape((cols, -1) + bias.shape[1:])
+    lanes = width // 2
+    tally = jnp.swapaxes(partial_counts.reshape(cols, rows, share), 0, 1)
+    tally = jnp.pad(tally, ((0, 0), (0, 0), (0, lanes - share)))
     return pl.pallas_call(
         functools.partial(pool_kernel, rows, cols),
         out_shape=(
             jax.ShapeDtypeStruct((cols, share, width), jnp.bfloat16),
-            jax.ShapeDtypeStruct((share, width // 3), jnp.float32),
+            jax.ShapeDtypeStruct((share, width // 2), jnp.float32),
             jax.ShapeDtypeStruct(bias.shape, bias.dtype),
         ),
-        in_specs=[pl.BlockSpec(memory_space=pltpu.VMEM)] * 2,
+        in_specs=[pl.BlockSpec(memory_space=pltpu.VMEM)] * 3,
         out_specs=(pl.BlockSpec(memory_space=pltpu.VMEM),) * 3,
         scratch_shapes=[
-            pltpu.VMEM((cols - 1, rows * share, width), jnp.bfloat16),
-            pltpu.VMEM((rows, share, width), jnp.float32),
-            pltpu.VMEM((rows - 1, share, width), jnp.float32),
+            pltpu.VMEM((rows - 1, cols, share, width), jnp.bfloat16),
+            pltpu.VMEM((cols, share, width), jnp.float32),
+            pltpu.VMEM((cols - 1, share, width), jnp.float32),
+            pltpu.VMEM((rows - 1, cols, lanes), jnp.float32),
+            pltpu.VMEM((cols, lanes), jnp.float32),
+            pltpu.VMEM((cols - 1, cols, lanes), jnp.float32),
+            pltpu.VMEM((cols, lanes), jnp.float32),
             pltpu.SemaphoreType.DMA((copies,)),
             pltpu.SemaphoreType.DMA((copies,)),
         ],
         compiler_params=pltpu.CompilerParams(collective_id=0, has_side_effects=True),
-    )(partial_sums.reshape(cols, rows * share, width), bias)
+    )(partial_sums.reshape(cols, rows, share, width), tally, bias)
 
 
 def tail_kernel(
@@ -318,15 +328,18 @@
         share_order(atom_token, tok_rows, share)[:, None]
         == jnp.arange(total_tokens, dtype=jnp.int32)[None, :]
     ).astype(jnp.bfloat16)
-    stacked = jnp.concatenate([atom_single, atom_cot, jnp.ones_like(atom_cot)], axis=1)
+    stacked = jnp.concatenate([atom_single, atom_cot], axis=1)
     partial_sums = lax.dot_general(
         onehot, stacked, (((0,), (0,)), ((), ())), preferred_element_type=jnp.float32
     ).astype(jnp.bfloat16)
+    partial_counts = jnp.sum(onehot.astype(jnp.float32), axis=0)
     bias_local = jnp.einsum("ijc,ch->hij", pair, w_bias, preferred_element_type=jnp.float32).astype(
         jnp.bfloat16
     )
-    row_pooled, share_counts, bias_blocks = pool_call(partial_sums, bias_local, share)
-    row_pooled = row_pooled.reshape(tok_rows, 3 * atom_width)
+    row_pooled, share_counts, bias_blocks = pool_call(
+        partial_sums, partial_counts, bias_local, share
+    )
+    row_pooled = row_pooled.reshape(tok_rows, 2 * atom_width)
     pooled = row_pooled[:, :atom_width]
     cot_pooled = row_pooled[:, atom_width : 2 * atom_width]
     single = token_cond.astype(jnp.float32) + jnp.dot(

time: 134 us -> 133 us (level)
  Pallas kernels: 58.2 us -> 56.2 us
    pallas_call x1, Pallas kernels: 31.9 us -> 29.9 us  [pool_call(): pl.pallas_call(functools.partial(pool_kernel, rows, cols), out_shape=(jax...]
where the time goes in v5:
time: 133 us; the launch traced here: 131 us
  Pallas kernels  56.2 us (42%)
  matrix products  26.6 us (20%)
  local copies, waits for them, and re-layouts  18.1 us (14%)
  waiting for transfers between devices  11.8 us (9%)
  starting transfers between devices  11.3 us (8%)
  other arithmetic  6.28 us (5%)
    pallas_call x1, Pallas kernels, pool_call(): pl.pallas_call(functools.partial(pool_kernel, rows, cols), out_shape=(jax...  29.9 us
    pallas_call x1, Pallas kernels, tail_call(): pl.pallas_call(functools.partial(tail_kernel, rows, cols), out_shape=(jax...  26.3 us
    all_to_all x2, starting transfers between devices, exchange_blocks(): return lax.all_to_all(blocks, axis, split_axis=0, concat_axis=0, tiled=True)  7.77 us
    all_to_all x1, waiting for transfers between devices, on_device(): lax.all_to_all(grad_logits, 'col', split_axis=2, concat_axis=0, tiled=True)  6.42 us
    dot_general x1, matrix products, on_device(): jnp.einsum('ijc,ch->hij', pair, w_bias, preferred_element_type=jnp.float32)  5.68 us
    all_to_all x2, waiting for transfers between devices, exchange_blocks(): return lax.all_to_all(blocks, axis, split_axis=0, concat_axis=0, tiled=True)  5.37 us
    dot_general x1, matrix products, on_device(): jnp.einsum('ijc,hij->hc', pair, bias_back, preferred_element_type=jnp.flo...  5.2 us
    convert_element_type x2, local copies, waits for them, and re-layouts, on_device(): bias_rows.astype(jnp.float32)  3.83 us
  transfers between devices with their start and end apart: 3, of which 3 were waited for; matrix products, arithmetic and copies ran while one was open for 19% of the time, Pallas kernels for 0%

profile of v5, /device:TPU:0, one launch (start us, length us, event | category | flops | bytes accessed | tf_op | source)
XLA Modules:
  0.0 131.4 jit_solution(14142309429778200028)
XLA Ops:
  0.6 0.8 fusion.31
  1.4 0.2 convert_reduce_fusion
  1.7 5.7 %convolution_convert_fusion = bf16[16,256,128]{2,0,1:T(8,128)(2,1)S(1)} fusion(bf16[256,128,128]{2,1,0:T(8,128)(2,1)} %param.14, bf16[128,16]{0,1:T(8,128)(2,1)} %param.17), kind=kOutput, calls=%fused_computation.6 | convolution fusion | flops 134742016 | bytes 9441280 | tf_op jit(solution)/shard_map/ijc,ch->hij/dot_general | solution.py:336
  7.4 1.3 copy.37
  8.7 0.6 pad.4.tally_ref
  9.3 1.4 %convolution_convert_fusion.1 = bf16[1024,256]{1,0:T(8,128)(2,1)} fusion(s32[256]{0:T(256)S(1)} %fusion.31, bf16[256,128]{1,0:T(8,128)(2,1)S(1)} %copy-done.9, bf16[256,128]{1,0:T(8,128)(2,1)S(1)} %copy-done.11), kind=kOutput, calls=%fused_computation.7 | convolution fusion | flops 135004160 | bytes 656384 | tf_op jit(solution)/shard_map/dot_general | solution.py:332
  10.7 29.9 %shard_map.121 = (bf16[8,32,256]{2,1,0:T(8,128)(2,1)}, f32[32,128]{1,0:T(8,128)}, bf16[8,2,256,128]{3,2,1,0:T(8,128)(2,1)}) custom-call(bf16[8,4,32,256]{3,2,1,0:T(8,128)(2,1)} %bitcast.87, f32[4,8,128]{2,1,0:T(8,128)} %pad.4.tally_ref, bf16[8,2,256,128]{3,2,1,0:T(8,128)(2,1)} %bitcast.85), custom_call_target="tpu_custom_call" | custom-call | tf_op jit(solution)/shard_map/pallas_call | solution.py:164
  40.6 1.2 fusion.35
  41.8 0.2 multiply_reduce_fusion.1
  42.2 0.3 fusion.13
  42.5 0.8 broadcast_in_dim.2
  43.3 4.1 %all-to-all-start = ((bf16[4,2,256,96]{2,3,1,0:T(8,128)(2,1)}), bf16[4,2,256,96]{2,3,1,0:T(8,128)(2,1)}, u32[]{:S(2)}, u32[]{:S(2)}) async-start(bf16[4,2,256,96]{2,3,1,0:T(8,128)(2,1)} %broadcast_in_dim.2), calls=%async_computation | async-start | bytes 786432 | tf_op jit(solution)/shard_map/all_to_all | solution.py:38
  47.5 0.6 constant_dynamic-slice_fusion.2.single_ref
  48.2 0.6 slice.44
  48.8 0.7 copy.47.inverse_ref
  49.5 1.4 %convert_bitcast_fusion = f32[2,256,8,128]{3,1,0,2:T(8,128)S(1)} fusion(bf16[8,2,256,128]{3,2,1,0:T(8,128)(2,1)} %get-tuple-element.11), kind=kLoop, calls=%fused_computation.1 | loop fusion | flops 524288 | bytes 3145728 | tf_op jit(solution)/shard_map/convert_element_type | solution.py:362
  50.9 1.9 %copy.40 = f32[2,256,8,128]{1,3,2,0:T(8,128)} copy(f32[2,256,8,128]{3,1,0,2:T(8,128)S(1)} %convert_bitcast_fusion) | data formatting | bytes 4194304 | tf_op jit(solution)/shard_map/convert_element_type | solution.py:362
  52.8 2.0 %copy.41 = f32[2,256,1024]{2,1,0:T(8,128)S(1)} copy(f32[2,256,1024]{1,2,0:T(8,128)} %bitcast.83) | data formatting | bytes 4194304 | tf_op jit(solution)/shard_map/convert_element_type | solution.py:362
  54.8 1.1 fusion.26
  55.9 0.7 constant_dynamic-slice_fusion
  56.6 1.2 convolution_convert_fusion.6
  57.8 1.9 %all-to-all-done = bf16[4,2,256,96]{2,3,1,0:T(8,128)(2,1)} async-done(((bf16[4,2,256,96]{2,3,1,0:T(8,128)(2,1)}), bf16[4,2,256,96]{2,3,1,0:T(8,128)(2,1)}, u32[]{:S(2)}, u32[]{:S(2)}) %all-to-all-start) | async-done | bytes 393248 | tf_op jit(solution)/shard_map/all_to_all | solution.py:38
  59.7 1.0 fusion.34
  60.8 0.2 copy.38
  61.4 0.5 multiply_add_fusion
  61.9 0.7 fusion.36
  62.5 0.7 copy-done.1
  63.2 0.6 multiply_reduce_fusion
  63.8 0.4 multiply_convert_fusion
  64.2 2.1 %copy.45 = bf16[2,256,1024]{1,0,2:T(2,128)(2,1)} copy(bf16[2,256,1024]{2,1,0:T(8,128)(2,1)S(1)} %multiply_convert_fusion) | data formatting | bytes 2097152 | tf_op jit(solution)/shard_map/convert_element_type | solution.py:381
  66.3 3.6 %all-to-all-start.1 = ((bf16[2,256,1024]{1,0,2:T(2,128)(2,1)}), bf16[2,256,1024]{1,0,2:T(2,128)(2,1)S(1)}, u32[]{:S(2)}, u32[]{:S(2)}) async-start(bf16[2,256,1024]{1,0,2:T(2,128)(2,1)} %copy.45), calls=%async_computation.1 | async-start | bytes 2097152 | tf_op jit(solution)/shard_map/all_to_all | solution.py:401
  69.8 3.3 %fusion.3 = bf16[1024,2,48]{0,2,1:T(8,128)(2,1)S(1)} fusion(bf16[256,2,48]{0,2,1:T(8,128)(2,1)S(1)} %bitcast.96, f32[2,256]{1,0:T(2,128)S(1)} %get-tuple-element.23, f32[2,256,1024]{2,1,0:T(8,128)} %copy-done.1), kind=kOutput, calls=%fused_computation.15 | convolution fusion | flops 52004352 | bytes 2344960 | tf_op jit(solution)/shard_map/hij,ihd->jhd/dot_general | solution.py:393
  73.4 3.5 %fusion.5 = bf16[256,2,48]{0,2,1:T(8,128)(2,1)S(1)} fusion(bf16[1024,2,48]{0,2,1:T(8,128)(2,1)S(1)} %copy-done.8, f32[2,256]{1,0:T(2,128)S(1)} %get-tuple-element.23, f32[2,256,1024]{2,1,0:T(8,128)} %copy-done.1), kind=kOutput, calls=%fused_computation.20 | convolution fusion | flops 51930624 | bytes 2344960 | tf_op jit(solution)/shard_map/hij,jhd->ihd/dot_general | solution.py:367
  77.1 0.3 fusion.2
  77.5 0.8 maximum_bitcast_fusion
  78.3 0.4 fusion.4
  78.7 6.4 %all-to-all-done.1 = bf16[2,256,1024]{1,0,2:T(2,128)(2,1)S(1)} async-done(((bf16[2,256,1024]{1,0,2:T(2,128)(2,1)}), bf16[2,256,1024]{1,0,2:T(2,128)(2,1)S(1)}, u32[]{:S(2)}, u32[]{:S(2)}) %all-to-all-start.1) | async-done | bytes 1048608 | tf_op jit(solution)/shard_map/all_to_all | solution.py:401
  85.2 2.5 %copy.46 = bf16[8,2,256,128]{3,1,0,2:T(2,128)(2,1)S(1)} copy(bf16[8,2,256,128]{2,1,3,0:T(2,128)(2,1)S(1)} %bitcast.84) | data formatting | bytes 2097152 | tf_op jit(solution)/shard_map/all_to_all | solution.py:401
  87.7 3.7 %all-to-all-start.2 = ((bf16[4,2,256,96]{2,3,1,0:T(8,128)(2,1)}), bf16[4,2,256,96]{2,3,1,0:T(8,128)(2,1)S(1)}, u32[]{:S(2)}, u32[]{:S(2)}) async-start(bf16[4,2,256,96]{2,3,1,0:T(8,128)(2,1)} %maximum_bitcast_fusion), calls=%async_computation.2 | async-start | bytes 786432 | tf_op jit(solution)/shard_map/all_to_all | solution.py:38
  91.3 0.2 convolution_convert_fusion.2
  91.6 5.2 %convolution_bitcast_fusion.1.weight_ref = f32[16,128]{1,0:T(8,128)} fusion(bf16[16,256,128]{2,0,1:T(8,128)(2,1)S(1)} %bitcast.82, bf16[256,128,128]{2,1,0:T(8,128)(2,1)} %param.14), kind=kOutput, calls=%fused_computation.21 | convolution fusion | flops 134217728 | bytes 9445376 | tf_op jit(solution)/shard_map/ijc,hij->hc/dot_general | solution.py:409
  96.8 3.4 %all-to-all-done.2 = bf16[4,2,256,96]{2,3,1,0:T(8,128)(2,1)S(1)} async-done(((bf16[4,2,256,96]{2,3,1,0:T(8,128)(2,1)}), bf16[4,2,256,96]{2,3,1,0:T(8,128)(2,1)S(1)}, u32[]{:S(2)}, u32[]{:S(2)}) %all-to-all-start.2) | async-done | bytes 393248 | tf_op jit(solution)/shard_map/all_to_all | solution.py:38
  100.3 0.4 fusion.1
  100.7 0.9 pad_maximum_fusion.both_ref
  101.7 26.3 %shard_map.122 = (bf16[8,4,32,256]{3,2,1,0:T(8,128)(2,1)}, f32[16,128]{1,0:T(8,128)}) custom-call(bf16[8,32,1536]{2,1,0:T(8,128)(2,1)} %pad_maximum_fusion.both_ref, f32[32,768]{1,0:T(8,128)} %constant_dynamic-slice_fusion.2.single_ref, f32[32,768]{1,0:T(8,128)} %get-tuple-element.28.grad_out_ref, f32[32,768]{1,0:T(8,128)} %get-tuple-element.27.normal_ref, ...), custom_call_target="tpu_custom_call" | custom-call | tf_op jit(solution)/shard_map/pallas_call | solution.py:287
  128.0 1.4 %fusion.6 = f32[256,256]{1,0:T(8,128)S(1)} fusion(bf16[1024,256]{1,0:T(8,128)(2,1)} %bitcast.98, s32[256]{0:T(256)S(1)} %fusion.31), kind=kOutput, calls=%fused_computation.25 | convolution fusion | flops 134479872 | bytes 787456 | tf_op jit(solution)/shard_map/dot_general | solution.py:427
  129.4 0.7 slice_add_fusion
  130.1 1.3 copy.51
  (45 shorter events, 1.4 us)
Async XLA Ops:
  0.6 41.5 %copy-start = (bf16[3,768,96]{1,2,0:T(8,128)(2,1)S(1)}, bf16[3,768,96]{1,2,0:T(8,128)(2,1)}, u32[]{:S(2)}) copy-start(bf16[3,768,96]{1,2,0:T(8,128)(2,1)} %param.16) | copy-start | bytes 1327108
  7.3 2.0 %copy-start.9 = (bf16[256,128]{1,0:T(8,128)(2,1)S(1)}, bf16[256,128]{1,0:T(8,128)(2,1)}, u32[]{:S(2)}) copy-start(bf16[256,128]{1,0:T(8,128)(2,1)} %param.12) | copy-start | bytes 196612
  7.3 2.0 %copy-start.11 = (bf16[256,128]{1,0:T(8,128)(2,1)S(1)}, bf16[256,128]{1,0:T(8,128)(2,1)}, u32[]{:S(2)}) copy-start(bf16[256,128]{1,0:T(8,128)(2,1)} %param.10) | copy-start | bytes 196612
  7.4 33.2 %copy-start.3 = (bf16[128,768]{1,0:T(8,128)(2,1)S(1)}, bf16[128,768]{1,0:T(8,128)(2,1)}, u32[]{:S(2)}) copy-start(bf16[128,768]{1,0:T(8,128)(2,1)} %pool_ref.1) | copy-start | bytes 589828
  7.4 33.2 %copy-start.6 = (bf16[256,768]{1,0:T(8,128)(2,1)S(1)}, bf16[256,768]{1,0:T(8,128)(2,1)}, u32[]{:S(2)}) copy-start(bf16[256,768]{1,0:T(8,128)(2,1)} %param.13) | copy-start | bytes 1179652
  43.3 16.4 %all-to-all-start = ((bf16[4,2,256,96]{2,3,1,0:T(8,128)(2,1)}), bf16[4,2,256,96]{2,3,1,0:T(8,128)(2,1)}, u32[]{:S(2)}, u32[]{:S(2)}) async-start(bf16[4,2,256,96]{2,3,1,0:T(8,128)(2,1)} %broadcast_in_dim.2), calls=%async_computation | async-start | bytes 786432 | tf_op jit(solution)/shard_map/all_to_all | solution.py:38
  52.8 2.0 %copy-start.2 = (bf16[768,128]{1,0:T(8,128)(2,1)S(1)}, bf16[768,128]{1,0:T(8,128)(2,1)}, u32[]{:S(2)}) copy-start(bf16[768,128]{1,0:T(8,128)(2,1)} %dec_ref.1) | copy-start | bytes 589828
  55.9 5.5 %copy-start.5 = (bf16[1,256,96]{1,2,0:T(8,128)(2,1)S(1)}, bf16[1,256,96]{1,2,0:T(8,128)(2,1)}, u32[]{:S(2)}) copy-start(bf16[1,256,96]{1,2,0:T(8,128)(2,1)} %slice.44) | copy-start | bytes 147460
  61.1 2.1 %copy-start.7 = (bf16[1024,2,48]{0,2,1:T(8,128)(2,1)}, bf16[1024,2,48]{0,2,1:T(8,128)(2,1)S(1)}, u32[]{:S(2)}) copy-start(bf16[1024,2,48]{0,2,1:T(8,128)(2,1)S(1)} %reshape_squeeze.9) | copy-start | bytes 589828
  61.9 1.3 %copy-start.1 = (f32[2,256,1024]{2,1,0:T(8,128)}, f32[2,256,1024]{2,1,0:T(8,128)S(1)}, u32[]{:S(2)}) copy-start(f32[2,256,1024]{2,1,0:T(8,128)S(1)} %multiply_add_fusion) | copy-start | bytes 6291460
  66.3 18.9 %all-to-all-start.1 = ((bf16[2,256,1024]{1,0,2:T(2,128)(2,1)}), bf16[2,256,1024]{1,0,2:T(2,128)(2,1)S(1)}, u32[]{:S(2)}, u32[]{:S(2)}) async-start(bf16[2,256,1024]{1,0,2:T(2,128)(2,1)} %copy.45), calls=%async_computation.1 | async-start | bytes 2097152 | tf_op jit(solution)/shard_map/all_to_all | solution.py:401
  69.8 3.5 %copy-start.8 = (bf16[1024,2,48]{0,2,1:T(8,128)(2,1)S(1)}, bf16[1024,2,48]{0,2,1:T(8,128)(2,1)}, u32[]{:S(2)}) copy-start(bf16[1024,2,48]{0,2,1:T(8,128)(2,1)} %copy-done.7) | copy-start | bytes 589828
  78.3 13.0 %copy-start.4 = (bf16[96,768]{1,0:T(8,128)(2,1)S(1)}, bf16[96,768]{1,0:T(8,128)(2,1)}, u32[]{:S(2)}) copy-start(bf16[96,768]{1,0:T(8,128)(2,1)} %param.18) | copy-start | bytes 442372
  87.7 12.5 %all-to-all-start.2 = ((bf16[4,2,256,96]{2,3,1,0:T(8,128)(2,1)}), bf16[4,2,256,96]{2,3,1,0:T(8,128)(2,1)S(1)}, u32[]{:S(2)}, u32[]{:S(2)}) async-start(bf16[4,2,256,96]{2,3,1,0:T(8,128)(2,1)} %maximum_bitcast_fusion), calls=%async_computation.2 | async-start | bytes 786432 | tf_op jit(solution)/shard_map/all_to_all | solution.py:38
  100.7 28.7 %copy-start.10 = (bf16[256,128]{1,0:T(8,128)(2,1)S(1)}, bf16[256,128]{1,0:T(8,128)(2,1)}, u32[]{:S(2)}) copy-start(bf16[256,128]{1,0:T(8,128)(2,1)} %param.12) | copy-start | bytes 196612
  100.7 28.7 %copy-start.12 = (bf16[256,128]{1,0:T(8,128)(2,1)S(1)}, bf16[256,128]{1,0:T(8,128)(2,1)}, u32[]{:S(2)}) copy-start(bf16[256,128]{1,0:T(8,128)(2,1)} %param.10) | copy-start | bytes 196612

commit v6 on v5

--- a/solution.py
+++ b/solution.py
@@ -199,6 +199,8 @@
     weight_ref,
     out_ref,
     weight_out_ref,
+    got_pair,
+    pair_sum,
     got_both,
     held,
     row_weights,
@@ -209,11 +211,24 @@
     row, col = lax.axis_index("row"), lax.axis_index("col")
     greet((("row", rows), ("col", cols)))
     width = single_ref.shape[-1]
-    copies = [
-        push(both_ref.at[peer], got_both.at[step - 1], send_sems, recv_sems, step - 1, "col", peer)
-        for step, peer in peers_of("col", cols)
+    chips = cols // 2
+    chip, side = col // 2, lax.rem(col, 2)
+    other = 1 - side
+    partner = chip * 2 + other
+    order = [(step, lax.rem(chip + step, chips)) for step in range(1, chips)] + [(0, chip)]
+    pair_copies = [
+        push(
+            both_ref.at[target, other],
+            got_pair.at[step],
+            send_sems,
+            recv_sems,
+            step,
+            "col",
+            partner,
+        )
+        for step, target in order
     ]
-    base = cols - 1
+    base = 2 * chips - 1
     row_weights[row] = weight_ref[...]
     weight_copies = [
         push(
@@ -228,7 +243,23 @@
         for step, peer in peers_of("row", rows)
     ]
     base += rows - 1
-    total = both_ref[col].astype(jnp.float32)
+    copies = []
+    for (step, target), pair_copy in zip(order, pair_copies):
+        pair_copy.wait()
+        total = both_ref[target, side].astype(jnp.float32) + got_pair[step].astype(jnp.float32)
+        if step > 0:
+            pair_sum[step - 1] = total.astype(jnp.bfloat16)
+            copies.append(
+                push(
+                    pair_sum.at[step - 1],
+                    got_both.at[step - 1],
+                    send_sems,
+                    recv_sems,
+                    chips + step - 1,
+                    "col",
+                    target * 2 + side,
+                )
+            )
     for at, copy in enumerate(copies):
         copy.wait()
         total = total + got_both[at].astype(jnp.float32)
@@ -265,10 +296,21 @@
     base += cols - 1
     for copy in copies:
         copy.wait()
-    copies = [
-        push(held, out_ref.at[col], send_sems, recv_sems, base + step - 1, "col", peer)
-        for step, peer in peers_of("col", cols)
+    far_copies = [
+        push(
+            held,
+            out_ref.at[col],
+            send_sems,
+            recv_sems,
+            base + step - 1,
+            "col",
+            target * 2 + side,
+        )
+        for step, target in order
+        if step > 0
     ]
+    base += chips - 1
+    copies = [push(held, out_ref.at[col], send_sems, recv_sems, base, "col", partner)]
     out_ref[col] = held[...]
     for copy in weight_copies:
         copy.wait()
@@ -276,6 +318,20 @@
     for at in range(1, cols):
         weight = weight + col_weights[at]
     weight_out_ref[...] = weight
+    for step, copy in enumerate(far_copies, 1):
+        copy.wait()
+        source = lax.rem(chip - step + chips, chips) * 2 + side
+        copies.append(
+            push(
+                out_ref.at[source],
+                out_ref.at[source],
+                send_sems,
+                recv_sems,
+                base + step,
+                "col",
+                partner,
+            )
+        )
     for copy in copies:
         copy.wait()
 
@@ -283,7 +339,8 @@
 def tail_call(both, single, grad_out, normal, inverse, counts, w_dec, w_pool, weight):
     rows, cols = lax.axis_size("row"), lax.axis_size("col")
     share, atom_width = counts.shape
-    copies = 3 * (cols - 1) + 2 * (rows - 1)
+    chips = cols // 2
+    copies = 2 * (2 * chips - 1) + cols - 1 + 2 * (rows - 1)
     return pl.pallas_call(
         functools.partial(tail_kernel, rows, cols),
         out_shape=(
@@ -293,7 +350,9 @@
         in_specs=[pl.BlockSpec(memory_space=pltpu.VMEM)] * 9,
         out_specs=(pl.BlockSpec(memory_space=pltpu.VMEM),) * 2,
         scratch_shapes=[
-            pltpu.VMEM((cols - 1, share, both.shape[-1]), jnp.bfloat16),
+            pltpu.VMEM((chips, share, both.shape[-1]), jnp.bfloat16),
+            pltpu.VMEM((chips - 1, share, both.shape[-1]), jnp.bfloat16),
+            pltpu.VMEM((chips - 1, share, both.shape[-1]), jnp.bfloat16),
             pltpu.VMEM((rows, share, 2 * atom_width), jnp.bfloat16),
             pltpu.VMEM((rows,) + weight.shape, jnp.float32),
             pltpu.VMEM((cols,) + weight.shape, jnp.float32),
@@ -302,7 +361,7 @@
         ],
         compiler_params=pltpu.CompilerParams(collective_id=1, has_side_effects=True),
     )(
-        both.reshape(cols, share, -1),
+        both.reshape(chips, 2, share, -1),
         single,
         grad_out,
         normal,

time: 133 us -> 129 us (0.970)
  Pallas kernels: 56.2 us -> 53.3 us
    pallas_call x1, Pallas kernels: 26.3 us -> 23.4 us  [tail_call(): pl.pallas_call(functools.partial(tail_kernel, rows, cols), out_shape=(jax...]
where the time goes in v6:
time: 129 us
  Pallas kernels  53.3 us (41%)
  matrix products  26.6 us (21%)
  local copies, waits for them, and re-layouts  18.1 us (14%)
  waiting for transfers between devices  11.8 us (9%)
  starting transfers between devices  11.3 us (9%)
  other arithmetic  6.28 us (5%)
    pallas_call x1, Pallas kernels, pool_call(): pl.pallas_call(functools.partial(pool_kernel, rows, cols), out_shape=(jax...  29.9 us
    pallas_call x1, Pallas kernels, tail_call(): pl.pallas_call(functools.partial(tail_kernel, rows, cols), out_shape=(jax...  23.4 us
    all_to_all x2, starting transfers between devices, exchange_blocks(): return lax.all_to_all(blocks, axis, split_axis=0, concat_axis=0, tiled=True)  7.77 us
    all_to_all x1, waiting for transfers between devices, on_device(): lax.all_to_all(grad_logits, 'col', split_axis=2, concat_axis=0, tiled=True)  6.42 us
    dot_general x1, matrix products, on_device(): jnp.einsum('ijc,ch->hij', pair, w_bias, preferred_element_type=jnp.float32)  5.68 us
    all_to_all x2, waiting for transfers between devices, exchange_blocks(): return lax.all_to_all(blocks, axis, split_axis=0, concat_axis=0, tiled=True)  5.37 us
    dot_general x1, matrix products, on_device(): jnp.einsum('ijc,hij->hc', pair, bias_back, preferred_element_type=jnp.flo...  5.2 us
    convert_element_type x2, local copies, waits for them, and re-layouts, on_device(): bias_rows.astype(jnp.float32)  3.83 us
  transfers between devices with their start and end apart: 3, of which 3 were waited for; matrix products, arithmetic and copies ran while one was open for 19% of the time, Pallas kernels for 0%

profile of v6, /device:TPU:0, one launch (start us, length us, event | category | flops | bytes accessed | tf_op | source)
XLA Modules:
  0.0 128.5 jit_solution(8493377992920622341)
XLA Ops:
  0.6 0.8 fusion.31
  1.4 0.2 convert_reduce_fusion
  1.7 5.7 %convolution_convert_fusion = bf16[16,256,128]{2,0,1:T(8,128)(2,1)S(1)} fusion(bf16[256,128,128]{2,1,0:T(8,128)(2,1)} %param.14, bf16[128,16]{0,1:T(8,128)(2,1)} %param.17), kind=kOutput, calls=%fused_computation.6 | convolution fusion | flops 134742016 | bytes 9441280 | tf_op jit(solution)/shard_map/ijc,ch->hij/dot_general | solution.py:395
  7.4 1.3 %copy.37 = bf16[16,256,128]{2,1,0:T(8,128)(2,1)} copy(bf16[16,256,128]{2,0,1:T(8,128)(2,1)S(1)} %convolution_convert_fusion) | data formatting | bytes 2097152 | tf_op jit(solution)/shard_map/convert_element_type | solution.py:395
  8.7 0.6 pad.4.tally_ref
  9.3 1.4 %convolution_convert_fusion.1 = bf16[1024,256]{1,0:T(8,128)(2,1)} fusion(s32[256]{0:T(256)S(1)} %fusion.31, bf16[256,128]{1,0:T(8,128)(2,1)S(1)} %copy-done.9, bf16[256,128]{1,0:T(8,128)(2,1)S(1)} %copy-done.11), kind=kOutput, calls=%fused_computation.7 | convolution fusion | flops 135004160 | bytes 656384 | tf_op jit(solution)/shard_map/dot_general | solution.py:391
  10.7 29.9 %shard_map.121 = (bf16[8,32,256]{2,1,0:T(8,128)(2,1)}, f32[32,128]{1,0:T(8,128)}, bf16[8,2,256,128]{3,2,1,0:T(8,128)(2,1)}) custom-call(bf16[8,4,32,256]{3,2,1,0:T(8,128)(2,1)} %bitcast.89, f32[4,8,128]{2,1,0:T(8,128)} %pad.4.tally_ref, bf16[8,2,256,128]{3,2,1,0:T(8,128)(2,1)} %bitcast.87), custom_call_target="tpu_custom_call" | custom-call | tf_op jit(solution)/shard_map/pallas_call | solution.py:164
  40.6 1.2 fusion.35
  41.8 0.2 multiply_reduce_fusion.1
  42.2 0.3 fusion.13
  42.5 0.8 broadcast_in_dim.2
  43.3 4.1 %all-to-all-start = ((bf16[4,2,256,96]{2,3,1,0:T(8,128)(2,1)}), bf16[4,2,256,96]{2,3,1,0:T(8,128)(2,1)}, u32[]{:S(2)}, u32[]{:S(2)}) async-start(bf16[4,2,256,96]{2,3,1,0:T(8,128)(2,1)} %broadcast_in_dim.2), calls=%async_computation | async-start | bytes 786432 | tf_op jit(solution)/shard_map/all_to_all | solution.py:38
  47.5 0.6 constant_dynamic-slice_fusion.2.single_ref
  48.2 0.6 slice.44
  48.8 0.7 copy.47.inverse_ref
  49.5 1.4 %convert_bitcast_fusion = f32[2,256,8,128]{3,1,0,2:T(8,128)S(1)} fusion(bf16[8,2,256,128]{3,2,1,0:T(8,128)(2,1)} %get-tuple-element.11), kind=kLoop, calls=%fused_computation.1 | loop fusion | flops 524288 | bytes 3145728 | tf_op jit(solution)/shard_map/convert_element_type | solution.py:421
  50.9 1.9 %copy.40 = f32[2,256,8,128]{1,3,2,0:T(8,128)} copy(f32[2,256,8,128]{3,1,0,2:T(8,128)S(1)} %convert_bitcast_fusion) | data formatting | bytes 4194304 | tf_op jit(solution)/shard_map/convert_element_type | solution.py:421
  52.8 2.0 %copy.41 = f32[2,256,1024]{2,1,0:T(8,128)S(1)} copy(f32[2,256,1024]{1,2,0:T(8,128)} %bitcast.85) | data formatting | bytes 4194304 | tf_op jit(solution)/shard_map/convert_element_type | solution.py:421
  54.8 1.1 fusion.26
  55.9 0.7 constant_dynamic-slice_fusion
  56.6 1.2 convolution_convert_fusion.6
  57.8 1.9 %all-to-all-done = bf16[4,2,256,96]{2,3,1,0:T(8,128)(2,1)} async-done(((bf16[4,2,256,96]{2,3,1,0:T(8,128)(2,1)}), bf16[4,2,256,96]{2,3,1,0:T(8,128)(2,1)}, u32[]{:S(2)}, u32[]{:S(2)}) %all-to-all-start) | async-done | bytes 393248 | tf_op jit(solution)/shard_map/all_to_all | solution.py:38
  59.7 1.0 fusion.34
  60.8 0.2 copy.38
  61.4 0.5 multiply_add_fusion
  61.9 0.7 fusion.36
  62.5 0.7 copy-done.1
  63.2 0.6 multiply_reduce_fusion
  63.8 0.4 multiply_convert_fusion
  64.2 2.1 %copy.45 = bf16[2,256,1024]{1,0,2:T(2,128)(2,1)} copy(bf16[2,256,1024]{2,1,0:T(8,128)(2,1)S(1)} %multiply_convert_fusion) | data formatting | bytes 2097152 | tf_op jit(solution)/shard_map/convert_element_type | solution.py:440
  66.3 3.6 %all-to-all-start.1 = ((bf16[2,256,1024]{1,0,2:T(2,128)(2,1)}), bf16[2,256,1024]{1,0,2:T(2,128)(2,1)S(1)}, u32[]{:S(2)}, u32[]{:S(2)}) async-start(bf16[2,256,1024]{1,0,2:T(2,128)(2,1)} %copy.45), calls=%async_computation.1 | async-start | bytes 2097152 | tf_op jit(solution)/shard_map/all_to_all | solution.py:460
  69.8 3.3 %fusion.3 = bf16[1024,2,48]{0,2,1:T(8,128)(2,1)S(1)} fusion(bf16[256,2,48]{0,2,1:T(8,128)(2,1)S(1)} %bitcast.98, f32[2,256]{1,0:T(2,128)S(1)} %get-tuple-element.23, f32[2,256,1024]{2,1,0:T(8,128)} %copy-done.1), kind=kOutput, calls=%fused_computation.15 | convolution fusion | flops 52004352 | bytes 2344960 | tf_op jit(solution)/shard_map/hij,ihd->jhd/dot_general | solution.py:452
  73.4 3.5 %fusion.5 = bf16[256,2,48]{0,2,1:T(8,128)(2,1)S(1)} fusion(bf16[1024,2,48]{0,2,1:T(8,128)(2,1)S(1)} %copy-done.8, f32[2,256]{1,0:T(2,128)S(1)} %get-tuple-element.23, f32[2,256,1024]{2,1,0:T(8,128)} %copy-done.1), kind=kOutput, calls=%fused_computation.20 | convolution fusion | flops 51930624 | bytes 2344960 | tf_op jit(solution)/shard_map/hij,jhd->ihd/dot_general | solution.py:426
  77.1 0.3 fusion.2
  77.5 0.8 maximum_bitcast_fusion
  78.3 0.4 fusion.4
  78.7 6.4 %all-to-all-done.1 = bf16[2,256,1024]{1,0,2:T(2,128)(2,1)S(1)} async-done(((bf16[2,256,1024]{1,0,2:T(2,128)(2,1)}), bf16[2,256,1024]{1,0,2:T(2,128)(2,1)S(1)}, u32[]{:S(2)}, u32[]{:S(2)}) %all-to-all-start.1) | async-done | bytes 1048608 | tf_op jit(solution)/shard_map/all_to_all | solution.py:460
  85.2 2.5 %copy.46 = bf16[8,2,256,128]{3,1,0,2:T(2,128)(2,1)S(1)} copy(bf16[8,2,256,128]{2,1,3,0:T(2,128)(2,1)S(1)} %bitcast.86) | data formatting | bytes 2097152 | tf_op jit(solution)/shard_map/all_to_all | solution.py:460
  87.7 3.7 %all-to-all-start.2 = ((bf16[4,2,256,96]{2,3,1,0:T(8,128)(2,1)}), bf16[4,2,256,96]{2,3,1,0:T(8,128)(2,1)S(1)}, u32[]{:S(2)}, u32[]{:S(2)}) async-start(bf16[4,2,256,96]{2,3,1,0:T(8,128)(2,1)} %maximum_bitcast_fusion), calls=%async_computation.2 | async-start | bytes 786432 | tf_op jit(solution)/shard_map/all_to_all | solution.py:38
  91.3 0.2 convolution_convert_fusion.2
  91.6 5.2 %convolution_bitcast_fusion.1.weight_ref = f32[16,128]{1,0:T(8,128)} fusion(bf16[16,256,128]{2,0,1:T(8,128)(2,1)S(1)} %bitcast.84, bf16[256,128,128]{2,1,0:T(8,128)(2,1)} %param.14), kind=kOutput, calls=%fused_computation.21 | convolution fusion | flops 134217728 | bytes 9445376 | tf_op jit(solution)/shard_map/ijc,hij->hc/dot_general | solution.py:468
  96.8 3.4 %all-to-all-done.2 = bf16[4,2,256,96]{2,3,1,0:T(8,128)(2,1)S(1)} async-done(((bf16[4,2,256,96]{2,3,1,0:T(8,128)(2,1)}), bf16[4,2,256,96]{2,3,1,0:T(8,128)(2,1)S(1)}, u32[]{:S(2)}, u32[]{:S(2)}) %all-to-all-start.2) | async-done | bytes 393248 | tf_op jit(solution)/shard_map/all_to_all | solution.py:38
  100.3 0.4 fusion.1
  100.7 0.9 pad_maximum_fusion.both_ref
  101.7 23.4 %shard_map.122 = (bf16[8,4,32,256]{3,2,1,0:T(8,128)(2,1)}, f32[16,128]{1,0:T(8,128)}) custom-call(bf16[4,2,32,1536]{3,2,1,0:T(8,128)(2,1)} %pad_maximum_fusion.both_ref, f32[32,768]{1,0:T(8,128)} %constant_dynamic-slice_fusion.2.single_ref, f32[32,768]{1,0:T(8,128)} %get-tuple-element.28.grad_out_ref, f32[32,768]{1,0:T(8,128)} %get-tuple-element.27.normal_ref, ...), custom_call_target="tpu_custom_call" | custom-call | tf_op jit(solution)/shard_map/pallas_call | solution.py:344
  125.1 1.4 %fusion.6 = f32[256,256]{1,0:T(8,128)S(1)} fusion(bf16[1024,256]{1,0:T(8,128)(2,1)} %bitcast.100, s32[256]{0:T(256)S(1)} %fusion.31), kind=kOutput, calls=%fused_computation.25 | convolution fusion | flops 134479872 | bytes 787456 | tf_op jit(solution)/shard_map/dot_general | solution.py:486
  126.5 0.7 slice_add_fusion
  127.2 1.3 %copy.52 = f32[128,16]{0,1:T(8,128)} copy(f32[128,16]{0,1:T(8,128)} %bitcast.99) | data formatting | bytes 16384
  (45 shorter events, 1.4 us)
Async XLA Ops:
  0.6 41.5 %copy-start = (bf16[3,768,96]{1,2,0:T(8,128)(2,1)S(1)}, bf16[3,768,96]{1,2,0:T(8,128)(2,1)}, u32[]{:S(2)}) copy-start(bf16[3,768,96]{1,2,0:T(8,128)(2,1)} %param.16) | copy-start | bytes 1327108
  7.3 2.0 %copy-start.9 = (bf16[256,128]{1,0:T(8,128)(2,1)S(1)}, bf16[256,128]{1,0:T(8,128)(2,1)}, u32[]{:S(2)}) copy-start(bf16[256,128]{1,0:T(8,128)(2,1)} %param.12) | copy-start | bytes 196612
  7.3 2.0 %copy-start.11 = (bf16[256,128]{1,0:T(8,128)(2,1)S(1)}, bf16[256,128]{1,0:T(8,128)(2,1)}, u32[]{:S(2)}) copy-start(bf16[256,128]{1,0:T(8,128)(2,1)} %param.10) | copy-start | bytes 196612
  7.4 33.2 %copy-start.3 = (bf16[128,768]{1,0:T(8,128)(2,1)S(1)}, bf16[128,768]{1,0:T(8,128)(2,1)}, u32[]{:S(2)}) copy-start(bf16[128,768]{1,0:T(8,128)(2,1)} %pool_ref.1) | copy-start | bytes 589828
  7.4 33.2 %copy-start.6 = (bf16[256,768]{1,0:T(8,128)(2,1)S(1)}, bf16[256,768]{1,0:T(8,128)(2,1)}, u32[]{:S(2)}) copy-start(bf16[256,768]{1,0:T(8,128)(2,1)} %param.13) | copy-start | bytes 1179652
  43.3 16.4 %all-to-all-start = ((bf16[4,2,256,96]{2,3,1,0:T(8,128)(2,1)}), bf16[4,2,256,96]{2,3,1,0:T(8,128)(2,1)}, u32[]{:S(2)}, u32[]{:S(2)}) async-start(bf16[4,2,256,96]{2,3,1,0:T(8,128)(2,1)} %broadcast_in_dim.2), calls=%async_computation | async-start | bytes 786432 | tf_op jit(solution)/shard_map/all_to_all | solution.py:38
  52.8 2.0 %copy-start.2 = (bf16[768,128]{1,0:T(8,128)(2,1)S(1)}, bf16[768,128]{1,0:T(8,128)(2,1)}, u32[]{:S(2)}) copy-start(bf16[768,128]{1,0:T(8,128)(2,1)} %dec_ref.1) | copy-start | bytes 589828
  55.9 5.5 %copy-start.5 = (bf16[1,256,96]{1,2,0:T(8,128)(2,1)S(1)}, bf16[1,256,96]{1,2,0:T(8,128)(2,1)}, u32[]{:S(2)}) copy-start(bf16[1,256,96]{1,2,0:T(8,128)(2,1)} %slice.44) | copy-start | bytes 147460
  61.1 2.1 %copy-start.7 = (bf16[1024,2,48]{0,2,1:T(8,128)(2,1)}, bf16[1024,2,48]{0,2,1:T(8,128)(2,1)S(1)}, u32[]{:S(2)}) copy-start(bf16[1024,2,48]{0,2,1:T(8,128)(2,1)S(1)} %reshape_squeeze.9) | copy-start | bytes 589828
  61.9 1.3 %copy-start.1 = (f32[2,256,1024]{2,1,0:T(8,128)}, f32[2,256,1024]{2,1,0:T(8,128)S(1)}, u32[]{:S(2)}) copy-start(f32[2,256,1024]{2,1,0:T(8,128)S(1)} %multiply_add_fusion) | copy-start | bytes 6291460
  66.3 18.9 %all-to-all-start.1 = ((bf16[2,256,1024]{1,0,2:T(2,128)(2,1)}), bf16[2,256,1024]{1,0,2:T(2,128)(2,1)S(1)}, u32[]{:S(2)}, u32[]{:S(2)}) async-start(bf16[2,256,1024]{1,0,2:T(2,128)(2,1)} %copy.45), calls=%async_computation.1 | async-start | bytes 2097152 | tf_op jit(solution)/shard_map/all_to_all | solution.py:460
  69.8 3.5 %copy-start.8 = (bf16[1024,2,48]{0,2,1:T(8,128)(2,1)S(1)}, bf16[1024,2,48]{0,2,1:T(8,128)(2,1)}, u32[]{:S(2)}) copy-start(bf16[1024,2,48]{0,2,1:T(8,128)(2,1)} %copy-done.7) | copy-start | bytes 589828
  78.3 13.0 %copy-start.4 = (bf16[96,768]{1,0:T(8,128)(2,1)S(1)}, bf16[96,768]{1,0:T(8,128)(2,1)}, u32[]{:S(2)}) copy-start(bf16[96,768]{1,0:T(8,128)(2,1)} %param.18) | copy-start | bytes 442372
  87.7 12.5 %all-to-all-start.2 = ((bf16[4,2,256,96]{2,3,1,0:T(8,128)(2,1)}), bf16[4,2,256,96]{2,3,1,0:T(8,128)(2,1)S(1)}, u32[]{:S(2)}, u32[]{:S(2)}) async-start(bf16[4,2,256,96]{2,3,1,0:T(8,128)(2,1)} %maximum_bitcast_fusion), calls=%async_computation.2 | async-start | bytes 786432 | tf_op jit(solution)/shard_map/all_to_all | solution.py:38
  100.7 25.8 %copy-start.10 = (bf16[256,128]{1,0:T(8,128)(2,1)S(1)}, bf16[256,128]{1,0:T(8,128)(2,1)}, u32[]{:S(2)}) copy-start(bf16[256,128]{1,0:T(8,128)(2,1)} %param.12) | copy-start | bytes 196612
  100.7 25.8 %copy-start.12 = (bf16[256,128]{1,0:T(8,128)(2,1)S(1)}, bf16[256,128]{1,0:T(8,128)(2,1)}, u32[]{:S(2)}) copy-start(bf16[256,128]{1,0:T(8,128)(2,1)} %param.10) | copy-start | bytes 196612

commit v7 on v6

--- a/solution.py
+++ b/solution.py
@@ -64,6 +64,8 @@
 
 def peers_of(axis, size):
     me = lax.axis_index(axis)
+    if size & (size - 1) == 0:
+        return [(step, me ^ step) for step in range(1, size)]
     return [(step, lax.rem(me + step, size)) for step in range(1, size)]
 
 

time: 129 us -> 130 us (level)
  no operation moved by 1% of the time
where the time goes in v7:
time: 130 us; the launch traced here: 129 us
  Pallas kernels  54.1 us (42%)
  matrix products  26.6 us (20%)
  local copies, waits for them, and re-layouts  18.1 us (14%)
  waiting for transfers between devices  11.8 us (9%)
  starting transfers between devices  11.3 us (9%)
  other arithmetic  6.28 us (5%)
    pallas_call x1, Pallas kernels, pool_call(): pl.pallas_call(functools.partial(pool_kernel, rows, cols), out_shape=(jax...  30.3 us
    pallas_call x1, Pallas kernels, tail_call(): pl.pallas_call(functools.partial(tail_kernel, rows, cols), out_shape=(jax...  23.8 us
    all_to_all x2, starting transfers between devices, exchange_blocks(): return lax.all_to_all(blocks, axis, split_axis=0, concat_axis=0, tiled=True)  7.77 us
    all_to_all x1, waiting for transfers between devices, on_device(): lax.all_to_all(grad_logits, 'col', split_axis=2, concat_axis=0, tiled=True)  6.42 us
    dot_general x1, matrix products, on_device(): jnp.einsum('ijc,ch->hij', pair, w_bias, preferred_element_type=jnp.float32)  5.68 us
    all_to_all x2, waiting for transfers between devices, exchange_blocks(): return lax.all_to_all(blocks, axis, split_axis=0, concat_axis=0, tiled=True)  5.39 us
    dot_general x1, matrix products, on_device(): jnp.einsum('ijc,hij->hc', pair, bias_back, preferred_element_type=jnp.flo...  5.2 us
    convert_element_type x2, local copies, waits for them, and re-layouts, on_device(): bias_rows.astype(jnp.float32)  3.83 us
  transfers between devices with their start and end apart: 3, of which 3 were waited for; matrix products, arithmetic and copies ran while one was open for 19% of the time, Pallas kernels for 0%

profile of v7, /device:TPU:0, one launch (start us, length us, event | category | flops | bytes accessed | tf_op | source)
XLA Modules:
  0.0 129.3 jit_solution(6682298591187655118)
XLA Ops:
  0.6 0.8 fusion.31
  1.4 0.2 convert_reduce_fusion
  1.7 5.7 %convolution_convert_fusion = bf16[16,256,128]{2,0,1:T(8,128)(2,1)S(1)} fusion(bf16[256,128,128]{2,1,0:T(8,128)(2,1)} %param.14, bf16[128,16]{0,1:T(8,128)(2,1)} %param.17), kind=kOutput, calls=%fused_computation.6 | convolution fusion | flops 134742016 | bytes 9441280 | tf_op jit(solution)/shard_map/ijc,ch->hij/dot_general | solution.py:397
  7.4 1.3 %copy.37 = bf16[16,256,128]{2,1,0:T(8,128)(2,1)} copy(bf16[16,256,128]{2,0,1:T(8,128)(2,1)S(1)} %convolution_convert_fusion) | data formatting | bytes 2097152 | tf_op jit(solution)/shard_map/convert_element_type | solution.py:397
  8.7 0.6 pad.4.tally_ref
  9.3 1.4 %convolution_convert_fusion.1 = bf16[1024,256]{1,0:T(8,128)(2,1)} fusion(s32[256]{0:T(256)S(1)} %fusion.31, bf16[256,128]{1,0:T(8,128)(2,1)S(1)} %copy-done.9, bf16[256,128]{1,0:T(8,128)(2,1)S(1)} %copy-done.11), kind=kOutput, calls=%fused_computation.7 | convolution fusion | flops 135004160 | bytes 656384 | tf_op jit(solution)/shard_map/dot_general | solution.py:393
  10.7 30.3 %shard_map.121 = (bf16[8,32,256]{2,1,0:T(8,128)(2,1)}, f32[32,128]{1,0:T(8,128)}, bf16[8,2,256,128]{3,2,1,0:T(8,128)(2,1)}) custom-call(bf16[8,4,32,256]{3,2,1,0:T(8,128)(2,1)} %bitcast.89, f32[4,8,128]{2,1,0:T(8,128)} %pad.4.tally_ref, bf16[8,2,256,128]{3,2,1,0:T(8,128)(2,1)} %bitcast.87), custom_call_target="tpu_custom_call" | custom-call | tf_op jit(solution)/shard_map/pallas_call | solution.py:166
  41.0 1.2 fusion.35
  42.2 0.2 multiply_reduce_fusion.1
  42.6 0.3 fusion.13
  42.9 0.8 broadcast_in_dim.2
  43.7 4.1 %all-to-all-start = ((bf16[4,2,256,96]{2,3,1,0:T(8,128)(2,1)}), bf16[4,2,256,96]{2,3,1,0:T(8,128)(2,1)}, u32[]{:S(2)}, u32[]{:S(2)}) async-start(bf16[4,2,256,96]{2,3,1,0:T(8,128)(2,1)} %broadcast_in_dim.2), calls=%async_computation | async-start | bytes 786432 | tf_op jit(solution)/shard_map/all_to_all | solution.py:38
  47.9 0.6 constant_dynamic-slice_fusion.2.single_ref
  48.6 0.6 slice.44
  49.2 0.7 copy.47.inverse_ref
  49.9 1.4 %convert_bitcast_fusion = f32[2,256,8,128]{3,1,0,2:T(8,128)S(1)} fusion(bf16[8,2,256,128]{3,2,1,0:T(8,128)(2,1)} %get-tuple-element.11), kind=kLoop, calls=%fused_computation.1 | loop fusion | flops 524288 | bytes 3145728 | tf_op jit(solution)/shard_map/convert_element_type | solution.py:423
  51.3 1.9 %copy.40 = f32[2,256,8,128]{1,3,2,0:T(8,128)} copy(f32[2,256,8,128]{3,1,0,2:T(8,128)S(1)} %convert_bitcast_fusion) | data formatting | bytes 4194304 | tf_op jit(solution)/shard_map/convert_element_type | solution.py:423
  53.2 2.0 %copy.41 = f32[2,256,1024]{2,1,0:T(8,128)S(1)} copy(f32[2,256,1024]{1,2,0:T(8,128)} %bitcast.85) | data formatting | bytes 4194304 | tf_op jit(solution)/shard_map/convert_element_type | solution.py:423
  55.2 1.1 fusion.26
  56.3 0.7 constant_dynamic-slice_fusion
  57.0 1.2 convolution_convert_fusion.6
  58.2 2.0 %all-to-all-done = bf16[4,2,256,96]{2,3,1,0:T(8,128)(2,1)} async-done(((bf16[4,2,256,96]{2,3,1,0:T(8,128)(2,1)}), bf16[4,2,256,96]{2,3,1,0:T(8,128)(2,1)}, u32[]{:S(2)}, u32[]{:S(2)}) %all-to-all-start) | async-done | bytes 393248 | tf_op jit(solution)/shard_map/all_to_all | solution.py:38
  60.2 1.0 fusion.34
  61.5 0.2 copy.39
  61.8 0.5 multiply_add_fusion
  62.3 0.7 fusion.36
  63.0 0.7 copy-done.1
  63.6 0.6 multiply_reduce_fusion
  64.2 0.4 multiply_convert_fusion
  64.6 2.1 %copy.45 = bf16[2,256,1024]{1,0,2:T(2,128)(2,1)} copy(bf16[2,256,1024]{2,1,0:T(8,128)(2,1)S(1)} %multiply_convert_fusion) | data formatting | bytes 2097152 | tf_op jit(solution)/shard_map/convert_element_type | solution.py:442
  66.7 3.6 %all-to-all-start.1 = ((bf16[2,256,1024]{1,0,2:T(2,128)(2,1)}), bf16[2,256,1024]{1,0,2:T(2,128)(2,1)S(1)}, u32[]{:S(2)}, u32[]{:S(2)}) async-start(bf16[2,256,1024]{1,0,2:T(2,128)(2,1)} %copy.45), calls=%async_computation.1 | async-start | bytes 2097152 | tf_op jit(solution)/shard_map/all_to_all | solution.py:462
  70.3 3.3 %fusion.3 = bf16[1024,2,48]{0,2,1:T(8,128)(2,1)S(1)} fusion(bf16[256,2,48]{0,2,1:T(8,128)(2,1)S(1)} %bitcast.98, f32[2,256]{1,0:T(2,128)S(1)} %get-tuple-element.23, f32[2,256,1024]{2,1,0:T(8,128)} %copy-done.1), kind=kOutput, calls=%fused_computation.15 | convolution fusion | flops 52004352 | bytes 2344960 | tf_op jit(solution)/shard_map/hij,ihd->jhd/dot_general | solution.py:454
  73.8 3.5 %fusion.5 = bf16[256,2,48]{0,2,1:T(8,128)(2,1)S(1)} fusion(bf16[1024,2,48]{0,2,1:T(8,128)(2,1)S(1)} %copy-done.8, f32[2,256]{1,0:T(2,128)S(1)} %get-tuple-element.23, f32[2,256,1024]{2,1,0:T(8,128)} %copy-done.1), kind=kOutput, calls=%fused_computation.20 | convolution fusion | flops 51930624 | bytes 2344960 | tf_op jit(solution)/shard_map/hij,jhd->ihd/dot_general | solution.py:428
  77.5 0.3 fusion.2
  77.9 0.8 maximum_bitcast_fusion
  78.7 0.4 fusion.4
  79.2 6.4 %all-to-all-done.1 = bf16[2,256,1024]{1,0,2:T(2,128)(2,1)S(1)} async-done(((bf16[2,256,1024]{1,0,2:T(2,128)(2,1)}), bf16[2,256,1024]{1,0,2:T(2,128)(2,1)S(1)}, u32[]{:S(2)}, u32[]{:S(2)}) %all-to-all-start.1) | async-done | bytes 1048608 | tf_op jit(solution)/shard_map/all_to_all | solution.py:462
  85.6 2.5 %copy.46 = bf16[8,2,256,128]{3,1,0,2:T(2,128)(2,1)S(1)} copy(bf16[8,2,256,128]{2,1,3,0:T(2,128)(2,1)S(1)} %bitcast.86) | data formatting | bytes 2097152 | tf_op jit(solution)/shard_map/all_to_all | solution.py:462
  88.1 3.7 %all-to-all-start.2 = ((bf16[4,2,256,96]{2,3,1,0:T(8,128)(2,1)}), bf16[4,2,256,96]{2,3,1,0:T(8,128)(2,1)S(1)}, u32[]{:S(2)}, u32[]{:S(2)}) async-start(bf16[4,2,256,96]{2,3,1,0:T(8,128)(2,1)} %maximum_bitcast_fusion), calls=%async_computation.2 | async-start | bytes 786432 | tf_op jit(solution)/shard_map/all_to_all | solution.py:38
  91.8 0.2 convolution_convert_fusion.2
  92.0 5.2 %convolution_bitcast_fusion.1.weight_ref = f32[16,128]{1,0:T(8,128)} fusion(bf16[16,256,128]{2,0,1:T(8,128)(2,1)S(1)} %bitcast.84, bf16[256,128,128]{2,1,0:T(8,128)(2,1)} %param.14), kind=kOutput, calls=%fused_computation.21 | convolution fusion | flops 134217728 | bytes 9445376 | tf_op jit(solution)/shard_map/ijc,hij->hc/dot_general | solution.py:470
  97.2 3.4 %all-to-all-done.2 = bf16[4,2,256,96]{2,3,1,0:T(8,128)(2,1)S(1)} async-done(((bf16[4,2,256,96]{2,3,1,0:T(8,128)(2,1)}), bf16[4,2,256,96]{2,3,1,0:T(8,128)(2,1)S(1)}, u32[]{:S(2)}, u32[]{:S(2)}) %all-to-all-start.2) | async-done | bytes 393248 | tf_op jit(solution)/shard_map/all_to_all | solution.py:38
  100.7 0.4 fusion.1
  101.1 0.9 pad_maximum_fusion.both_ref
  102.1 23.8 %shard_map.122 = (bf16[8,4,32,256]{3,2,1,0:T(8,128)(2,1)}, f32[16,128]{1,0:T(8,128)}) custom-call(bf16[4,2,32,1536]{3,2,1,0:T(8,128)(2,1)} %pad_maximum_fusion.both_ref, f32[32,768]{1,0:T(8,128)} %constant_dynamic-slice_fusion.2.single_ref, f32[32,768]{1,0:T(8,128)} %get-tuple-element.28.grad_out_ref, f32[32,768]{1,0:T(8,128)} %get-tuple-element.27.normal_ref, ...), custom_call_target="tpu_custom_call" | custom-call | tf_op jit(solution)/shard_map/pallas_call | solution.py:346
  125.9 1.4 %fusion.6 = f32[256,256]{1,0:T(8,128)S(1)} fusion(bf16[1024,256]{1,0:T(8,128)(2,1)} %bitcast.100, s32[256]{0:T(256)S(1)} %fusion.31), kind=kOutput, calls=%fused_computation.25 | convolution fusion | flops 134479872 | bytes 787456 | tf_op jit(solution)/shard_map/dot_general | solution.py:488
  127.3 0.7 slice_add_fusion
  128.0 1.3 %copy.52 = f32[128,16]{0,1:T(8,128)} copy(f32[128,16]{0,1:T(8,128)} %bitcast.99) | data formatting | bytes 16384
  (45 shorter events, 1.4 us)
Async XLA Ops:
  0.6 41.9 %copy-start = (bf16[3,768,96]{1,2,0:T(8,128)(2,1)S(1)}, bf16[3,768,96]{1,2,0:T(8,128)(2,1)}, u32[]{:S(2)}) copy-start(bf16[3,768,96]{1,2,0:T(8,128)(2,1)} %param.16) | copy-start | bytes 1327108
  7.3 2.0 %copy-start.9 = (bf16[256,128]{1,0:T(8,128)(2,1)S(1)}, bf16[256,128]{1,0:T(8,128)(2,1)}, u32[]{:S(2)}) copy-start(bf16[256,128]{1,0:T(8,128)(2,1)} %param.12) | copy-start | bytes 196612
  7.3 2.0 %copy-start.11 = (bf16[256,128]{1,0:T(8,128)(2,1)S(1)}, bf16[256,128]{1,0:T(8,128)(2,1)}, u32[]{:S(2)}) copy-start(bf16[256,128]{1,0:T(8,128)(2,1)} %param.10) | copy-start | bytes 196612
  7.4 33.6 %copy-start.3 = (bf16[128,768]{1,0:T(8,128)(2,1)S(1)}, bf16[128,768]{1,0:T(8,128)(2,1)}, u32[]{:S(2)}) copy-start(bf16[128,768]{1,0:T(8,128)(2,1)} %pool_ref.1) | copy-start | bytes 589828
  7.4 33.6 %copy-start.6 = (bf16[256,768]{1,0:T(8,128)(2,1)S(1)}, bf16[256,768]{1,0:T(8,128)(2,1)}, u32[]{:S(2)}) copy-start(bf16[256,768]{1,0:T(8,128)(2,1)} %param.13) | copy-start | bytes 1179652
  43.7 16.4 %all-to-all-start = ((bf16[4,2,256,96]{2,3,1,0:T(8,128)(2,1)}), bf16[4,2,256,96]{2,3,1,0:T(8,128)(2,1)}, u32[]{:S(2)}, u32[]{:S(2)}) async-start(bf16[4,2,256,96]{2,3,1,0:T(8,128)(2,1)} %broadcast_in_dim.2), calls=%async_computation | async-start | bytes 786432 | tf_op jit(solution)/shard_map/all_to_all | solution.py:38
  53.2 2.0 %copy-start.2 = (bf16[768,128]{1,0:T(8,128)(2,1)S(1)}, bf16[768,128]{1,0:T(8,128)(2,1)}, u32[]{:S(2)}) copy-start(bf16[768,128]{1,0:T(8,128)(2,1)} %dec_ref.1) | copy-start | bytes 589828
  56.3 5.5 %copy-start.5 = (bf16[1,256,96]{1,2,0:T(8,128)(2,1)S(1)}, bf16[1,256,96]{1,2,0:T(8,128)(2,1)}, u32[]{:S(2)}) copy-start(bf16[1,256,96]{1,2,0:T(8,128)(2,1)} %slice.44) | copy-start | bytes 147460
  61.5 2.1 %copy-start.7 = (bf16[1024,2,48]{0,2,1:T(8,128)(2,1)}, bf16[1024,2,48]{0,2,1:T(8,128)(2,1)S(1)}, u32[]{:S(2)}) copy-start(bf16[1024,2,48]{0,2,1:T(8,128)(2,1)S(1)} %reshape_squeeze.9) | copy-start | bytes 589828
  62.3 1.3 %copy-start.1 = (f32[2,256,1024]{2,1,0:T(8,128)}, f32[2,256,1024]{2,1,0:T(8,128)S(1)}, u32[]{:S(2)}) copy-start(f32[2,256,1024]{2,1,0:T(8,128)S(1)} %multiply_add_fusion) | copy-start | bytes 6291460
  66.7 18.9 %all-to-all-start.1 = ((bf16[2,256,1024]{1,0,2:T(2,128)(2,1)}), bf16[2,256,1024]{1,0,2:T(2,128)(2,1)S(1)}, u32[]{:S(2)}, u32[]{:S(2)}) async-start(bf16[2,256,1024]{1,0,2:T(2,128)(2,1)} %copy.45), calls=%async_computation.1 | async-start | bytes 2097152 | tf_op jit(solution)/shard_map/all_to_all | solution.py:462
  70.2 3.5 %copy-start.8 = (bf16[1024,2,48]{0,2,1:T(8,128)(2,1)S(1)}, bf16[1024,2,48]{0,2,1:T(8,128)(2,1)}, u32[]{:S(2)}) copy-start(bf16[1024,2,48]{0,2,1:T(8,128)(2,1)} %copy-done.7) | copy-start | bytes 589828
  78.7 13.0 %copy-start.4 = (bf16[96,768]{1,0:T(8,128)(2,1)S(1)}, bf16[96,768]{1,0:T(8,128)(2,1)}, u32[]{:S(2)}) copy-start(bf16[96,768]{1,0:T(8,128)(2,1)} %param.18) | copy-start | bytes 442372
  88.1 12.5 %all-to-all-start.2 = ((bf16[4,2,256,96]{2,3,1,0:T(8,128)(2,1)}), bf16[4,2,256,96]{2,3,1,0:T(8,128)(2,1)S(1)}, u32[]{:S(2)}, u32[]{:S(2)}) async-start(bf16[4,2,256,96]{2,3,1,0:T(8,128)(2,1)} %maximum_bitcast_fusion), calls=%async_computation.2 | async-start | bytes 786432 | tf_op jit(solution)/shard_map/all_to_all | solution.py:38
  101.1 26.2 %copy-start.10 = (bf16[256,128]{1,0:T(8,128)(2,1)S(1)}, bf16[256,128]{1,0:T(8,128)(2,1)}, u32[]{:S(2)}) copy-start(bf16[256,128]{1,0:T(8,128)(2,1)} %param.12) | copy-start | bytes 196612
  101.1 26.2 %copy-start.12 = (bf16[256,128]{1,0:T(8,128)(2,1)S(1)}, bf16[256,128]{1,0:T(8,128)(2,1)}, u32[]{:S(2)}) copy-start(bf16[256,128]{1,0:T(8,128)(2,1)} %param.10) | copy-start | bytes 196612
